TPU v7x, 32 devices: a whole 2x2x4 slice. The times are simulated.
32 devices in a mesh: dp: 32 (over z, y, x, core).
Axes of the slice: x: 2, y: 2, z: 4, core: 2. Of those that a mesh axis runs over, the one named last changes fastest.
Arguments:
- short_input: bfloat16 [96, 128, 1024], P('dp'), may hold values from -6 to 6
- short_lengths: int32 [96], P('dp'), may hold values from 32 to 128
- short_cotangent: bfloat16 [96, 128, 1024], P('dp'), may hold values from -6 to 6
- long_input: bfloat16 [32, 512, 1024], P('dp'), may hold values from -6 to 6
- long_lengths: int32 [32], P('dp'), may hold values from 128 to 512
- long_cotangent: bfloat16 [32, 512, 1024], P('dp'), may hold values from -6 to 6
- packed_weight: bfloat16 [1024, 3072], P('dp'), may hold values from -0.1875 to 0.1875
- output_weight: bfloat16 [1024, 1024], P('dp'), may hold values from -0.75 to 0.75
- inner_weight: bfloat16 [1024, 4096], P('dp'), may hold values from -0.1875 to 0.1875
- down_weight: bfloat16 [4096, 1024], P('dp'), may hold values from -0.09375 to 0.09375
- first_gain: float32 [1024], replicated, may hold values from 0.1 to 1.9
- second_gain: float32 [1024], replicated, may hold values from 0.1 to 1.9
- query_bias: float32 [1024], replicated, may hold values from -3 to 3
- value_bias: float32 [1024], replicated, may hold values from -3 to 3
- output_bias: float32 [1024], replicated, may hold values from -3 to 3
- inner_bias: float32 [4096], replicated, may hold values from -3 to 3
- down_bias: float32 [1024], replicated, may hold values from -3 to 3
- first_beta: float32 [1024], replicated, may hold values from -3 to 3
- second_beta: float32 [1024], replicated, may hold values from -3 to 3
Outputs:
- short_output: bfloat16 [96, 128, 1024], P('dp')
- short_input_grad: bfloat16 [96, 128, 1024], P('dp')
- long_output: bfloat16 [32, 512, 1024], P('dp')
- long_input_grad: bfloat16 [32, 512, 1024], P('dp')
- query_bias_grad: float32 [1024], replicated
- value_bias_grad: float32 [1024], replicated
- output_bias_grad: float32 [1024], replicated
- inner_bias_grad: float32 [4096], replicated
- down_bias_grad: float32 [1024], replicated
- first_beta_grad: float32 [1024], replicated
- second_beta_grad: float32 [1024], replicated
All inputs are finite; a program needn't handle non-finite values.
Results may differ from a plain program's by a relative error of at most 0.014.
Values may be sent and summed in bfloat16 or wider, within the bound.
No kernel may reach another device: no remote copies, remote signals or barrier semaphores. Data moves between devices by JAX's collectives and lax.ppermute only.
A program may use at most 192 MiB of HBM per device.

v0:
```python
from functools import partial

import jax
import jax.numpy as jnp
from jax import lax
from jax.experimental import pallas as pl
from jax.experimental.pallas import tpu as pltpu
from jax.sharding import PartitionSpec as P

HEADS = 16
HEAD_DIM = 64
BF = jnp.bfloat16
F32 = jnp.float32
VMEM_BYTES = 60 * 1024 * 1024


def dot(left, right):
    return lax.dot_general(left, right, (((1,), (0,)), ((), ())), preferred_element_type=F32)


def dot_t(left, right):
    return lax.dot_general(left, right, (((1,), (1,)), ((), ())), preferred_element_type=F32)


def sequences(short_seqs, short_len, long_seqs, long_len):
    spans = [(i * short_len, short_len) for i in range(short_seqs)]
    base = short_seqs * short_len
    return spans, [(base + i * long_len, long_len) for i in range(long_seqs)]


def row_mask(short_lengths, long_lengths, shape):
    short_seqs, short_len, long_seqs, long_len = shape
    pieces = []
    for count, length, refs in (
        (short_seqs, short_len, short_lengths),
        (long_seqs, long_len, long_lengths),
    ):
        for i in range(count):
            rows = lax.broadcasted_iota(jnp.int32, (length, 1), 0)
            pieces.append(jnp.where(rows < refs[i], 1.0, 0.0).astype(F32))
    return jnp.concatenate(pieces, axis=0)


def head_lanes(block, half):
    lanes = lax.broadcasted_iota(jnp.int32, block.shape, 1)
    keep = lanes < HEAD_DIM if half == 0 else lanes >= HEAD_DIM
    return jnp.where(keep, block, jnp.zeros_like(block))


def flip(block):
    return jnp.transpose(block, (1, 0))


def attention_forward_kernel(
    shape, short_lengths, long_lengths, short_x, long_x, wq, wk, wv, wo, qb, vb, ob,
    q_out, k_out, v_out, short_p, long_p, mixed_t, xhat_out, rstd_out, x_all, mixed,
):
    step = pl.program_id(0)
    steps = pl.num_programs(0)
    short_seqs, short_len, long_seqs, long_len = shape
    base = short_seqs * short_len
    width = wq.shape[1]
    short_spans, long_spans = sequences(*shape)

    @pl.when(step == 0)
    def _():
        x_all[:base, :] = short_x[...]
        x_all[base:, :] = long_x[...]

    x = x_all[...]
    q_out[...] = ((dot(x, wq[...]) + qb[...]).astype(BF).astype(F32) * HEAD_DIM ** (-0.5)).astype(BF)
    k_out[...] = dot(x, wk[...]).astype(BF)
    v_out[...] = (dot(x, wv[...]) + vb[...]).astype(BF)
    for pair in range(width // 128):
        lanes = slice(128 * pair, 128 * pair + 128)
        v_t = flip(v_out[:, lanes])
        for which, spans, refs, probs in (
            (0, short_spans, short_lengths, short_p),
            (1, long_spans, long_lengths, long_p),
        ):
            for seq, (start, length) in enumerate(spans):
                k2 = k_out[start : start + length, lanes]
                rows = lax.broadcasted_iota(jnp.int32, (length, 1), 0)
                usable = rows < refs[seq]
                block = min(length, 256)
                for half in range(2):
                    k_head = head_lanes(k2, half)
                    v_head = v_t[HEAD_DIM * half : HEAD_DIM * half + HEAD_DIM, start : start + length]
                    for at in range(0, length, block):
                        scores = dot_t(k_head, q_out[start + at : start + at + block, lanes])
                        scores = jnp.where(usable, scores, -1e30)
                        top = jnp.max(scores, axis=0, keepdims=True)
                        powers = jnp.exp(scores - top)
                        total = jnp.sum(powers, axis=0, keepdims=True)
                        prob = (powers * (1.0 / total)).astype(BF)
                        probs[seq, 2 * pair + half, :, at : at + block] = prob
                        feature = 128 * pair + HEAD_DIM * half
                        mixed_t[feature : feature + HEAD_DIM, start + at : start + at + block] = dot(v_head, prob)
        offset = pl.multiple_of(step * width + 128 * pair, 128)
        mixed[:, pl.ds(offset, 128)] = flip(mixed_t[lanes, :]).astype(BF)

    @pl.when(step == steps - 1)
    def _():
        first_sum = x_all[...].astype(F32) + (dot(mixed[...], wo[...]) + ob[...])
        center = first_sum - jnp.mean(first_sum, axis=-1, keepdims=True)
        spread = jnp.mean(center * center, axis=-1, keepdims=True)
        rstd = lax.rsqrt(spread + 1e-06)
        xhat_out[...] = center * rstd
        rstd_out[...] = rstd


def attention_forward(shape, lengths, xs, packed_w, output_w, vectors):
    short_seqs, short_len, long_seqs, long_len = shape
    rows = short_seqs * short_len + long_seqs * long_len
    width = xs[0].shape[1]
    block = 256
    heads = block // HEAD_DIM
    steps = width // block
    whole = lambda shp: pl.BlockSpec(shp, lambda j: (0,) * len(shp))
    smem = pl.BlockSpec(memory_space=pltpu.SMEM)
    column = lambda off: pl.BlockSpec((width, block), lambda j: (0, j + off * steps))
    row_block = pl.BlockSpec((1, block), lambda j: (0, j))
    out_col = pl.BlockSpec((rows, block), lambda j: (0, j))
    return pl.pallas_call(
        partial(attention_forward_kernel, shape),
        grid=(steps,),
        in_specs=[
            smem, smem, whole(xs[0].shape), whole(xs[1].shape),
            column(0), column(1), column(2), whole((width, width)),
            row_block, row_block, whole((1, width)),
        ],
        out_specs=[
            out_col, out_col, out_col,
            pl.BlockSpec((short_seqs, heads, short_len, short_len), lambda j: (0, j, 0, 0)),
            pl.BlockSpec((long_seqs, heads, long_len, long_len), lambda j: (0, j, 0, 0)),
            pl.BlockSpec((block, rows), lambda j: (j, 0)),
            whole((rows, width)), whole((rows, 1)),
        ],
        out_shape=[
            jax.ShapeDtypeStruct((rows, width), BF),
            jax.ShapeDtypeStruct((rows, width), BF),
            jax.ShapeDtypeStruct((rows, width), BF),
            jax.ShapeDtypeStruct((short_seqs, HEADS, short_len, short_len), BF),
            jax.ShapeDtypeStruct((long_seqs, HEADS, long_len, long_len), BF),
            jax.ShapeDtypeStruct((width, rows), F32),
            jax.ShapeDtypeStruct((rows, width), F32),
            jax.ShapeDtypeStruct((rows, 1), F32),
        ],
        scratch_shapes=[pltpu.VMEM((rows, width), BF), pltpu.VMEM((rows, width), BF)],
        compiler_params=pltpu.CompilerParams(vmem_limit_bytes=VMEM_BYTES),
        name="attention_forward",
    )(*lengths, *xs, packed_w, packed_w, packed_w, output_w, vectors["query_bias"], vectors["value_bias"], vectors["output_bias"])


def gelu_and_slope(value):
    density = jnp.exp(value * value * -0.5)
    t = 1.0 / (1.0 + (0.3275911 * 0.5 ** 0.5) * jnp.abs(value))
    poly = t * (0.254829592 + t * (-0.284496736 + t * (1.421413741 + t * (-1.453152027 + t * 1.061405429))))
    tail = 0.5 * poly * density
    share = jnp.where(value < 0.0, tail, 1.0 - tail)
    return value * share, share + value * (density * 0.3989422804014327)


def inner_kernel(xhat, gain, beta, wi, bi, active, slope, first):
    @pl.when(pl.program_id(0) == 0)
    def _():
        first[...] = (xhat[...] * gain[...] + beta[...]).astype(BF)

    value = dot(first[...], wi[...]) + bi[...]
    act, slp = gelu_and_slope(value)
    active[...] = act.astype(BF)
    slope[...] = slp.astype(BF)


def inner_forward(xhat, gain, beta, inner_w, inner_bias, block=512):
    rows, width = xhat.shape
    units = inner_w.shape[1]
    whole = lambda shp: pl.BlockSpec(shp, lambda j: (0,) * len(shp))
    col = pl.BlockSpec((rows, block), lambda j: (0, j))
    return pl.pallas_call(
        inner_kernel,
        grid=(units // block,),
        in_specs=[
            whole((rows, width)), whole((1, width)), whole((1, width)),
            pl.BlockSpec((width, block), lambda j: (0, j)), pl.BlockSpec((1, block), lambda j: (0, j)),
        ],
        out_specs=[col, col],
        out_shape=[jax.ShapeDtypeStruct((rows, units), BF)] * 2,
        scratch_shapes=[pltpu.VMEM((rows, width), BF)],
        compiler_params=pltpu.CompilerParams(vmem_limit_bytes=VMEM_BYTES),
        name="inner_forward",
    )(xhat, gain, beta, inner_w, inner_bias)


def norm_gradient(grad, xhat, rstd, gain):
    scaled = grad * gain
    mean = jnp.mean(scaled, axis=-1, keepdims=True)
    along = jnp.mean(scaled * xhat, axis=-1, keepdims=True)
    return rstd * (scaled - mean - xhat * along)


def feed_kernel(
    shape, steps, short_lengths, long_lengths, xhat, rstd, short_ct, long_ct, active, slope, wd, wi, wo,
    gain1, beta1, gain2, beta2, down_bias,
    short_out, long_out, grad_mixed, grad_first_sum, second_beta_sum, down_sum, inner_sum, first_beta_sum, output_sum,
    total, grad_down,
):
    step = pl.program_id(0)
    short_seqs, short_len, long_seqs, long_len = shape
    base = short_seqs * short_len

    @pl.when(step == 0)
    def _():
        total[...] = xhat[...] * gain1[...] + beta1[...] + down_bias[...]

    @pl.when(step < steps)
    def _():
        total[...] += dot(active[...], wd[...])

    @pl.when(step == steps - 1)
    def _():
        keep = row_mask(short_lengths, long_lengths, shape)
        second = total[...]
        center = second - jnp.mean(second, axis=-1, keepdims=True)
        spread = jnp.mean(center * center, axis=-1, keepdims=True)
        rstd2 = lax.rsqrt(spread + 1e-06)
        xhat2 = center * rstd2
        output = ((xhat2 * gain2[...] + beta2[...]) * keep).astype(BF)
        short_out[...] = output[:base]
        long_out[...] = output[base:]
        grad_out = jnp.concatenate([short_ct[...], long_ct[...]], axis=0).astype(F32) * keep
        second_beta_sum[...] = jnp.sum(grad_out, axis=0, keepdims=True)
        grad_second = norm_gradient(grad_out, xhat2, rstd2, gain2[...])
        low = grad_second.astype(BF)
        grad_down[...] = low
        down_sum[...] = jnp.sum(low.astype(F32), axis=0, keepdims=True)
        total[...] = grad_second

    @pl.when(step >= steps)
    def _():
        grad_inner = (dot_t(grad_down[...], wd[...]) * slope[...].astype(F32)).astype(BF)
        inner_sum[...] = jnp.sum(grad_inner.astype(F32), axis=0, keepdims=True)
        total[...] += dot_t(grad_inner, wi[...])

    @pl.when(step == 2 * steps - 1)
    def _():
        grad_first = total[...]
        first_beta_sum[...] = jnp.sum(grad_first, axis=0, keepdims=True)
        result = norm_gradient(grad_first, xhat[...], rstd[...], gain1[...])
        grad_first_sum[...] = result
        branch = result.astype(BF)
        output_sum[...] = jnp.sum(branch.astype(F32), axis=0, keepdims=True)
        grad_mixed[...] = dot_t(branch, wo[...]).astype(BF)


def feed_back(shape, lengths, xhat, rstd, cts, active, slope, down_w, inner_w, output_w, vectors, block=512):
    rows, width = xhat.shape
    units = down_w.shape[0]
    steps = units // block
    whole = lambda shp: pl.BlockSpec(shp, lambda j: (0,) * len(shp))
    smem = pl.BlockSpec(memory_space=pltpu.SMEM)
    vec = whole((1, width))
    late = lambda j: jnp.maximum(j - steps, 0)
    vector_out = jax.ShapeDtypeStruct((1, width), F32)
    return pl.pallas_call(
        partial(feed_kernel, shape, steps),
        grid=(2 * steps,),
        in_specs=[
            smem, smem, whole((rows, width)), whole((rows, 1)), whole(cts[0].shape), whole(cts[1].shape),
            pl.BlockSpec((rows, block), lambda j: (0, jnp.minimum(j, steps - 1))),
            pl.BlockSpec((rows, block), lambda j: (0, late(j))),
            pl.BlockSpec((block, width), lambda j: (lax.rem(j, steps), 0)),
            pl.BlockSpec((width, block), lambda j: (0, late(j))),
            whole((width, width)), vec, vec, vec, vec, vec,
        ],
        out_specs=[
            whole(cts[0].shape), whole(cts[1].shape), whole((rows, width)), whole((rows, width)),
            vec, vec, pl.BlockSpec((1, block), lambda j: (0, late(j))), vec, vec,
        ],
        out_shape=[
            jax.ShapeDtypeStruct(cts[0].shape, BF), jax.ShapeDtypeStruct(cts[1].shape, BF),
            jax.ShapeDtypeStruct((rows, width), BF), jax.ShapeDtypeStruct((rows, width), F32),
            vector_out, vector_out, jax.ShapeDtypeStruct((1, units), F32), vector_out, vector_out,
        ],
        scratch_shapes=[pltpu.VMEM((rows, width), F32), pltpu.VMEM((rows, width), BF)],
        compiler_params=pltpu.CompilerParams(vmem_limit_bytes=VMEM_BYTES),
        name="feed_back",
    )(
        *lengths, xhat, rstd, *cts, active, slope, down_w, inner_w, output_w,
        vectors["first_gain"], vectors["first_beta"], vectors["second_gain"], vectors["second_beta"], vectors["down_bias"],
    )


def attention_backward_kernel(
    shape, short_lengths, long_lengths, q, k, v, gm, short_p, long_p, mixed_t, wq, wk, wv, grad_first_sum,
    short_grad, long_grad, query_sum, value_sum, grad_packed, total,
):
    step = pl.program_id(0)
    steps = pl.num_programs(0)
    short_seqs, short_len, long_seqs, long_len = shape
    base = short_seqs * short_len
    width = q.shape[1]
    short_spans, long_spans = sequences(*shape)
    scale = HEAD_DIM ** (-0.5)
    for pair in range(width // 128):
        lanes = slice(128 * pair, 128 * pair + 128)
        gm_t = flip(gm[:, lanes]).astype(F32)
        k_t = flip(k[:, lanes])
        product = gm_t * mixed_t[lanes, :]
        delta = [jnp.sum(product[HEAD_DIM * h : HEAD_DIM * h + HEAD_DIM], axis=0, keepdims=True) for h in range(2)]
        for spans, probs in ((short_spans, short_p), (long_spans, long_p)):
            for seq, (start, length) in enumerate(spans):
                here = slice(start, start + length)
                gm2, v2, q2 = gm[here, lanes], v[here, lanes], q[here, lanes]
                grad_value = grad_key = None
                grad_query_t = []
                for half in range(2):
                    prob = probs[seq, 2 * pair + half]
                    grad_p = dot_t(head_lanes(v2, half), gm2)
                    grad_s = (prob.astype(F32) * (grad_p - delta[half][:, here])).astype(BF)
                    dv = dot(prob, head_lanes(gm2, half))
                    dk = dot(grad_s, head_lanes(q2, half))
                    grad_value = dv if half == 0 else grad_value + dv
                    grad_key = dk if half == 0 else grad_key + dk
                    grad_query_t.append(dot(k_t[HEAD_DIM * half : HEAD_DIM * half + HEAD_DIM, here], grad_s))
                grad_packed[here, 128 * pair : 128 * pair + 128] = (
                    flip(jnp.concatenate(grad_query_t, axis=0)) * scale
                ).astype(BF)
                grad_packed[here, width + 128 * pair : width + 128 * pair + 128] = grad_key.astype(BF)
                grad_packed[here, 2 * width + 128 * pair : 2 * width + 128 * pair + 128] = grad_value.astype(BF)
    query_sum[...] = jnp.sum(grad_packed[:, :width].astype(F32), axis=0, keepdims=True)
    value_sum[...] = jnp.sum(grad_packed[:, 2 * width :].astype(F32), axis=0, keepdims=True)
    part = (
        dot_t(grad_packed[:, :width], wq[...])
        + dot_t(grad_packed[:, width : 2 * width], wk[...])
        + dot_t(grad_packed[:, 2 * width :], wv[...])
    )

    @pl.when(step == 0)
    def _():
        total[...] = grad_first_sum[...] + part

    @pl.when(step > 0)
    def _():
        total[...] += part

    @pl.when(step == steps - 1)
    def _():
        keep = row_mask(short_lengths, long_lengths, shape)
        result = (total[...] * keep).astype(BF)
        short_grad[...] = result[:base]
        long_grad[...] = result[base:]


def attention_backward(shape, lengths, q, k, v, gm, short_p, long_p, mixed_t, packed_w, grad_first_sum):
    short_seqs, short_len, long_seqs, long_len = shape
    rows, width = q.shape
    block = 256
    heads = block // HEAD_DIM
    steps = width // block
    base = short_seqs * short_len
    whole = lambda shp: pl.BlockSpec(shp, lambda j: (0,) * len(shp))
    smem = pl.BlockSpec(memory_space=pltpu.SMEM)
    column = lambda off: pl.BlockSpec((width, block), lambda j: (0, j + off * steps))
    col = pl.BlockSpec((rows, block), lambda j: (0, j))
    vec = pl.BlockSpec((1, block), lambda j: (0, j))
    return pl.pallas_call(
        partial(attention_backward_kernel, shape),
        grid=(steps,),
        in_specs=[
            smem, smem, col, col, col, col,
            pl.BlockSpec((short_seqs, heads, short_len, short_len), lambda j: (0, j, 0, 0)),
            pl.BlockSpec((long_seqs, heads, long_len, long_len), lambda j: (0, j, 0, 0)),
            pl.BlockSpec((block, rows), lambda j: (j, 0)),
            column(0), column(1), column(2), whole((rows, width)),
        ],
        out_specs=[whole((base, width)), whole((rows - base, width)), vec, vec],
        out_shape=[
            jax.ShapeDtypeStruct((base, width), BF), jax.ShapeDtypeStruct((rows - base, width), BF),
            jax.ShapeDtypeStruct((1, width), F32), jax.ShapeDtypeStruct((1, width), F32),
        ],
        scratch_shapes=[pltpu.VMEM((rows, 3 * block), BF), pltpu.VMEM((rows, width), F32)],
        compiler_params=pltpu.CompilerParams(vmem_limit_bytes=VMEM_BYTES),
        name="attention_backward",
    )(*lengths, q, k, v, gm, short_p, long_p, mixed_t, packed_w, packed_w, packed_w, grad_first_sum)


def local(
    short_input, short_lengths, short_cotangent, long_input, long_lengths, long_cotangent,
    packed_weight, output_weight, inner_weight, down_weight,
    first_gain, second_gain, query_bias, value_bias, output_bias, inner_bias, down_bias, first_beta, second_beta,
):
    short_seqs, short_len, width = short_input.shape
    long_seqs, long_len, _ = long_input.shape
    shape = (short_seqs, short_len, long_seqs, long_len)
    lengths = (short_lengths, long_lengths)
    vectors = dict(
        first_gain=first_gain, second_gain=second_gain, query_bias=query_bias, value_bias=value_bias,
        output_bias=output_bias, inner_bias=inner_bias, down_bias=down_bias, first_beta=first_beta, second_beta=second_beta,
    )
    vectors = {name: item.reshape(1, -1) for name, item in vectors.items()}
    xs = (short_input.reshape(-1, width), long_input.reshape(-1, width))
    cts = (short_cotangent.reshape(-1, width), long_cotangent.reshape(-1, width))
    packed_w, output_w, inner_w, down_w = gather_all(packed_weight, output_weight, inner_weight, down_weight)
    q, k, v, short_p, long_p, mixed_t, xhat, rstd = attention_forward(shape, lengths, xs, packed_w, output_w, vectors)
    active, slope = inner_forward(xhat, vectors["first_gain"], vectors["first_beta"], inner_w, vectors["inner_bias"])
    (
        short_out, long_out, gm, grad_first_sum, second_beta_sum, down_sum, inner_sum, first_beta_sum, output_sum,
    ) = feed_back(shape, lengths, xhat, rstd, cts, active, slope, down_w, inner_w, output_w, vectors)
    short_grad, long_grad, query_sum, value_sum = attention_backward(
        shape, lengths, q, k, v, gm, short_p, long_p, mixed_t, packed_w, grad_first_sum
    )
    sums = sum_all(jnp.concatenate(
        [query_sum, value_sum, output_sum, inner_sum, down_sum, first_beta_sum, second_beta_sum], axis=1
    ).reshape(-1))
    outs = []
    at = 0
    for size in (width, width, width, inner_bias.shape[0], width, width, width):
        outs.append(lax.slice_in_dim(sums, at, at + size))
        at += size
    return (
        short_out.reshape(short_input.shape), short_grad.reshape(short_input.shape),
        long_out.reshape(long_input.shape), long_grad.reshape(long_input.shape), *outs,
    )


def gather_all(*shards):
    return [lax.all_gather(shard, "dp", axis=0, tiled=True) for shard in shards]


def sum_all(vector):
    return lax.psum(vector, "dp")


def solution(mesh):
    rows = P("dp", None, None)
    in_specs = (rows, P("dp"), rows, rows, P("dp"), rows) + (P("dp", None),) * 4 + (P(),) * 9
    out_specs = (rows,) * 4 + (P(),) * 7
    return jax.shard_map(local, mesh=mesh, in_specs=in_specs, out_specs=out_specs, check_vma=False)
```

profile of v0, /device:TPU:0, one launch (start us, length us, event | category | flops | bytes accessed | tf_op | source)
XLA Modules:
  0.0 419.7 jit_solution(46107418313719528)
XLA Ops:
  7.2 0.0 all-gather.7.cloned.1.call-start
  7.2 0.7 all-gather.7.cloned.1.call-update
  7.9 0.0 all-gather.5.cloned.1.call-start
  8.0 0.7 all-gather.5.cloned.1.call-update
  8.7 0.0 all-gather.9.cloned.1.call-start
  8.7 0.7 all-gather.9.cloned.1.call-update
  9.4 0.0 all-gather.11.cloned.1.call-start
  9.4 0.5 all-gather.11.cloned.1.call-update
  10.6 59.4 %all-gather.7.cloned.1.call-done.wo = bf16[1024,1024]{1,0:T(8,128)(2,1)} async-done(((bf16[32,1024]{1,0:T(8,128)(2,1)}), bf16[1024,1024]{1,0:T(8,128)(2,1)}) %all-gather.7.cloned.1.call-update) | async-done | bytes 2097168 | tf_op jit(solution)/shard_map/all_gather | solution.py:428
  70.0 71.3 %all-gather.5.cloned.1.call-done.wq.wk.wv = bf16[1024,3072]{1,0:T(8,128)(2,1)} async-done(((bf16[32,3072]{1,0:T(8,128)(2,1)}), bf16[1024,3072]{1,0:T(8,128)(2,1)}) %all-gather.5.cloned.1.call-update) | async-done | bytes 6291472 | tf_op jit(solution)/shard_map/all_gather | solution.py:428
  141.2 43.9 %attention_forward.1 = (bf16[896,1024]{1,0:T(8,128)(2,1)}, bf16[896,1024]{1,0:T(8,128)(2,1)}, bf16[896,1024]{1,0:T(8,128)(2,1)}, bf16[3,16,128,128]{3,2,1,0:T(8,...) custom-call(s32[3]{0:T(128)} %short_lengths.5, ...), custom_call_target="tpu_custom_call" | custom-call | tf_op jit(solution)/shard_map/attention_forward/pallas_call | solution.py:124
  185.1 34.7 %all-gather.9.cloned.1.call-done.wi = bf16[1024,4096]{1,0:T(8,128)(2,1)} async-done(((bf16[32,4096]{1,0:T(8,128)(2,1)}), bf16[1024,4096]{1,0:T(8,128)(2,1)}) %all-gather.9.cloned.1.call-update) | async-done | bytes 8388624 | tf_op jit(solution)/shard_map/all_gather | solution.py:428
  219.9 24.6 %inner_forward.1 = (bf16[896,4096]{1,0:T(8,128)(2,1)}, bf16[896,4096]{1,0:T(8,128)(2,1)}) custom-call(f32[896,1024]{1,0:T(8,128)} %get-tuple-element.34.xhat, f32[1,1024]{1,0:T(1,128)} %bitcast.23, f32[1,1024]{1,0:T(1,128)} %bitcast.25, bf16[1024,4096]{1,0:T(8,128)(2,1)} %all-gather.9.cloned.1.call-done.wi, f32[1,4096]{1,0:T(1,128)} %bitcast.27), custom_call_target="tpu_custom_call" | custom-call | tf_op jit(solution)/shard_map/inner_forward/pallas_call | solution.py:180
  244.4 54.2 %all-gather.11.cloned.1.call-done.wd = bf16[4096,1024]{1,0:T(8,128)(2,1)} async-done(((bf16[128,1024]{1,0:T(8,128)(2,1)}), bf16[4096,1024]{1,0:T(8,128)(2,1)}) %all-gather.11.cloned.1.call-update) | async-done | bytes 8388624 | tf_op jit(solution)/shard_map/all_gather | solution.py:428
  298.7 43.4 %feed_back.1 = (bf16[384,1024]{1,0:T(8,128)(2,1)}, bf16[512,1024]{1,0:T(8,128)(2,1)}, bf16[896,1024]{1,0:T(8,128)(2,1)}, f32[896,1024]{1,0:T(8,128)}, f32[1,1024...) custom-call(s32[3]{0:T(128)} %short_lengths.5, ...), custom_call_target="tpu_custom_call" | custom-call | tf_op jit(solution)/shard_map/feed_back/pallas_call | solution.py:265
  342.0 0.0 copy-start.4
  342.1 0.0 copy-start
  342.1 0.0 copy-start.3
  342.1 0.0 copy-start.2
  342.1 0.0 copy-start.1
  342.1 28.7 %attention_backward.1 = (bf16[384,1024]{1,0:T(8,128)(2,1)}, bf16[512,1024]{1,0:T(8,128)(2,1)}, f32[1,1024]{1,0:T(1,128)}, f32[1,1024]{1,0:T(1,128)}) custom-call(s32[3]{0:T(128)} %short_lengths.5, s32[1]{0:T(128)S(6)} %copy.36.long_lengths, bf16[896,1024]{1,0:T(8,128)(2,1)} %get-tuple-element.39.q, bf16[896,1024]{1,0:T(8,128)(2,1)} %get-tuple-element.40.k, ...), custom_call_target="tpu_custom_call" | custom-call | tf_op jit(solution)/shard_map/attention_backward/pallas_call | solution.py:367
  370.8 0.7 constant_dynamic-update-slice_fusion.6
  371.5 0.7 constant_dynamic-update-slice_fusion.5
  372.2 0.0 copy-done.4
  372.2 0.0 copy-done
  372.3 0.0 copy-done.3
  372.3 0.0 copy-done.2
  372.3 0.0 copy-done.1
  372.3 39.6 %psum.7 = f32[10240]{0:T(1024)S(1)} all-reduce(f32[10240]{0:T(1024)S(1)} %bitcast.22), channel_id=1, replica_groups=mesh['dp'=32] {'dp'}, use_global_device_ids=true, to_apply=%region_0.0 | all-reduce | flops 10240 | bytes 81920 | tf_op jit(solution)/shard_map/psum | solution.py:432
  412.0 0.6 slice.31
  412.6 0.6 fusion
  (5 shorter events, 0.0 us)
Async XLA Ops:
  7.2 62.8 %all-gather.7.cloned.1.call-start = ((), (), s32[]{:S(2)}) async-start(), calls=%async_computation.1 | async-start | bytes 2162688 | tf_op jit(solution)/shard_map/all_gather | solution.py:428
  7.9 133.3 %all-gather.5.cloned.1.call-start = ((), (), s32[]{:S(2)}) async-start(), calls=%async_computation | async-start | bytes 6488064 | tf_op jit(solution)/shard_map/all_gather | solution.py:428
  8.7 211.2 %all-gather.9.cloned.1.call-start = ((), (), s32[]{:S(2)}) async-start(), calls=%async_computation.2 | async-start | bytes 8650752 | tf_op jit(solution)/shard_map/all_gather | solution.py:428
  9.4 289.3 %all-gather.11.cloned.1.call-start = ((), (), s32[]{:S(2)}) async-start(), calls=%async_computation.3 | async-start | bytes 8650752 | tf_op jit(solution)/shard_map/all_gather | solution.py:428
  342.0 30.2 %copy-start.4 = (f32[1,1024]{1,0:T(1,128)S(1)}, f32[1,1024]{1,0:T(1,128)}, u32[]{:S(2)}) copy-start(f32[1,1024]{1,0:T(1,128)} %get-tuple-element.52) | copy-start | bytes 12292
  342.1 30.2 %copy-start = (f32[1,4096]{1,0:T(1,128)S(1)}, f32[1,4096]{1,0:T(1,128)}, u32[]{:S(2)}) copy-start(f32[1,4096]{1,0:T(1,128)} %get-tuple-element.53) | copy-start | bytes 49156
  342.1 30.2 %copy-start.3 = (f32[1,1024]{1,0:T(1,128)S(1)}, f32[1,1024]{1,0:T(1,128)}, u32[]{:S(2)}) copy-start(f32[1,1024]{1,0:T(1,128)} %get-tuple-element.54) | copy-start | bytes 12292
  342.1 30.2 %copy-start.2 = (f32[1,1024]{1,0:T(1,128)S(1)}, f32[1,1024]{1,0:T(1,128)}, u32[]{:S(2)}) copy-start(f32[1,1024]{1,0:T(1,128)} %get-tuple-element.55) | copy-start | bytes 12292
  342.1 30.2 %copy-start.1 = (f32[1,1024]{1,0:T(1,128)S(1)}, f32[1,1024]{1,0:T(1,128)}, u32[]{:S(2)}) copy-start(f32[1,1024]{1,0:T(1,128)} %get-tuple-element.56) | copy-start | bytes 12292
Sparse Core Ops, SparseCore 0:
  10.9 59.0 all-gather.6
  72.8 68.3 all-gather.4
  144.1 75.7 all-gather.8
  222.6 76.0 all-gather.10
where the time goes:
time: 420 us
  waiting for transfers between devices  222 us (53%)
  Pallas kernels  141 us (34%)
  blocking collectives  39.6 us (9%)
  between operations  14.5 us (3%)
    all_gather x4, waiting for transfers between devices, gather_all(): return [lax.all_gather(shard, 'dp', axis=0, tiled=True) for shard in shards]  220 us
    pallas_call x1, Pallas kernels, attention_forward(): pl.pallas_call(partial(attention_forward_kernel, shape), grid=(steps,), i...  43.9 us
    pallas_call x1, Pallas kernels, feed_back(): pl.pallas_call(partial(feed_kernel, shape, steps), grid=(2 * steps,), in_...  43.4 us
    psum x1, blocking collectives, sum_all(): return lax.psum(vector, 'dp')  39.6 us
    pallas_call x1, Pallas kernels, attention_backward(): pl.pallas_call(partial(attention_backward_kernel, shape), grid=(steps,),...  28.7 us
    pallas_call x1, Pallas kernels, inner_forward(): pl.pallas_call(inner_kernel, grid=(units // block,), in_specs=[whole((row...  24.6 us
  transfers between devices with their start and end apart: 4, of which 4 were waited for; matrix products, arithmetic and copies ran while one was open for 0% of the time, Pallas kernels for 16%

commit v1 on v0

--- a/solution.py
+++ b/solution.py
@@ -52,25 +52,55 @@
 
 
 def attention_forward_kernel(
-    shape, short_lengths, long_lengths, short_x, long_x, wq, wk, wv, wo, qb, vb, ob,
-    q_out, k_out, v_out, short_p, long_p, mixed_t, xhat_out, rstd_out, x_all, mixed,
+    shape, slots, me, short_lengths, long_lengths, short_x, long_x, *refs,
 ):
+    pieces, refs = refs[: 3 * len(slots)], refs[3 * len(slots) :]
+    (
+        qb, vb, ob, q_out, k_out, v_out, short_p, long_p, mixed_t, xhat_out, rstd_out, packed_out, output_out,
+        x_all, mixed, packed, wo, in_sems, out_sems,
+    ) = refs
     step = pl.program_id(0)
     steps = pl.num_programs(0)
     short_seqs, short_len, long_seqs, long_len = shape
     base = short_seqs * short_len
-    width = wq.shape[1]
+    width = q_out.shape[1]
+    half_width = packed.shape[2]
     short_spans, long_spans = sequences(*shape)
+    targets = (packed.at[0], packed.at[1], wo)
 
     @pl.when(step == 0)
     def _():
+        for part in range(3):
+            for ref, masks in zip(pieces[part::3], slots):
+                tall = ref.shape[0] // len(masks)
+                for slot, mask in enumerate(masks):
+                    mask = jnp.where(jnp.bitwise_and(me[0], 1) == 0, mask[0], mask[1])
+                    place = pl.multiple_of(jnp.bitwise_xor(me[0], mask) * tall, tall)
+                    pltpu.make_async_copy(
+                        ref.at[pl.ds(slot * tall, tall)], targets[part].at[pl.ds(place, tall)], in_sems.at[part]
+                    ).start()
         x_all[:base, :] = short_x[...]
         x_all[base:, :] = long_x[...]
 
+    keeps = [
+        pltpu.make_async_copy(packed.at[0], packed_out.at[0], out_sems.at[0]),
+        pltpu.make_async_copy(packed.at[1], packed_out.at[1], out_sems.at[1]),
+        pltpu.make_async_copy(wo, output_out, out_sems.at[2]),
+    ]
+    for part, first_step in enumerate((0, steps // 2, steps - 1)):
+        @pl.when(step == first_step)
+        def _():
+            pltpu.make_async_copy(targets[part], targets[part], in_sems.at[part]).wait()
+            keeps[part].start()
+
     x = x_all[...]
-    q_out[...] = ((dot(x, wq[...]) + qb[...]).astype(BF).astype(F32) * HEAD_DIM ** (-0.5)).astype(BF)
-    k_out[...] = dot(x, wk[...]).astype(BF)
-    v_out[...] = (dot(x, wv[...]) + vb[...]).astype(BF)
+    side = step // (steps // 2)
+    turn = lax.rem(step, steps // 2)
+    third = half_width // 3
+    weight = lambda which: packed[side, :, pl.ds(pl.multiple_of(which * third + turn * width, width), width)]
+    q_out[...] = ((dot(x, weight(0)) + qb[...]).astype(BF).astype(F32) * HEAD_DIM ** (-0.5)).astype(BF)
+    k_out[...] = dot(x, weight(1)).astype(BF)
+    v_out[...] = (dot(x, weight(2)) + vb[...]).astype(BF)
     for pair in range(width // 128):
         lanes = slice(128 * pair, 128 * pair + 128)
         v_t = flip(v_out[:, lanes])
@@ -107,9 +137,11 @@
         rstd = lax.rsqrt(spread + 1e-06)
         xhat_out[...] = center * rstd
         rstd_out[...] = rstd
-
-
-def attention_forward(shape, lengths, xs, packed_w, output_w, vectors):
+        for keep in keeps:
+            keep.wait()
+
+
+def attention_forward(shape, lengths, xs, weights, vectors):
     short_seqs, short_len, long_seqs, long_len = shape
     rows = short_seqs * short_len + long_seqs * long_len
     width = xs[0].shape[1]
@@ -118,23 +150,23 @@
     steps = width // block
     whole = lambda shp: pl.BlockSpec(shp, lambda j: (0,) * len(shp))
     smem = pl.BlockSpec(memory_space=pltpu.SMEM)
-    column = lambda off: pl.BlockSpec((width, block), lambda j: (0, j + off * steps))
+    anywhere = pl.BlockSpec(memory_space=pl.ANY)
     row_block = pl.BlockSpec((1, block), lambda j: (0, j))
     out_col = pl.BlockSpec((rows, block), lambda j: (0, j))
+    half_width = 3 * width // 2
     return pl.pallas_call(
-        partial(attention_forward_kernel, shape),
+        partial(attention_forward_kernel, shape, weights["slots"]),
         grid=(steps,),
         in_specs=[
-            smem, smem, whole(xs[0].shape), whole(xs[1].shape),
-            column(0), column(1), column(2), whole((width, width)),
-            row_block, row_block, whole((1, width)),
+            smem, smem, smem, whole(xs[0].shape), whole(xs[1].shape),
+            *[anywhere] * len(weights["pieces"]), row_block, row_block, whole((1, width)),
         ],
         out_specs=[
             out_col, out_col, out_col,
             pl.BlockSpec((short_seqs, heads, short_len, short_len), lambda j: (0, j, 0, 0)),
             pl.BlockSpec((long_seqs, heads, long_len, long_len), lambda j: (0, j, 0, 0)),
             pl.BlockSpec((block, rows), lambda j: (j, 0)),
-            whole((rows, width)), whole((rows, 1)),
+            whole((rows, width)), whole((rows, 1)), anywhere, anywhere,
         ],
         out_shape=[
             jax.ShapeDtypeStruct((rows, width), BF),
@@ -145,11 +177,21 @@
             jax.ShapeDtypeStruct((width, rows), F32),
             jax.ShapeDtypeStruct((rows, width), F32),
             jax.ShapeDtypeStruct((rows, 1), F32),
-        ],
-        scratch_shapes=[pltpu.VMEM((rows, width), BF), pltpu.VMEM((rows, width), BF)],
+            jax.ShapeDtypeStruct((2, width, half_width), BF),
+            jax.ShapeDtypeStruct((width, width), BF),
+        ],
+        scratch_shapes=[
+            pltpu.VMEM((rows, width), BF), pltpu.VMEM((rows, width), BF),
+            pltpu.VMEM((2, width, half_width), BF), pltpu.VMEM((width, width), BF),
+            pltpu.SemaphoreType.DMA((3,)), pltpu.SemaphoreType.DMA((3,)),
+        ],
         compiler_params=pltpu.CompilerParams(vmem_limit_bytes=VMEM_BYTES),
+        cost_estimate=pl.CostEstimate(flops=36 * 10**9, bytes_accessed=40 * 10**6, transcendentals=5 * 10**6),
         name="attention_forward",
-    )(*lengths, *xs, packed_w, packed_w, packed_w, output_w, vectors["query_bias"], vectors["value_bias"], vectors["output_bias"])
+    )(
+        weights["me"], *lengths, *xs, *weights["pieces"],
+        vectors["query_bias"], vectors["value_bias"], vectors["output_bias"],
+    )
 
 
 def gelu_and_slope(value):
@@ -166,15 +208,27 @@
     def _():
         first[...] = (xhat[...] * gain[...] + beta[...]).astype(BF)
 
-    value = dot(first[...], wi[...]) + bi[...]
+    value = dot(first[...], wi[...].reshape(first.shape[1], -1)) + bi[...]
     act, slp = gelu_and_slope(value)
     active[...] = act.astype(BF)
     slope[...] = slp.astype(BF)
 
 
-def inner_forward(xhat, gain, beta, inner_w, inner_bias, block=512):
+def inner_block(feed_w, block, turn):
+    shards, _, width = feed_w.shape
+    per = width // block
+    return pl.BlockSpec((shards, width // shards, block), lambda j: (0, turn(j) // per, lax.rem(turn(j), per)))
+
+
+def down_block(feed_w, block, turn):
+    shards, tall, width = feed_w.shape
+    tall = tall // 2
+    return pl.BlockSpec((block // tall, tall, width), lambda j: (turn(j), 1, 0))
+
+
+def inner_forward(xhat, gain, beta, feed_w, inner_bias, block=512):
     rows, width = xhat.shape
-    units = inner_w.shape[1]
+    units = inner_bias.shape[1]
     whole = lambda shp: pl.BlockSpec(shp, lambda j: (0,) * len(shp))
     col = pl.BlockSpec((rows, block), lambda j: (0, j))
     return pl.pallas_call(
@@ -182,14 +236,14 @@
         grid=(units // block,),
         in_specs=[
             whole((rows, width)), whole((1, width)), whole((1, width)),
-            pl.BlockSpec((width, block), lambda j: (0, j)), pl.BlockSpec((1, block), lambda j: (0, j)),
+            inner_block(feed_w, block, lambda j: j), pl.BlockSpec((1, block), lambda j: (0, j)),
         ],
         out_specs=[col, col],
         out_shape=[jax.ShapeDtypeStruct((rows, units), BF)] * 2,
         scratch_shapes=[pltpu.VMEM((rows, width), BF)],
         compiler_params=pltpu.CompilerParams(vmem_limit_bytes=VMEM_BYTES),
         name="inner_forward",
-    )(xhat, gain, beta, inner_w, inner_bias)
+    )(xhat, gain, beta, feed_w, inner_bias)
 
 
 def norm_gradient(grad, xhat, rstd, gain):
@@ -215,7 +269,7 @@
 
     @pl.when(step < steps)
     def _():
-        total[...] += dot(active[...], wd[...])
+        total[...] += dot(active[...], wd[...].reshape(-1, wd.shape[2]))
 
     @pl.when(step == steps - 1)
     def _():
@@ -238,9 +292,9 @@
 
     @pl.when(step >= steps)
     def _():
-        grad_inner = (dot_t(grad_down[...], wd[...]) * slope[...].astype(F32)).astype(BF)
+        grad_inner = (dot_t(grad_down[...], wd[...].reshape(-1, wd.shape[2])) * slope[...].astype(F32)).astype(BF)
         inner_sum[...] = jnp.sum(grad_inner.astype(F32), axis=0, keepdims=True)
-        total[...] += dot_t(grad_inner, wi[...])
+        total[...] += dot_t(grad_inner, wi[...].reshape(total.shape[1], -1))
 
     @pl.when(step == 2 * steps - 1)
     def _():
@@ -253,9 +307,9 @@
         grad_mixed[...] = dot_t(branch, wo[...]).astype(BF)
 
 
-def feed_back(shape, lengths, xhat, rstd, cts, active, slope, down_w, inner_w, output_w, vectors, block=512):
+def feed_back(shape, lengths, xhat, rstd, cts, active, slope, feed_w, output_w, vectors, block=512):
     rows, width = xhat.shape
-    units = down_w.shape[0]
+    units = active.shape[1]
     steps = units // block
     whole = lambda shp: pl.BlockSpec(shp, lambda j: (0,) * len(shp))
     smem = pl.BlockSpec(memory_space=pltpu.SMEM)
@@ -269,8 +323,8 @@
             smem, smem, whole((rows, width)), whole((rows, 1)), whole(cts[0].shape), whole(cts[1].shape),
             pl.BlockSpec((rows, block), lambda j: (0, jnp.minimum(j, steps - 1))),
             pl.BlockSpec((rows, block), lambda j: (0, late(j))),
-            pl.BlockSpec((block, width), lambda j: (lax.rem(j, steps), 0)),
-            pl.BlockSpec((width, block), lambda j: (0, late(j))),
+            down_block(feed_w, block, lambda j: lax.rem(j, steps)),
+            inner_block(feed_w, block, late),
             whole((width, width)), vec, vec, vec, vec, vec,
         ],
         out_specs=[
@@ -286,7 +340,7 @@
         compiler_params=pltpu.CompilerParams(vmem_limit_bytes=VMEM_BYTES),
         name="feed_back",
     )(
-        *lengths, xhat, rstd, *cts, active, slope, down_w, inner_w, output_w,
+        *lengths, xhat, rstd, *cts, active, slope, feed_w, feed_w, output_w,
         vectors["first_gain"], vectors["first_beta"], vectors["second_gain"], vectors["second_beta"], vectors["down_bias"],
     )
 
@@ -331,9 +385,9 @@
     query_sum[...] = jnp.sum(grad_packed[:, :width].astype(F32), axis=0, keepdims=True)
     value_sum[...] = jnp.sum(grad_packed[:, 2 * width :].astype(F32), axis=0, keepdims=True)
     part = (
-        dot_t(grad_packed[:, :width], wq[...])
-        + dot_t(grad_packed[:, width : 2 * width], wk[...])
-        + dot_t(grad_packed[:, 2 * width :], wv[...])
+        dot_t(grad_packed[:, :width], wq[0])
+        + dot_t(grad_packed[:, width : 2 * width], wk[0])
+        + dot_t(grad_packed[:, 2 * width :], wv[0])
     )
 
     @pl.when(step == 0)
@@ -361,7 +415,8 @@
     base = short_seqs * short_len
     whole = lambda shp: pl.BlockSpec(shp, lambda j: (0,) * len(shp))
     smem = pl.BlockSpec(memory_space=pltpu.SMEM)
-    column = lambda off: pl.BlockSpec((width, block), lambda j: (0, j + off * steps))
+    half = steps // 2
+    column = lambda off: pl.BlockSpec((1, width, block), lambda j: (j // half, 0, lax.rem(j, half) + off * half))
     col = pl.BlockSpec((rows, block), lambda j: (0, j))
     vec = pl.BlockSpec((1, block), lambda j: (0, j))
     return pl.pallas_call(
@@ -401,12 +456,12 @@
     vectors = {name: item.reshape(1, -1) for name, item in vectors.items()}
     xs = (short_input.reshape(-1, width), long_input.reshape(-1, width))
     cts = (short_cotangent.reshape(-1, width), long_cotangent.reshape(-1, width))
-    packed_w, output_w, inner_w, down_w = gather_all(packed_weight, output_weight, inner_weight, down_weight)
-    q, k, v, short_p, long_p, mixed_t, xhat, rstd = attention_forward(shape, lengths, xs, packed_w, output_w, vectors)
-    active, slope = inner_forward(xhat, vectors["first_gain"], vectors["first_beta"], inner_w, vectors["inner_bias"])
+    weights = gather_weights(packed_weight, output_weight, inner_weight, down_weight)
+    q, k, v, short_p, long_p, mixed_t, xhat, rstd, packed_w, output_w = attention_forward(shape, lengths, xs, weights, vectors)
+    active, slope = inner_forward(xhat, vectors["first_gain"], vectors["first_beta"], weights["feed"], vectors["inner_bias"])
     (
         short_out, long_out, gm, grad_first_sum, second_beta_sum, down_sum, inner_sum, first_beta_sum, output_sum,
-    ) = feed_back(shape, lengths, xhat, rstd, cts, active, slope, down_w, inner_w, output_w, vectors)
+    ) = feed_back(shape, lengths, xhat, rstd, cts, active, slope, weights["feed"], output_w, vectors)
     short_grad, long_grad, query_sum, value_sum = attention_backward(
         shape, lengths, q, k, v, gm, short_p, long_p, mixed_t, packed_w, grad_first_sum
     )
@@ -424,12 +479,85 @@
     )
 
 
-def gather_all(*shards):
-    return [lax.all_gather(shard, "dp", axis=0, tiled=True) for shard in shards]
+def exchange(block, mask):
+    count = lax.axis_size("dp")
+    return lax.ppermute(block, "dp", [(i, i ^ mask(i)) for i in range(count)])
+
+
+CORE, X, Y, Z_NEAR, Z_FAR = 1, 2, 4, 8, 16
+
+
+def side_first(index):
+    return X if index & CORE == 0 else Y
+
+
+def side_second(index):
+    return Y if index & CORE == 0 else X
+
+
+def gather_by_exchange(shard):
+    held = jnp.concatenate([shard, exchange(shard, lambda i: Z_FAR)])
+    held = jnp.concatenate([held, exchange(held, side_first)])
+    held = jnp.concatenate([held, exchange(held, lambda i: Z_NEAR)])
+    other = exchange(held, side_second)
+    return [held, other, exchange(held, lambda i: CORE), exchange(other, lambda i: CORE)]
+
+
+def exchange_slots():
+    def mask(core, swap, far, slot):
+        owner = core ^ swap
+        return (
+            swap * CORE + far * side_second(owner) + Z_FAR * (slot & 1)
+            + side_first(owner) * (slot >> 1 & 1) + Z_NEAR * (slot >> 2)
+        )
+
+    return [
+        [(mask(0, swap, far, slot), mask(1, swap, far, slot)) for slot in range(8)]
+        for swap in (0, 1) for far in (0, 1)
+    ]
+
+
+def gather_weights(packed, output, inner, down):
+    count = lax.axis_size("dp")
+    width = output.shape[1]
+    half = width // 2
+    sides = [
+        jnp.concatenate([packed[:, i * width + at : i * width + at + half] for i in range(3)], axis=1) for at in (0, half)
+    ]
+    parts = [*sides, output]
+    tall = inner.shape[0]
+    blocks = inner.shape[1] // width
+    if count == 32:
+        feed = jnp.concatenate(
+            [inner.reshape(tall, blocks, width).transpose(1, 0, 2).reshape(blocks * tall, width), down], axis=0
+        )
+        feed = lax.all_gather(feed, "dp", axis=0, tiled=False)
+        gathered = [gather_by_exchange(part) for part in parts]
+        return dict(
+            me=lax.axis_index("dp").reshape(1).astype(jnp.int32), slots=exchange_slots(),
+            pieces=[gathered[part][piece] for piece in range(4) for part in range(3)], feed=feed,
+        )
+    whole = [lax.all_gather(part, "dp", axis=0, tiled=True) for part in (*parts, inner, down)]
+    shards = 32
+    feed = jnp.concatenate(
+        [
+            whole[3].reshape(shards, -1, blocks, width).transpose(0, 2, 1, 3).reshape(shards, -1, width),
+            whole[4].reshape(shards, -1, width),
+        ],
+        axis=1,
+    )
+    return dict(me=jnp.zeros((1,), jnp.int32), slots=[[(i, i) for i in range(shards)]], pieces=whole[:3], feed=feed)
 
 
 def sum_all(vector):
-    return lax.psum(vector, "dp")
+    count = lax.axis_size("dp")
+    if count & (count - 1):
+        return lax.psum(vector, "dp")
+    bit = 1
+    while bit < count:
+        vector = vector + exchange(vector, lambda i: bit)
+        bit *= 2
+    return vector
 
 
 def solution(mesh):

time: 420 us -> 283 us (0.67)
  waiting for transfers between devices: 222 us -> 72.6 us
  starting transfers between devices: 0.15 us -> 46 us
  blocking collectives: 39.6 us -> 0 us
    all_gather x4 -> x1, waiting for transfers between devices: 220 us -> 0.32 us  [gather_weights(): feed = lax.all_gather(feed, 'dp', axis=0, tiled=False)]
    ppermute x0 -> x23, waiting for transfers between devices: none -> 72.3 us  [exchange(): return lax.ppermute(block, 'dp', [(i, i ^ mask(i)) for i in range(count)])]
    ppermute x0 -> x23, starting transfers between devices: none -> 46 us  [exchange(): return lax.ppermute(block, 'dp', [(i, i ^ mask(i)) for i in range(count)])]
    psum x1 -> x0, blocking collectives: 39.6 us -> none  [sum_all(): return lax.psum(vector, 'dp')]
  transfers between devices with their start and end apart: 4 -> 24, of which waited for: 4 -> 15; matrix products, arithmetic and copies ran while one was open for 0% -> 0% of each run, Pallas kernels for 16% -> 16%
where the time goes in v1:
time: 283 us; the launch traced here: 281 us
  Pallas kernels  142 us (50%)
  waiting for transfers between devices  72.6 us (26%)
  starting transfers between devices  46 us (16%)
  between operations  15 us (5%)
  local copies, waits for them, and re-layouts  3.79 us (1%)
    ppermute x23, waiting for transfers between devices, exchange(): return lax.ppermute(block, 'dp', [(i, i ^ mask(i)) for i in range(count)])  72.3 us
    ppermute x23, starting transfers between devices, exchange(): return lax.ppermute(block, 'dp', [(i, i ^ mask(i)) for i in range(count)])  46 us
    pallas_call x1, Pallas kernels, attention_forward(): pl.pallas_call(partial(attention_forward_kernel, shape, weights['slots'])...  44.5 us
    pallas_call x1, Pallas kernels, feed_back(): pl.pallas_call(partial(feed_kernel, shape, steps), grid=(2 * steps,), in_...  43.9 us
    pallas_call x1, Pallas kernels, attention_backward(): pl.pallas_call(partial(attention_backward_kernel, shape), grid=(steps,),...  28.8 us
    pallas_call x1, Pallas kernels, inner_forward(): pl.pallas_call(inner_kernel, grid=(units // block,), in_specs=[whole((row...  24.7 us
  transfers between devices with their start and end apart: 24, of which 15 were waited for; matrix products, arithmetic and copies ran while one was open for 0% of the time, Pallas kernels for 16%

profile of v1, /device:TPU:0, one launch (start us, length us, event | category | flops | bytes accessed | tf_op | source)
XLA Modules:
  0.0 281.4 jit_solution(7479957939702671879)
XLA Ops:
  7.2 1.0 copy.33
  8.3 1.8 pad_maximum_fusion.2
  10.1 4.1 %collective-permute-start.6 = (bf16[32,1024]{1,0:T(8,128)(2,1)S(1)}, bf16[32,1024]{1,0:T(8,128)(2,1)S(1)}, u32[]{:S(2)}, u32[]{:S(2)}) collective-permute-start(bf16[32,1024]{1,0:T(8,128)(2,1)S(1)} %copy-done.2), channel_id=1, source_target_pairs={{0,16},{1,17},{2,18},{3,19},{4,20},{5,21},{6,22},{7,23},{8,24},{9,... | collective-permute-start | bytes 196616 | tf_op jit(solution)/shard_map/ppermute | solution.py:484
  14.2 0.1 collective-permute-start
  14.3 3.0 %collective-permute-start.3 = (bf16[32,1536]{1,0:T(8,128)(2,1)S(1)}, bf16[32,1536]{1,0:T(8,128)(2,1)S(1)}, u32[]{:S(2)}, u32[]{:S(2)}) collective-permute-start(bf16[32,1536]{1,0:T(8,128)(2,1)S(1)} %pad_maximum_fusion.10), channel_id=1, source_target_pairs={{0,16},{1,17},{2,18},{3,19},{4,20},{5,21},{6,22},{7,23},{8,24},{9,... | collective-permute-start | bytes 294920 | tf_op jit(solution)/shard_map/ppermute | solution.py:484
  17.3 0.6 collective-permute-done.6
  17.9 2.0 collective-permute-start.7
  19.9 6.5 %collective-permute-done.3 = bf16[32,1536]{1,0:T(8,128)(2,1)S(1)} collective-permute-done((bf16[32,1536]{1,0:T(8,128)(2,1)S(1)}, bf16[32,1536]{1,0:T(8,128)(2,1)S(1)}, u32[]{:S(2)}, u32[]{:S(2)}) %collective-permute-start.3) | collective-permute-done | bytes 98336 | tf_op jit(solution)/shard_map/ppermute | solution.py:484
  26.4 1.9 collective-permute-start.4
  28.3 0.3 collective-permute-start.1
  28.6 3.6 %collective-permute-done.4 = bf16[64,1536]{1,0:T(8,128)(2,1)S(1)} collective-permute-done((bf16[64,1536]{1,0:T(8,128)(2,1)S(1)}, bf16[64,1536]{1,0:T(8,128)(2,1)S(1)}, u32[]{:S(2)}, u32[]{:S(2)}) %collective-permute-start.4) | collective-permute-done | bytes 196640 | tf_op jit(solution)/shard_map/ppermute | solution.py:484
  32.2 4.5 %collective-permute-start.5 = (bf16[128,1536]{1,0:T(8,128)(2,1)S(1)}, bf16[128,1536]{1,0:T(8,128)(2,1)S(1)}, u32[]{:S(2)}, u32[]{:S(2)}) collective-permute-start(bf16[128,1536]{1,0:T(8,128)(2,1)S(1)} %pad_maximum_fusion.4), channel_id=1, source_target_pairs={{0,8},{1,9},{2,10},{3,11},{4,12},{5,13},{6,14},{7,15},{8,0},{9,1},... | collective-permute-start | bytes 1179656 | tf_op jit(solution)/shard_map/ppermute | solution.py:484
  36.7 2.1 collective-permute-start.2
  38.8 0.1 collective-permute-start.8
  38.9 10.2 %collective-permute-done.5 = bf16[128,1536]{1,0:T(8,128)(2,1)S(1)} collective-permute-done((bf16[128,1536]{1,0:T(8,128)(2,1)S(1)}, bf16[128,1536]{1,0:T(8,128)(2,1)S(1)}, u32[]{:S(2)}, u32[]{:S(2)}) %collective-permute-start.5) | collective-permute-done | bytes 393248 | tf_op jit(solution)/shard_map/ppermute | solution.py:484
  49.1 0.1 pad_maximum_fusion.1.refs_1_
  49.2 2.2 collective-permute-start.10
  51.4 19.2 %collective-permute-done.2 = bf16[128,1536]{1,0:T(8,128)(2,1)S(1)} collective-permute-done((bf16[128,1536]{1,0:T(8,128)(2,1)S(1)}, bf16[128,1536]{1,0:T(8,128)(2,1)S(1)}, u32[]{:S(2)}, u32[]{:S(2)}) %collective-permute-start.2) | collective-permute-done | bytes 393248 | tf_op jit(solution)/shard_map/ppermute | solution.py:484
  70.7 1.7 collective-permute-start.9
  72.4 10.9 %collective-permute-done.8 = bf16[128,1024]{1,0:T(8,128)(2,1)S(1)} collective-permute-done((bf16[128,1024]{1,0:T(8,128)(2,1)S(1)}, bf16[128,1024]{1,0:T(8,128)(2,1)S(1)}, u32[]{:S(2)}, u32[]{:S(2)}) %collective-permute-start.8) | collective-permute-done | bytes 262176 | tf_op jit(solution)/shard_map/ppermute | solution.py:484
  83.3 0.1 collective-permute-start.14
  83.4 1.3 collective-permute-start.11
  84.7 0.4 collective-permute-start.13
  85.2 0.1 collective-permute-done.14.refs_8_
  85.3 0.1 collective-permute-start.12
  85.4 0.4 collective-permute-start.16
  85.8 0.1 collective-permute-start.15
  86.0 10.3 %collective-permute-done.11.refs_5_ = bf16[256,1024]{1,0:T(8,128)(2,1)} collective-permute-done((bf16[256,1024]{1,0:T(8,128)(2,1)S(1)}, bf16[256,1024]{1,0:T(8,128)(2,1)}, u32[]{:S(2)}, u32[]{:S(2)}) %collective-permute-start.11) | collective-permute-done | bytes 524320 | tf_op jit(solution)/shard_map/ppermute | solution.py:484
  97.0 1.6 collective-permute-done.17.refs_11_
  98.6 44.5 %attention_forward.1 = (bf16[896,1024]{1,0:T(8,128)(2,1)}, bf16[896,1024]{1,0:T(8,128)(2,1)}, bf16[896,1024]{1,0:T(8,128)(2,1)}, bf16[3,16,128,128]{3,2,1,0:T(8,...) custom-call(s32[1]{0:T(128)} %bitcast.me, ...), custom_call_target="tpu_custom_call" | custom-call | flops 35999997952 | bytes 40000000 | tf_op jit(solution)/shard_map/attention_forward/pallas_call | solution.py:157
  143.1 0.3 all-gather.3.cloned.1.call-done
  143.4 24.7 %inner_forward.1 = (bf16[896,4096]{1,0:T(8,128)(2,1)}, bf16[896,4096]{1,0:T(8,128)(2,1)}) custom-call(f32[896,1024]{1,0:T(8,128)} %get-tuple-element.36.xhat, f32[1,1024]{1,0:T(1,128)} %bitcast.37, f32[1,1024]{1,0:T(1,128)} %bitcast.39, bf16[32,256,1024]{2,1,0:T(8,128)(2,1)} %bitcast.27, f32[1,4096]{1,0:T(1,128)} %bitcast.36), custom_call_target="tpu_custom_call" | custom-call | tf_op jit(solution)/shard_map/inner_forward/pallas_call | solution.py:234
  168.1 43.9 %feed_back.1 = (bf16[384,1024]{1,0:T(8,128)(2,1)}, bf16[512,1024]{1,0:T(8,128)(2,1)}, bf16[896,1024]{1,0:T(8,128)(2,1)}, f32[896,1024]{1,0:T(8,128)}, f32[1,1024...) custom-call(s32[3]{0:T(128)} %short_lengths.5, ...), custom_call_target="tpu_custom_call" | custom-call | tf_op jit(solution)/shard_map/feed_back/pallas_call | solution.py:319
  212.2 28.8 %attention_backward.1 = (bf16[384,1024]{1,0:T(8,128)(2,1)}, bf16[512,1024]{1,0:T(8,128)(2,1)}, f32[1,1024]{1,0:T(1,128)}, f32[1,1024]{1,0:T(1,128)}) custom-call(s32[3]{0:T(128)} %short_lengths.5, s32[1]{0:T(128)S(6)} %copy.43.long_lengths, bf16[896,1024]{1,0:T(8,128)(2,1)} %get-tuple-element.42.q, bf16[896,1024]{1,0:T(8,128)(2,1)} %get-tuple-element.43.k, ...), custom_call_target="tpu_custom_call" | custom-call | tf_op jit(solution)/shard_map/attention_backward/pallas_call | solution.py:422
  241.0 0.7 constant_dynamic-update-slice_fusion.10
  241.7 0.7 constant_dynamic-update-slice_fusion.9
  242.4 0.3 collective-permute-start.18
  242.8 0.9 collective-permute-done.18
  243.7 3.2 %collective-permute-start.19 = (f32[10240]{0:T(1024)S(1)}, f32[10240]{0:T(1024)S(1)}, u32[]{:S(2)}, u32[]{:S(2)}) collective-permute-start(f32[10240]{0:T(1024)S(1)} %add.15), channel_id=1, source_target_pairs={{0,2},{1,3},{2,0},{3,1},{4,6},{5,7},{6,4},{7,5},{8,10},{9,11},{10,... | collective-permute-start | bytes 122888 | tf_op jit(solution)/shard_map/ppermute | solution.py:484
  247.0 2.0 collective-permute-done.19
  249.0 1.6 collective-permute-start.20
  250.6 2.4 collective-permute-done.20
  253.0 3.6 %collective-permute-start.21 = (f32[10240]{0:T(1024)S(1)}, f32[10240]{0:T(1024)S(1)}, u32[]{:S(2)}, u32[]{:S(2)}) collective-permute-start(f32[10240]{0:T(1024)S(1)} %add.17), channel_id=1, source_target_pairs={{0,8},{1,9},{2,10},{3,11},{4,12},{5,13},{6,14},{7,15},{8,0},{9,1},... | collective-permute-start | bytes 122888 | tf_op jit(solution)/shard_map/ppermute | solution.py:484
  256.6 2.0 collective-permute-done.21
  258.6 12.8 %collective-permute-start.22 = (f32[10240]{0:T(1024)S(1)}, f32[10240]{0:T(1024)S(1)}, u32[]{:S(2)}, u32[]{:S(2)}) collective-permute-start(f32[10240]{0:T(1024)S(1)} %add.18), channel_id=1, source_target_pairs={{0,16},{1,17},{2,18},{3,19},{4,20},{5,21},{6,22},{7,23},{8,24},{9,... | collective-permute-start | bytes 122888 | tf_op jit(solution)/shard_map/ppermute | solution.py:484
  271.4 2.0 collective-permute-done.22
  273.4 0.6 slice.55
  274.0 0.6 fusion.1
  (60 shorter events, 0.5 us)
Async XLA Ops:
  7.2 2.9 %copy-start.2 = (bf16[32,1024]{1,0:T(8,128)(2,1)S(1)}, bf16[32,1024]{1,0:T(8,128)(2,1)}, u32[]{:S(2)}) copy-start(bf16[32,1024]{1,0:T(8,128)(2,1)} %param.26) | copy-start | bytes 196612
  7.2 7.0 %copy-start.3 = (bf16[32,3072]{1,0:T(8,128)(2,1)S(1)}, bf16[32,3072]{1,0:T(8,128)(2,1)}, u32[]{:S(2)}) copy-start(bf16[32,3072]{1,0:T(8,128)(2,1)} %param.25) | copy-start | bytes 589828
  7.2 136.2 %all-gather.3.cloned.1.call-start = ((), (), s32[]{:S(2)}) async-start(), calls=%async_computation | async-start | bytes 17301504 | tf_op jit(solution)/shard_map/all_gather | solution.py:534
  10.1 7.8 %collective-permute-start.6 = (bf16[32,1024]{1,0:T(8,128)(2,1)S(1)}, bf16[32,1024]{1,0:T(8,128)(2,1)S(1)}, u32[]{:S(2)}, u32[]{:S(2)}) collective-permute-start(bf16[32,1024]{1,0:T(8,128)(2,1)S(1)} %copy-done.2), channel_id=1, source_target_pairs={{0,16},{1,17},{2,18},{3,19},{4,20},{5,21},{6,22},{7,23},{8,24},{9,... | collective-permute-start | bytes 196616 | tf_op jit(solution)/shard_map/ppermute | solution.py:484
  14.2 14.0 %collective-permute-start = (bf16[32,1536]{1,0:T(8,128)(2,1)S(1)}, bf16[32,1536]{1,0:T(8,128)(2,1)S(1)}, u32[]{:S(2)}, u32[]{:S(2)}) collective-permute-start(bf16[32,1536]{1,0:T(8,128)(2,1)S(1)} %pad_maximum_fusion.9), channel_id=1, source_target_pairs={{0,16},{1,17},{2,18},{3,19},{4,20},{5,21},{6,22},{7,23},{8,24},{9,... | collective-permute-start | bytes 294920 | tf_op jit(solution)/shard_map/ppermute | solution.py:484
  14.3 12.0 %collective-permute-start.3 = (bf16[32,1536]{1,0:T(8,128)(2,1)S(1)}, bf16[32,1536]{1,0:T(8,128)(2,1)S(1)}, u32[]{:S(2)}, u32[]{:S(2)}) collective-permute-start(bf16[32,1536]{1,0:T(8,128)(2,1)S(1)} %pad_maximum_fusion.10), channel_id=1, source_target_pairs={{0,16},{1,17},{2,18},{3,19},{4,20},{5,21},{6,22},{7,23},{8,24},{9,... | collective-permute-start | bytes 294920 | tf_op jit(solution)/shard_map/ppermute | solution.py:484
  17.9 20.9 %collective-permute-start.7 = (bf16[64,1024]{1,0:T(8,128)(2,1)S(1)}, bf16[64,1024]{1,0:T(8,128)(2,1)S(1)}, u32[]{:S(2)}, u32[]{:S(2)}) collective-permute-start(bf16[64,1024]{1,0:T(8,128)(2,1)S(1)} %pad_maximum_fusion.8), channel_id=1, source_target_pairs={{0,2},{1,5},{2,0},{3,7},{4,6},{5,1},{6,4},{7,3},{8,10},{9,13},{10,... | collective-permute-start | bytes 393224 | tf_op jit(solution)/shard_map/ppermute | solution.py:484
  26.4 5.7 %collective-permute-start.4 = (bf16[64,1536]{1,0:T(8,128)(2,1)S(1)}, bf16[64,1536]{1,0:T(8,128)(2,1)S(1)}, u32[]{:S(2)}, u32[]{:S(2)}) collective-permute-start(bf16[64,1536]{1,0:T(8,128)(2,1)S(1)} %pad_maximum_fusion.7), channel_id=1, source_target_pairs={{0,2},{1,5},{2,0},{3,7},{4,6},{5,1},{6,4},{7,3},{8,10},{9,13},{10,... | collective-permute-start | bytes 589832 | tf_op jit(solution)/shard_map/ppermute | solution.py:484
  28.3 8.4 %collective-permute-start.1 = (bf16[64,1536]{1,0:T(8,128)(2,1)S(1)}, bf16[64,1536]{1,0:T(8,128)(2,1)S(1)}, u32[]{:S(2)}, u32[]{:S(2)}) collective-permute-start(bf16[64,1536]{1,0:T(8,128)(2,1)S(1)} %pad_maximum_fusion.6), channel_id=1, source_target_pairs={{0,2},{1,5},{2,0},{3,7},{4,6},{5,1},{6,4},{7,3},{8,10},{9,13},{10,... | collective-permute-start | bytes 589832 | tf_op jit(solution)/shard_map/ppermute | solution.py:484
  32.2 16.9 %collective-permute-start.5 = (bf16[128,1536]{1,0:T(8,128)(2,1)S(1)}, bf16[128,1536]{1,0:T(8,128)(2,1)S(1)}, u32[]{:S(2)}, u32[]{:S(2)}) collective-permute-start(bf16[128,1536]{1,0:T(8,128)(2,1)S(1)} %pad_maximum_fusion.4), channel_id=1, source_target_pairs={{0,8},{1,9},{2,10},{3,11},{4,12},{5,13},{6,14},{7,15},{8,0},{9,1},... | collective-permute-start | bytes 1179656 | tf_op jit(solution)/shard_map/ppermute | solution.py:484
  36.7 33.9 %collective-permute-start.2 = (bf16[128,1536]{1,0:T(8,128)(2,1)S(1)}, bf16[128,1536]{1,0:T(8,128)(2,1)S(1)}, u32[]{:S(2)}, u32[]{:S(2)}) collective-permute-start(bf16[128,1536]{1,0:T(8,128)(2,1)S(1)} %pad_maximum_fusion.3), channel_id=1, source_target_pairs={{0,8},{1,9},{2,10},{3,11},{4,12},{5,13},{6,14},{7,15},{8,0},{9,1},... | collective-permute-start | bytes 1179656 | tf_op jit(solution)/shard_map/ppermute | solution.py:484
  38.8 44.5 %collective-permute-start.8 = (bf16[128,1024]{1,0:T(8,128)(2,1)S(1)}, bf16[128,1024]{1,0:T(8,128)(2,1)S(1)}, u32[]{:S(2)}, u32[]{:S(2)}) collective-permute-start(bf16[128,1024]{1,0:T(8,128)(2,1)S(1)} %pad_maximum_fusion.5), channel_id=1, source_target_pairs={{0,8},{1,9},{2,10},{3,11},{4,12},{5,13},{6,14},{7,15},{8,0},{9,1},... | collective-permute-start | bytes 786440 | tf_op jit(solution)/shard_map/ppermute | solution.py:484
  49.1 49.4 %copy-start = (bf16[256,1536]{1,0:T(8,128)(2,1)}, bf16[256,1536]{1,0:T(8,128)(2,1)S(1)}, u32[]{:S(2)}) copy-start(bf16[256,1536]{1,0:T(8,128)(2,1)S(1)} %pad_maximum_fusion.1.refs_1_) | copy-start | bytes 2359300
  49.2 36.3 %collective-permute-start.10 = (bf16[256,1536]{1,0:T(8,128)(2,1)S(1)}, bf16[256,1536]{1,0:T(8,128)(2,1)S(1)}, u32[]{:S(2)}, u32[]{:S(2)}) collective-permute-start(bf16[256,1536]{1,0:T(8,128)(2,1)S(1)} %pad_maximum_fusion.1.refs_1_), channel_id=1, source_target_pairs={{0,4},{1,3},{2,6},{3,1},{4,0},{5,7},{6,2},{7,5},{8,12},{9,11},{10,... | collective-permute-start | bytes 2359304 | tf_op jit(solution)/shard_map/ppermute | solution.py:484
  70.7 27.9 %copy-start.1 = (bf16[256,1536]{1,0:T(8,128)(2,1)}, bf16[256,1536]{1,0:T(8,128)(2,1)S(1)}, u32[]{:S(2)}) copy-start(bf16[256,1536]{1,0:T(8,128)(2,1)S(1)} %pad_maximum_fusion.refs_0_) | copy-start | bytes 2359300
  70.7 15.1 %collective-permute-start.9 = (bf16[256,1536]{1,0:T(8,128)(2,1)S(1)}, bf16[256,1536]{1,0:T(8,128)(2,1)}, u32[]{:S(2)}, u32[]{:S(2)}) collective-permute-start(bf16[256,1536]{1,0:T(8,128)(2,1)S(1)} %pad_maximum_fusion.refs_0_), channel_id=1, source_target_pairs={{0,4},{1,3},{2,6},{3,1},{4,0},{5,7},{6,2},{7,5},{8,12},{9,11},{10,... | collective-permute-start | bytes 2359304 | tf_op jit(solution)/shard_map/ppermute | solution.py:484
  83.3 15.3 %copy-start.5 = (bf16[256,1024]{1,0:T(8,128)(2,1)}, bf16[256,1024]{1,0:T(8,128)(2,1)S(1)}, u32[]{:S(2)}) copy-start(bf16[256,1024]{1,0:T(8,128)(2,1)S(1)} %constant_dynamic-update-slice_fusion.refs_2_) | copy-start | bytes 1572868
  83.3 2.0 collective-permute-start.14
  83.4 12.9 %collective-permute-start.11 = (bf16[256,1024]{1,0:T(8,128)(2,1)S(1)}, bf16[256,1024]{1,0:T(8,128)(2,1)}, u32[]{:S(2)}, u32[]{:S(2)}) collective-permute-start(bf16[256,1024]{1,0:T(8,128)(2,1)S(1)} %constant_dynamic-update-slice_fusion.refs_2_), channel_id=1, source_target_pairs={{0,4},{1,3},{2,6},{3,1},{4,0},{5,7},{6,2},{7,5},{8,12},{9,11},{10,... | collective-permute-start | bytes 1572872 | tf_op jit(solution)/shard_map/ppermute | solution.py:484
  84.7 12.2 %collective-permute-start.13 = (bf16[256,1536]{1,0:T(8,128)(2,1)S(1)}, bf16[256,1536]{1,0:T(8,128)(2,1)}, u32[]{:S(2)}, u32[]{:S(2)}) collective-permute-start(bf16[256,1536]{1,0:T(8,128)(2,1)S(1)} %pad_maximum_fusion.1.refs_1_), channel_id=1, source_target_pairs={{0,1},{1,0},{2,3},{3,2},{4,5},{5,4},{6,7},{7,6},{8,9},{9,8},{10,11... | collective-permute-start | bytes 2359304 | tf_op jit(solution)/shard_map/ppermute | solution.py:484
  85.3 13.3 %copy-start.11 = (bf16[256,1024]{1,0:T(8,128)(2,1)}, bf16[256,1024]{1,0:T(8,128)(2,1)S(1)}, u32[]{:S(2)}) copy-start(bf16[256,1024]{1,0:T(8,128)(2,1)S(1)} %collective-permute-done.14.refs_8_) | copy-start | bytes 1572868
  85.3 11.7 %collective-permute-start.12 = (bf16[256,1536]{1,0:T(8,128)(2,1)S(1)}, bf16[256,1536]{1,0:T(8,128)(2,1)}, u32[]{:S(2)}, u32[]{:S(2)}) collective-permute-start(bf16[256,1536]{1,0:T(8,128)(2,1)S(1)} %pad_maximum_fusion.refs_0_), channel_id=1, source_target_pairs={{0,1},{1,0},{2,3},{3,2},{4,5},{5,4},{6,7},{7,6},{8,9},{9,8},{10,11... | collective-permute-start | bytes 2359304 | tf_op jit(solution)/shard_map/ppermute | solution.py:484
  85.4 13.1 %copy-start.10 = (bf16[256,1536]{1,0:T(8,128)(2,1)}, bf16[256,1536]{1,0:T(8,128)(2,1)S(1)}, u32[]{:S(2)}) copy-start(bf16[256,1536]{1,0:T(8,128)(2,1)S(1)} %collective-permute-done.10.refs_4_) | copy-start | bytes 2359300
  85.4 13.1 %collective-permute-start.16 = (bf16[256,1536]{1,0:T(8,128)(2,1)S(1)}, bf16[256,1536]{1,0:T(8,128)(2,1)}, u32[]{:S(2)}, u32[]{:S(2)}) collective-permute-start(bf16[256,1536]{1,0:T(8,128)(2,1)S(1)} %collective-permute-done.10.refs_4_), channel_id=1, source_target_pairs={{0,1},{1,0},{2,3},{3,2},{4,5},{5,4},{6,7},{7,6},{8,9},{9,8},{10,11... | collective-permute-start | bytes 2359304 | tf_op jit(solution)/shard_map/ppermute | solution.py:484
  85.8 12.7 %collective-permute-start.15 = (bf16[256,1536]{1,0:T(8,128)(2,1)}, bf16[256,1536]{1,0:T(8,128)(2,1)}, u32[]{:S(2)}, u32[]{:S(2)}) collective-permute-start(bf16[256,1536]{1,0:T(8,128)(2,1)} %collective-permute-done.9.refs_3_), channel_id=1, source_target_pairs={{0,1},{1,0},{2,3},{3,2},{4,5},{5,4},{6,7},{7,6},{8,9},{9,8},{10,11... | collective-permute-start | bytes 2359304 | tf_op jit(solution)/shard_map/ppermute | solution.py:484
  96.3 2.3 collective-permute-start.17
  212.1 30.3 %copy-start.9 = (f32[1,1024]{1,0:T(1,128)S(1)}, f32[1,1024]{1,0:T(1,128)}, u32[]{:S(2)}) copy-start(f32[1,1024]{1,0:T(1,128)} %get-tuple-element.56) | copy-start | bytes 12292
  212.1 30.3 %copy-start.4 = (f32[1,4096]{1,0:T(1,128)S(1)}, f32[1,4096]{1,0:T(1,128)}, u32[]{:S(2)}) copy-start(f32[1,4096]{1,0:T(1,128)} %get-tuple-element.57) | copy-start | bytes 49156
  212.1 30.3 %copy-start.8 = (f32[1,1024]{1,0:T(1,128)S(1)}, f32[1,1024]{1,0:T(1,128)}, u32[]{:S(2)}) copy-start(f32[1,1024]{1,0:T(1,128)} %get-tuple-element.58) | copy-start | bytes 12292
  212.1 30.3 %copy-start.7 = (f32[1,1024]{1,0:T(1,128)S(1)}, f32[1,1024]{1,0:T(1,128)}, u32[]{:S(2)}) copy-start(f32[1,1024]{1,0:T(1,128)} %get-tuple-element.59) | copy-start | bytes 12292
  212.1 30.3 %copy-start.6 = (f32[1,1024]{1,0:T(1,128)S(1)}, f32[1,1024]{1,0:T(1,128)}, u32[]{:S(2)}) copy-start(f32[1,1024]{1,0:T(1,128)} %get-tuple-element.60) | copy-start | bytes 12292
  242.4 1.3 collective-permute-start.18
  243.7 5.2 %collective-permute-start.19 = (f32[10240]{0:T(1024)S(1)}, f32[10240]{0:T(1024)S(1)}, u32[]{:S(2)}, u32[]{:S(2)}) collective-permute-start(f32[10240]{0:T(1024)S(1)} %add.15), channel_id=1, source_target_pairs={{0,2},{1,3},{2,0},{3,1},{4,6},{5,7},{6,4},{7,5},{8,10},{9,11},{10,... | collective-permute-start | bytes 122888 | tf_op jit(solution)/shard_map/ppermute | solution.py:484
  249.0 4.0 %collective-permute-start.20 = (f32[10240]{0:T(1024)S(1)}, f32[10240]{0:T(1024)S(1)}, u32[]{:S(2)}, u32[]{:S(2)}) collective-permute-start(f32[10240]{0:T(1024)S(1)} %add.16), channel_id=1, source_target_pairs={{0,4},{1,5},{2,6},{3,7},{4,0},{5,1},{6,2},{7,3},{8,12},{9,13},{10,... | collective-permute-start | bytes 122888 | tf_op jit(solution)/shard_map/ppermute | solution.py:484
  253.0 5.6 %collective-permute-start.21 = (f32[10240]{0:T(1024)S(1)}, f32[10240]{0:T(1024)S(1)}, u32[]{:S(2)}, u32[]{:S(2)}) collective-permute-start(f32[10240]{0:T(1024)S(1)} %add.17), channel_id=1, source_target_pairs={{0,8},{1,9},{2,10},{3,11},{4,12},{5,13},{6,14},{7,15},{8,0},{9,1},... | collective-permute-start | bytes 122888 | tf_op jit(solution)/shard_map/ppermute | solution.py:484
  258.6 14.8 %collective-permute-start.22 = (f32[10240]{0:T(1024)S(1)}, f32[10240]{0:T(1024)S(1)}, u32[]{:S(2)}, u32[]{:S(2)}) collective-permute-start(f32[10240]{0:T(1024)S(1)} %add.18), channel_id=1, source_target_pairs={{0,16},{1,17},{2,18},{3,19},{4,20},{5,21},{6,22},{7,23},{8,24},{9,... | collective-permute-start | bytes 122888 | tf_op jit(solution)/shard_map/ppermute | solution.py:484
Sparse Core Ops, SparseCore 0:
  10.9 132.4 all-gather.2

commit v2 on v1

--- a/solution.py
+++ b/solution.py
@@ -12,6 +12,7 @@
 BF = jnp.bfloat16
 F32 = jnp.float32
 VMEM_BYTES = 60 * 1024 * 1024
+FEED_BLOCK = 1024
 
 
 def dot(left, right):
@@ -195,23 +196,9 @@
 
 
 def gelu_and_slope(value):
-    density = jnp.exp(value * value * -0.5)
-    t = 1.0 / (1.0 + (0.3275911 * 0.5 ** 0.5) * jnp.abs(value))
-    poly = t * (0.254829592 + t * (-0.284496736 + t * (1.421413741 + t * (-1.453152027 + t * 1.061405429))))
-    tail = 0.5 * poly * density
-    share = jnp.where(value < 0.0, tail, 1.0 - tail)
-    return value * share, share + value * (density * 0.3989422804014327)
-
-
-def inner_kernel(xhat, gain, beta, wi, bi, active, slope, first):
-    @pl.when(pl.program_id(0) == 0)
-    def _():
-        first[...] = (xhat[...] * gain[...] + beta[...]).astype(BF)
-
-    value = dot(first[...], wi[...].reshape(first.shape[1], -1)) + bi[...]
-    act, slp = gelu_and_slope(value)
-    active[...] = act.astype(BF)
-    slope[...] = slp.astype(BF)
+    share = 0.5 + 0.5 * lax.erf(value * 0.5 ** 0.5)
+    density = jnp.exp2(value * (value * -0.7213475204444817)) * 0.3989422804014327
+    return value * share, share + value * density
 
 
 def inner_block(feed_w, block, turn):
@@ -224,26 +211,6 @@
     shards, tall, width = feed_w.shape
     tall = tall // 2
     return pl.BlockSpec((block // tall, tall, width), lambda j: (turn(j), 1, 0))
-
-
-def inner_forward(xhat, gain, beta, feed_w, inner_bias, block=512):
-    rows, width = xhat.shape
-    units = inner_bias.shape[1]
-    whole = lambda shp: pl.BlockSpec(shp, lambda j: (0,) * len(shp))
-    col = pl.BlockSpec((rows, block), lambda j: (0, j))
-    return pl.pallas_call(
-        inner_kernel,
-        grid=(units // block,),
-        in_specs=[
-            whole((rows, width)), whole((1, width)), whole((1, width)),
-            inner_block(feed_w, block, lambda j: j), pl.BlockSpec((1, block), lambda j: (0, j)),
-        ],
-        out_specs=[col, col],
-        out_shape=[jax.ShapeDtypeStruct((rows, units), BF)] * 2,
-        scratch_shapes=[pltpu.VMEM((rows, width), BF)],
-        compiler_params=pltpu.CompilerParams(vmem_limit_bytes=VMEM_BYTES),
-        name="inner_forward",
-    )(xhat, gain, beta, feed_w, inner_bias)
 
 
 def norm_gradient(grad, xhat, rstd, gain):
@@ -253,94 +220,144 @@
     return rstd * (scaled - mean - xhat * along)
 
 
+def fold(block):
+    return jnp.sum(block.reshape(block.shape[0] // 8, 8, block.shape[1]), axis=0)
+
+
 def feed_kernel(
-    shape, steps, short_lengths, long_lengths, xhat, rstd, short_ct, long_ct, active, slope, wd, wi, wo,
+    shape, steps, keep, xhat, rstd, short_ct, long_ct, wi, wd, wo, inner_bias,
     gain1, beta1, gain2, beta2, down_bias,
     short_out, long_out, grad_mixed, grad_first_sum, second_beta_sum, down_sum, inner_sum, first_beta_sum, output_sum,
-    total, grad_down,
+    total, low, value, slope, sums,
 ):
     step = pl.program_id(0)
     short_seqs, short_len, long_seqs, long_len = shape
     base = short_seqs * short_len
+    rows, width = xhat.shape
+    chunk = 128
+    wide = lambda ref: ref[...].reshape(width, -1)
+    tall = lambda ref: ref[...].reshape(-1, width)
+
+    def first_part():
+        value[lax.rem(step, 2)] = dot(low[...], wide(wi)) + inner_bias[...]
+
+    def second_part():
+        act, slp = gelu_and_slope(value[lax.rem(step + 1, 2)])
+        slope[step - 1] = slp.astype(BF)
+        total[...] += dot(act.astype(BF), tall(wd))
 
     @pl.when(step == 0)
     def _():
-        total[...] = xhat[...] * gain1[...] + beta1[...] + down_bias[...]
-
-    @pl.when(step < steps)
-    def _():
-        total[...] += dot(active[...], wd[...].reshape(-1, wd.shape[2]))
-
-    @pl.when(step == steps - 1)
-    def _():
-        keep = row_mask(short_lengths, long_lengths, shape)
-        second = total[...]
-        center = second - jnp.mean(second, axis=-1, keepdims=True)
-        spread = jnp.mean(center * center, axis=-1, keepdims=True)
-        rstd2 = lax.rsqrt(spread + 1e-06)
-        xhat2 = center * rstd2
-        output = ((xhat2 * gain2[...] + beta2[...]) * keep).astype(BF)
-        short_out[...] = output[:base]
-        long_out[...] = output[base:]
-        grad_out = jnp.concatenate([short_ct[...], long_ct[...]], axis=0).astype(F32) * keep
-        second_beta_sum[...] = jnp.sum(grad_out, axis=0, keepdims=True)
-        grad_second = norm_gradient(grad_out, xhat2, rstd2, gain2[...])
-        low = grad_second.astype(BF)
-        grad_down[...] = low
-        down_sum[...] = jnp.sum(low.astype(F32), axis=0, keepdims=True)
-        total[...] = grad_second
-
-    @pl.when(step >= steps)
-    def _():
-        grad_inner = (dot_t(grad_down[...], wd[...].reshape(-1, wd.shape[2])) * slope[...].astype(F32)).astype(BF)
+        def body(i, _):
+            here = pl.ds(pl.multiple_of(i * chunk, chunk), chunk)
+            first = xhat[here, :] * gain1[...] + beta1[...]
+            low[here, :] = first.astype(BF)
+            total[here, :] = first + down_bias[...]
+            return 0
+
+        lax.fori_loop(0, rows // chunk, body, 0)
+        first_part()
+
+    @pl.when((step > 0) & (step < steps))
+    def _():
+        first_part()
+        second_part()
+
+    @pl.when(step == steps)
+    def _():
+        second_part()
+        sums[...] = jnp.zeros_like(sums)
+
+        def rows_of(source, out, start):
+            def body(i, _):
+                there = pl.ds(pl.multiple_of(i * chunk, chunk), chunk)
+                here = pl.ds(pl.multiple_of(start + i * chunk, chunk), chunk)
+                second = total[here, :]
+                center = second - jnp.mean(second, axis=-1, keepdims=True)
+                spread = jnp.mean(center * center, axis=-1, keepdims=True)
+                rstd2 = lax.rsqrt(spread + 1e-06)
+                xhat2 = center * rstd2
+                usable = keep[here, :]
+                out[there, :] = ((xhat2 * gain2[...] + beta2[...]) * usable).astype(BF)
+                grad_out = source[there, :].astype(F32) * usable
+                grad_second = norm_gradient(grad_out, xhat2, rstd2, gain2[...])
+                rounded = grad_second.astype(BF)
+                low[here, :] = rounded
+                total[here, :] = grad_second
+                sums[0] += fold(grad_out)
+                sums[1] += fold(rounded.astype(F32))
+                return 0
+
+            lax.fori_loop(0, source.shape[0] // chunk, body, 0)
+
+        rows_of(short_ct, short_out, 0)
+        rows_of(long_ct, long_out, base)
+        second_beta_sum[...] = jnp.sum(sums[0], axis=0, keepdims=True)
+        down_sum[...] = jnp.sum(sums[1], axis=0, keepdims=True)
+
+    @pl.when(step > steps)
+    def _():
+        grad_inner = (dot_t(low[...], tall(wd)) * slope[2 * steps - step].astype(F32)).astype(BF)
         inner_sum[...] = jnp.sum(grad_inner.astype(F32), axis=0, keepdims=True)
-        total[...] += dot_t(grad_inner, wi[...].reshape(total.shape[1], -1))
-
-    @pl.when(step == 2 * steps - 1)
-    def _():
-        grad_first = total[...]
-        first_beta_sum[...] = jnp.sum(grad_first, axis=0, keepdims=True)
-        result = norm_gradient(grad_first, xhat[...], rstd[...], gain1[...])
-        grad_first_sum[...] = result
-        branch = result.astype(BF)
-        output_sum[...] = jnp.sum(branch.astype(F32), axis=0, keepdims=True)
-        grad_mixed[...] = dot_t(branch, wo[...]).astype(BF)
-
-
-def feed_back(shape, lengths, xhat, rstd, cts, active, slope, feed_w, output_w, vectors, block=512):
+        total[...] += dot_t(grad_inner, wide(wi))
+
+    @pl.when(step == 2 * steps)
+    def _():
+        sums[...] = jnp.zeros_like(sums)
+
+        def body(i, _):
+            here = pl.ds(pl.multiple_of(i * chunk, chunk), chunk)
+            grad_first = total[here, :]
+            result = norm_gradient(grad_first, xhat[here, :], rstd[here, :], gain1[...])
+            grad_first_sum[here, :] = result
+            branch = result.astype(BF)
+            low[here, :] = branch
+            sums[0] += fold(grad_first)
+            sums[1] += fold(branch.astype(F32))
+            return 0
+
+        lax.fori_loop(0, rows // chunk, body, 0)
+        first_beta_sum[...] = jnp.sum(sums[0], axis=0, keepdims=True)
+        output_sum[...] = jnp.sum(sums[1], axis=0, keepdims=True)
+        grad_mixed[...] = dot_t(low[...], wo[...]).astype(BF)
+
+
+def feed_forward_and_back(shape, keep, xhat, rstd, cts, feed_w, output_w, vectors, block=FEED_BLOCK):
     rows, width = xhat.shape
-    units = active.shape[1]
+    units = vectors["inner_bias"].shape[1]
     steps = units // block
     whole = lambda shp: pl.BlockSpec(shp, lambda j: (0,) * len(shp))
-    smem = pl.BlockSpec(memory_space=pltpu.SMEM)
     vec = whole((1, width))
-    late = lambda j: jnp.maximum(j - steps, 0)
+    back = lambda j: 2 * steps - j
+    inner_turn = lambda j: jnp.where(j <= steps, jnp.minimum(j, steps - 1), back(j))
+    down_turn = lambda j: jnp.where(j <= steps, jnp.maximum(j - 1, 0), back(j))
     vector_out = jax.ShapeDtypeStruct((1, width), F32)
     return pl.pallas_call(
         partial(feed_kernel, shape, steps),
-        grid=(2 * steps,),
+        grid=(2 * steps + 1,),
         in_specs=[
-            smem, smem, whole((rows, width)), whole((rows, 1)), whole(cts[0].shape), whole(cts[1].shape),
-            pl.BlockSpec((rows, block), lambda j: (0, jnp.minimum(j, steps - 1))),
-            pl.BlockSpec((rows, block), lambda j: (0, late(j))),
-            down_block(feed_w, block, lambda j: lax.rem(j, steps)),
-            inner_block(feed_w, block, late),
-            whole((width, width)), vec, vec, vec, vec, vec,
+            whole((rows, 1)), whole((rows, width)), whole((rows, 1)), whole(cts[0].shape), whole(cts[1].shape),
+            inner_block(feed_w, block, inner_turn), down_block(feed_w, block, down_turn), whole((width, width)),
+            pl.BlockSpec((1, block), lambda j: (0, jnp.minimum(j, steps - 1))), vec, vec, vec, vec, vec,
         ],
         out_specs=[
             whole(cts[0].shape), whole(cts[1].shape), whole((rows, width)), whole((rows, width)),
-            vec, vec, pl.BlockSpec((1, block), lambda j: (0, late(j))), vec, vec,
+            vec, vec, pl.BlockSpec((1, block), lambda j: (0, jnp.minimum(back(j), steps - 1))), vec, vec,
         ],
         out_shape=[
             jax.ShapeDtypeStruct(cts[0].shape, BF), jax.ShapeDtypeStruct(cts[1].shape, BF),
             jax.ShapeDtypeStruct((rows, width), BF), jax.ShapeDtypeStruct((rows, width), F32),
             vector_out, vector_out, jax.ShapeDtypeStruct((1, units), F32), vector_out, vector_out,
         ],
-        scratch_shapes=[pltpu.VMEM((rows, width), F32), pltpu.VMEM((rows, width), BF)],
+        scratch_shapes=[
+            pltpu.VMEM((rows, width), F32), pltpu.VMEM((rows, width), BF), pltpu.VMEM((2, rows, block), F32),
+            pltpu.VMEM((steps, rows, block), BF), pltpu.VMEM((2, 8, width), F32),
+        ],
         compiler_params=pltpu.CompilerParams(vmem_limit_bytes=VMEM_BYTES),
-        name="feed_back",
+        cost_estimate=pl.CostEstimate(flops=65 * 10**9, bytes_accessed=60 * 10**6, transcendentals=4 * 10**6),
+        name="feed_forward_and_back",
     )(
-        *lengths, xhat, rstd, *cts, active, slope, feed_w, feed_w, output_w,
+        keep, xhat, rstd, *cts, feed_w, feed_w, output_w, vectors["inner_bias"],
         vectors["first_gain"], vectors["first_beta"], vectors["second_gain"], vectors["second_beta"], vectors["down_bias"],
     )
 
@@ -458,10 +475,13 @@
     cts = (short_cotangent.reshape(-1, width), long_cotangent.reshape(-1, width))
     weights = gather_weights(packed_weight, output_weight, inner_weight, down_weight)
     q, k, v, short_p, long_p, mixed_t, xhat, rstd, packed_w, output_w = attention_forward(shape, lengths, xs, weights, vectors)
-    active, slope = inner_forward(xhat, vectors["first_gain"], vectors["first_beta"], weights["feed"], vectors["inner_bias"])
+    keep = jnp.concatenate([
+        (jnp.arange(item.shape[1])[None, :] < length[:, None]).reshape(-1, 1)
+        for item, length in ((short_input, short_lengths), (long_input, long_lengths))
+    ], axis=0).astype(F32)
     (
         short_out, long_out, gm, grad_first_sum, second_beta_sum, down_sum, inner_sum, first_beta_sum, output_sum,
-    ) = feed_back(shape, lengths, xhat, rstd, cts, active, slope, weights["feed"], output_w, vectors)
+    ) = feed_forward_and_back(shape, keep, xhat, rstd, cts, weights["feed"], output_w, vectors)
     short_grad, long_grad, query_sum, value_sum = attention_backward(
         shape, lengths, q, k, v, gm, short_p, long_p, mixed_t, packed_w, grad_first_sum
     )

time: 283 us -> 252 us (0.89)
  Pallas kernels: 142 us -> 125 us
  starting transfers between devices: 46 us -> 29.1 us
    ppermute x23, starting transfers between devices: 46 us -> 29 us  [exchange(): return lax.ppermute(block, 'dp', [(i, i ^ mask(i)) for i in range(count)])]
    pallas_call x2 -> x1, Pallas kernels: 68.7 us -> 51.9 us  [feed_forward_and_back(): pl.pallas_call(partial(feed_kernel, shape, steps), grid=(2 * steps + 1,),...]
    all_gather x1, waiting for transfers between devices: 0.32 us -> 5.91 us  [gather_weights(): feed = lax.all_gather(feed, 'dp', axis=0, tiled=False)]
    ppermute x23, waiting for transfers between devices: 72.3 us -> 69 us  [exchange(): return lax.ppermute(block, 'dp', [(i, i ^ mask(i)) for i in range(count)])]
  transfers between devices with their start and end apart: 24 -> 24, of which waited for: 15 -> 14; matrix products, arithmetic and copies ran while one was open for 0% -> 1% of each run, Pallas kernels for 16% -> 18%
where the time goes in v2:
time: 252 us
  Pallas kernels  125 us (50%)
  waiting for transfers between devices  74.9 us (30%)
  starting transfers between devices  29.1 us (12%)
  between operations  15 us (6%)
  local copies, waits for them, and re-layouts  5.63 us (2%)
    ppermute x23, waiting for transfers between devices, exchange(): return lax.ppermute(block, 'dp', [(i, i ^ mask(i)) for i in range(count)])  69 us
    pallas_call x1, Pallas kernels, feed_forward_and_back(): pl.pallas_call(partial(feed_kernel, shape, steps), grid=(2 * steps + 1,),...  51.9 us
    pallas_call x1, Pallas kernels, attention_forward(): pl.pallas_call(partial(attention_forward_kernel, shape, weights['slots'])...  44.5 us
    ppermute x23, starting transfers between devices, exchange(): return lax.ppermute(block, 'dp', [(i, i ^ mask(i)) for i in range(count)])  29 us
    pallas_call x1, Pallas kernels, attention_backward(): pl.pallas_call(partial(attention_backward_kernel, shape), grid=(steps,),...  28.6 us
    all_gather x1, waiting for transfers between devices, gather_weights(): feed = lax.all_gather(feed, 'dp', axis=0, tiled=False)  5.91 us
  transfers between devices with their start and end apart: 24, of which 14 were waited for; matrix products, arithmetic and copies ran while one was open for 1% of the time, Pallas kernels for 18%

profile of v2, /device:TPU:0, one launch (start us, length us, event | category | flops | bytes accessed | tf_op | source)
XLA Modules:
  0.0 251.7 jit_solution(13803566042193480030)
XLA Ops:
  7.2 1.0 copy.42
  8.3 1.8 pad_maximum_fusion.2
  10.1 4.1 %collective-permute-start.3 = (bf16[32,1536]{1,0:T(8,128)(2,1)S(1)}, bf16[32,1536]{1,0:T(8,128)(2,1)S(1)}, u32[]{:S(2)}, u32[]{:S(2)}) collective-permute-start(bf16[32,1536]{1,0:T(8,128)(2,1)S(1)} %pad_maximum_fusion.10), channel_id=1, source_target_pairs={{0,16},{1,17},{2,18},{3,19},{4,20},{5,21},{6,22},{7,23},{8,24},{9,... | collective-permute-start | bytes 294920 | tf_op jit(solution)/shard_map/ppermute | solution.py:504
  14.2 0.1 collective-permute-start.6
  14.3 2.9 %collective-permute-start = (bf16[32,1536]{1,0:T(8,128)(2,1)S(1)}, bf16[32,1536]{1,0:T(8,128)(2,1)S(1)}, u32[]{:S(2)}, u32[]{:S(2)}) collective-permute-start(bf16[32,1536]{1,0:T(8,128)(2,1)S(1)} %pad_maximum_fusion.9), channel_id=1, source_target_pairs={{0,16},{1,17},{2,18},{3,19},{4,20},{5,21},{6,22},{7,23},{8,24},{9,... | collective-permute-start | bytes 294920 | tf_op jit(solution)/shard_map/ppermute | solution.py:504
  17.2 7.6 %collective-permute-done.6 = bf16[32,1024]{1,0:T(8,128)(2,1)S(1)} collective-permute-done((bf16[32,1024]{1,0:T(8,128)(2,1)S(1)}, bf16[32,1024]{1,0:T(8,128)(2,1)S(1)}, u32[]{:S(2)}, u32[]{:S(2)}) %collective-permute-start.6) | collective-permute-done | bytes 65568 | tf_op jit(solution)/shard_map/ppermute | solution.py:504
  24.9 1.8 collective-permute-start.7
  26.7 0.4 collective-permute-start.4
  27.1 1.8 collective-permute-start.1
  28.9 3.6 %collective-permute-done.4 = bf16[64,1536]{1,0:T(8,128)(2,1)S(1)} collective-permute-done((bf16[64,1536]{1,0:T(8,128)(2,1)S(1)}, bf16[64,1536]{1,0:T(8,128)(2,1)S(1)}, u32[]{:S(2)}, u32[]{:S(2)}) %collective-permute-start.4) | collective-permute-done | bytes 196640 | tf_op jit(solution)/shard_map/ppermute | solution.py:504
  32.5 1.3 collective-permute-start.5
  33.8 0.8 collective-permute-done.1
  34.6 2.7 %collective-permute-start.2 = (bf16[128,1536]{1,0:T(8,128)(2,1)S(1)}, bf16[128,1536]{1,0:T(8,128)(2,1)S(1)}, u32[]{:S(2)}, u32[]{:S(2)}) collective-permute-start(bf16[128,1536]{1,0:T(8,128)(2,1)S(1)} %pad_maximum_fusion.3), channel_id=1, source_target_pairs={{0,8},{1,9},{2,10},{3,11},{4,12},{5,13},{6,14},{7,15},{8,0},{9,1},... | collective-permute-start | bytes 1179656 | tf_op jit(solution)/shard_map/ppermute | solution.py:504
  37.3 0.1 collective-permute-start.8
  37.4 9.3 %collective-permute-done.5 = bf16[128,1536]{1,0:T(8,128)(2,1)S(1)} collective-permute-done((bf16[128,1536]{1,0:T(8,128)(2,1)S(1)}, bf16[128,1536]{1,0:T(8,128)(2,1)S(1)}, u32[]{:S(2)}, u32[]{:S(2)}) %collective-permute-start.5) | collective-permute-done | bytes 393248 | tf_op jit(solution)/shard_map/ppermute | solution.py:504
  46.7 1.4 collective-permute-start.10
  48.1 18.5 %collective-permute-done.2 = bf16[128,1536]{1,0:T(8,128)(2,1)S(1)} collective-permute-done((bf16[128,1536]{1,0:T(8,128)(2,1)S(1)}, bf16[128,1536]{1,0:T(8,128)(2,1)S(1)}, u32[]{:S(2)}, u32[]{:S(2)}) %collective-permute-start.2) | collective-permute-done | bytes 393248 | tf_op jit(solution)/shard_map/ppermute | solution.py:504
  66.7 1.3 collective-permute-start.9
  68.0 7.8 %collective-permute-done.8 = bf16[128,1024]{1,0:T(8,128)(2,1)S(1)} collective-permute-done((bf16[128,1024]{1,0:T(8,128)(2,1)S(1)}, bf16[128,1024]{1,0:T(8,128)(2,1)S(1)}, u32[]{:S(2)}, u32[]{:S(2)}) %collective-permute-start.8) | collective-permute-done | bytes 262176 | tf_op jit(solution)/shard_map/ppermute | solution.py:504
  75.8 0.9 collective-permute-start.11
  76.8 2.9 %collective-permute-start.14 = (bf16[256,1024]{1,0:T(8,128)(2,1)S(1)}, bf16[256,1024]{1,0:T(8,128)(2,1)S(1)}, u32[]{:S(2)}, u32[]{:S(2)}) collective-permute-start(bf16[256,1024]{1,0:T(8,128)(2,1)S(1)} %constant_dynamic-update-slice_fusion.refs_2_), channel_id=1, source_target_pairs={{0,1},{1,0},{2,3},{3,2},{4,5},{5,4},{6,7},{7,6},{8,9},{9,8},{10,11... | collective-permute-start | bytes 1572872 | tf_op jit(solution)/shard_map/ppermute | solution.py:504
  79.7 5.4 %collective-permute-done.11.refs_5_ = bf16[256,1024]{1,0:T(8,128)(2,1)S(1)} collective-permute-done((bf16[256,1024]{1,0:T(8,128)(2,1)S(1)}, bf16[256,1024]{1,0:T(8,128)(2,1)S(1)}, u32[]{:S(2)}, u32[]{:S(2)}) %collective-permute-start.11) | collective-permute-done | bytes 524320 | tf_op jit(solution)/shard_map/ppermute | solution.py:504
  85.1 1.6 collective-permute-start.12
  86.7 0.1 collective-permute-start.16
  86.7 0.4 collective-permute-start.15
  87.2 0.8 copy-done.13
  88.0 0.1 collective-permute-start.17
  88.8 0.1 fusion
  88.9 1.0 copy.37.keep
  89.9 2.6 %collective-permute-done.17.refs_11_ = bf16[256,1024]{1,0:T(8,128)(2,1)} collective-permute-done((bf16[256,1024]{1,0:T(8,128)(2,1)S(1)}, bf16[256,1024]{1,0:T(8,128)(2,1)}, u32[]{:S(2)}, u32[]{:S(2)}) %collective-permute-start.17) | collective-permute-done | bytes 524320 | tf_op jit(solution)/shard_map/ppermute | solution.py:504
  92.5 44.5 %attention_forward.1 = (bf16[896,1024]{1,0:T(8,128)(2,1)}, bf16[896,1024]{1,0:T(8,128)(2,1)}, bf16[896,1024]{1,0:T(8,128)(2,1)}, bf16[3,16,128,128]{3,2,1,0:T(8,...) custom-call(s32[1]{0:T(128)} %bitcast.1.me, ...), custom_call_target="tpu_custom_call" | custom-call | flops 35999997952 | bytes 40000000 | tf_op jit(solution)/shard_map/attention_forward/pallas_call | solution.py:158
  137.0 5.9 %all-gather.3.cloned.1.call-done = bf16[8192,1024]{1,0:T(8,128)(2,1)} async-done(((bf16[256,1024]{1,0:T(8,128)(2,1)}), bf16[8192,1024]{1,0:T(8,128)(2,1)}) %all-gather.3.cloned.1.call-update) | async-done | bytes 16777232 | tf_op jit(solution)/shard_map/all_gather | solution.py:554
  142.9 51.9 %feed_forward_and_back.1 = (bf16[384,1024]{1,0:T(8,128)(2,1)}, bf16[512,1024]{1,0:T(8,128)(2,1)}, bf16[896,1024]{1,0:T(8,128)(2,1)}, f32[896,1024]{1,0:T(8,128)}...) custom-call(f32[896,1]{1,0:T(8,128)} %copy.37.keep, ...), custom_call_target="tpu_custom_call" | custom-call | flops 65000001536 | bytes 60000000 | tf_op jit(solution)/shard_map/feed_forward_and_back/pallas_call | solution.py:335
  194.9 28.6 %attention_backward.1 = (bf16[384,1024]{1,0:T(8,128)(2,1)}, bf16[512,1024]{1,0:T(8,128)(2,1)}, f32[1,1024]{1,0:T(1,128)}, f32[1,1024]{1,0:T(1,128)}) custom-call(s32[3]{0:T(128)} %short_lengths.3, s32[1]{0:T(128)} %copy.53.long_lengths, bf16[896,1024]{1,0:T(8,128)(2,1)} %get-tuple-element.38.q, bf16[896,1024]{1,0:T(8,128)(2,1)} %get-tuple-element.39.k, ...), custom_call_target="tpu_custom_call" | custom-call | tf_op jit(solution)/shard_map/attention_backward/pallas_call | solution.py:439
  223.5 0.7 constant_dynamic-update-slice_fusion.10
  224.2 0.7 constant_dynamic-update-slice_fusion.9
  225.0 0.3 collective-permute-start.18
  225.3 1.0 collective-permute-done.18
  226.2 1.3 collective-permute-start.19
  227.5 2.7 %collective-permute-done.19 = f32[10240]{0:T(1024)S(1)} collective-permute-done((f32[10240]{0:T(1024)S(1)}, f32[10240]{0:T(1024)S(1)}, u32[]{:S(2)}, u32[]{:S(2)}) %collective-permute-start.19) | collective-permute-done | bytes 40992 | tf_op jit(solution)/shard_map/ppermute | solution.py:504
  230.3 1.5 collective-permute-start.20
  231.7 2.5 %collective-permute-done.20 = f32[10240]{0:T(1024)S(1)} collective-permute-done((f32[10240]{0:T(1024)S(1)}, f32[10240]{0:T(1024)S(1)}, u32[]{:S(2)}, u32[]{:S(2)}) %collective-permute-start.20) | collective-permute-done | bytes 40992 | tf_op jit(solution)/shard_map/ppermute | solution.py:504
  234.3 0.4 collective-permute-start.21
  234.7 3.6 %collective-permute-done.21 = f32[10240]{0:T(1024)S(1)} collective-permute-done((f32[10240]{0:T(1024)S(1)}, f32[10240]{0:T(1024)S(1)}, u32[]{:S(2)}, u32[]{:S(2)}) %collective-permute-start.21) | collective-permute-done | bytes 40992 | tf_op jit(solution)/shard_map/ppermute | solution.py:504
  238.3 1.7 collective-permute-start.22
  240.0 3.6 %collective-permute-done.22 = f32[10240]{0:T(1024)S(1)} collective-permute-done((f32[10240]{0:T(1024)S(1)}, f32[10240]{0:T(1024)S(1)}, u32[]{:S(2)}, u32[]{:S(2)}) %collective-permute-start.22) | collective-permute-done | bytes 40992 | tf_op jit(solution)/shard_map/ppermute | solution.py:504
  243.6 0.6 fusion.2
  244.2 0.6 slice.55
  (69 shorter events, 0.5 us)
Async XLA Ops:
  7.2 2.9 %copy-start.3 = (bf16[32,3072]{1,0:T(8,128)(2,1)S(1)}, bf16[32,3072]{1,0:T(8,128)(2,1)}, u32[]{:S(2)}) copy-start(bf16[32,3072]{1,0:T(8,128)(2,1)} %param.25) | copy-start | bytes 589828
  7.2 7.0 %copy-start.2 = (bf16[32,1024]{1,0:T(8,128)(2,1)S(1)}, bf16[32,1024]{1,0:T(8,128)(2,1)}, u32[]{:S(2)}) copy-start(bf16[32,1024]{1,0:T(8,128)(2,1)} %param.26) | copy-start | bytes 196612
  7.2 135.7 %all-gather.3.cloned.1.call-start = ((), (), s32[]{:S(2)}) async-start(), calls=%async_computation | async-start | bytes 17301504 | tf_op jit(solution)/shard_map/all_gather | solution.py:554
  10.1 16.5 %collective-permute-start.3 = (bf16[32,1536]{1,0:T(8,128)(2,1)S(1)}, bf16[32,1536]{1,0:T(8,128)(2,1)S(1)}, u32[]{:S(2)}, u32[]{:S(2)}) collective-permute-start(bf16[32,1536]{1,0:T(8,128)(2,1)S(1)} %pad_maximum_fusion.10), channel_id=1, source_target_pairs={{0,16},{1,17},{2,18},{3,19},{4,20},{5,21},{6,22},{7,23},{8,24},{9,... | collective-permute-start | bytes 294920 | tf_op jit(solution)/shard_map/ppermute | solution.py:504
  14.2 10.6 %collective-permute-start.6 = (bf16[32,1024]{1,0:T(8,128)(2,1)S(1)}, bf16[32,1024]{1,0:T(8,128)(2,1)S(1)}, u32[]{:S(2)}, u32[]{:S(2)}) collective-permute-start(bf16[32,1024]{1,0:T(8,128)(2,1)S(1)} %copy-done.2), channel_id=1, source_target_pairs={{0,16},{1,17},{2,18},{3,19},{4,20},{5,21},{6,22},{7,23},{8,24},{9,... | collective-permute-start | bytes 196616 | tf_op jit(solution)/shard_map/ppermute | solution.py:504
  14.3 12.7 %collective-permute-start = (bf16[32,1536]{1,0:T(8,128)(2,1)S(1)}, bf16[32,1536]{1,0:T(8,128)(2,1)S(1)}, u32[]{:S(2)}, u32[]{:S(2)}) collective-permute-start(bf16[32,1536]{1,0:T(8,128)(2,1)S(1)} %pad_maximum_fusion.9), channel_id=1, source_target_pairs={{0,16},{1,17},{2,18},{3,19},{4,20},{5,21},{6,22},{7,23},{8,24},{9,... | collective-permute-start | bytes 294920 | tf_op jit(solution)/shard_map/ppermute | solution.py:504
  24.9 12.3 %collective-permute-start.7 = (bf16[64,1024]{1,0:T(8,128)(2,1)S(1)}, bf16[64,1024]{1,0:T(8,128)(2,1)S(1)}, u32[]{:S(2)}, u32[]{:S(2)}) collective-permute-start(bf16[64,1024]{1,0:T(8,128)(2,1)S(1)} %pad_maximum_fusion.8), channel_id=1, source_target_pairs={{0,2},{1,5},{2,0},{3,7},{4,6},{5,1},{6,4},{7,3},{8,10},{9,13},{10,... | collective-permute-start | bytes 393224 | tf_op jit(solution)/shard_map/ppermute | solution.py:504
  26.7 5.7 %collective-permute-start.4 = (bf16[64,1536]{1,0:T(8,128)(2,1)S(1)}, bf16[64,1536]{1,0:T(8,128)(2,1)S(1)}, u32[]{:S(2)}, u32[]{:S(2)}) collective-permute-start(bf16[64,1536]{1,0:T(8,128)(2,1)S(1)} %pad_maximum_fusion.7), channel_id=1, source_target_pairs={{0,2},{1,5},{2,0},{3,7},{4,6},{5,1},{6,4},{7,3},{8,10},{9,13},{10,... | collective-permute-start | bytes 589832 | tf_op jit(solution)/shard_map/ppermute | solution.py:504
  27.1 7.4 %collective-permute-start.1 = (bf16[64,1536]{1,0:T(8,128)(2,1)S(1)}, bf16[64,1536]{1,0:T(8,128)(2,1)S(1)}, u32[]{:S(2)}, u32[]{:S(2)}) collective-permute-start(bf16[64,1536]{1,0:T(8,128)(2,1)S(1)} %pad_maximum_fusion.6), channel_id=1, source_target_pairs={{0,2},{1,5},{2,0},{3,7},{4,6},{5,1},{6,4},{7,3},{8,10},{9,13},{10,... | collective-permute-start | bytes 589832 | tf_op jit(solution)/shard_map/ppermute | solution.py:504
  32.5 14.2 %collective-permute-start.5 = (bf16[128,1536]{1,0:T(8,128)(2,1)S(1)}, bf16[128,1536]{1,0:T(8,128)(2,1)S(1)}, u32[]{:S(2)}, u32[]{:S(2)}) collective-permute-start(bf16[128,1536]{1,0:T(8,128)(2,1)S(1)} %pad_maximum_fusion.4), channel_id=1, source_target_pairs={{0,8},{1,9},{2,10},{3,11},{4,12},{5,13},{6,14},{7,15},{8,0},{9,1},... | collective-permute-start | bytes 1179656 | tf_op jit(solution)/shard_map/ppermute | solution.py:504
  34.6 32.0 %collective-permute-start.2 = (bf16[128,1536]{1,0:T(8,128)(2,1)S(1)}, bf16[128,1536]{1,0:T(8,128)(2,1)S(1)}, u32[]{:S(2)}, u32[]{:S(2)}) collective-permute-start(bf16[128,1536]{1,0:T(8,128)(2,1)S(1)} %pad_maximum_fusion.3), channel_id=1, source_target_pairs={{0,8},{1,9},{2,10},{3,11},{4,12},{5,13},{6,14},{7,15},{8,0},{9,1},... | collective-permute-start | bytes 1179656 | tf_op jit(solution)/shard_map/ppermute | solution.py:504
  37.3 38.5 %collective-permute-start.8 = (bf16[128,1024]{1,0:T(8,128)(2,1)S(1)}, bf16[128,1024]{1,0:T(8,128)(2,1)S(1)}, u32[]{:S(2)}, u32[]{:S(2)}) collective-permute-start(bf16[128,1024]{1,0:T(8,128)(2,1)S(1)} %pad_maximum_fusion.5), channel_id=1, source_target_pairs={{0,8},{1,9},{2,10},{3,11},{4,12},{5,13},{6,14},{7,15},{8,0},{9,1},... | collective-permute-start | bytes 786440 | tf_op jit(solution)/shard_map/ppermute | solution.py:504
  46.7 45.8 %copy-start = (bf16[256,1536]{1,0:T(8,128)(2,1)}, bf16[256,1536]{1,0:T(8,128)(2,1)S(1)}, u32[]{:S(2)}) copy-start(bf16[256,1536]{1,0:T(8,128)(2,1)S(1)} %pad_maximum_fusion.1.refs_1_) | copy-start | bytes 2359300
  46.7 42.1 %copy-start.10 = (s32[3]{0:T(128)S(1)}, s32[3]{0:T(128)}, u32[]{:S(2)}) copy-start(s32[3]{0:T(128)} %short_lengths.3) | copy-start | bytes 40
  46.7 40.0 %collective-permute-start.10 = (bf16[256,1536]{1,0:T(8,128)(2,1)S(1)}, bf16[256,1536]{1,0:T(8,128)(2,1)S(1)}, u32[]{:S(2)}, u32[]{:S(2)}) collective-permute-start(bf16[256,1536]{1,0:T(8,128)(2,1)S(1)} %pad_maximum_fusion.1.refs_1_), channel_id=1, source_target_pairs={{0,4},{1,3},{2,6},{3,1},{4,0},{5,7},{6,2},{7,5},{8,12},{9,11},{10,... | collective-permute-start | bytes 2359304 | tf_op jit(solution)/shard_map/ppermute | solution.py:504
  66.7 25.8 %copy-start.1 = (bf16[256,1536]{1,0:T(8,128)(2,1)}, bf16[256,1536]{1,0:T(8,128)(2,1)S(1)}, u32[]{:S(2)}) copy-start(bf16[256,1536]{1,0:T(8,128)(2,1)S(1)} %pad_maximum_fusion.refs_0_) | copy-start | bytes 2359300
  66.7 20.1 %collective-permute-start.9 = (bf16[256,1536]{1,0:T(8,128)(2,1)S(1)}, bf16[256,1536]{1,0:T(8,128)(2,1)}, u32[]{:S(2)}, u32[]{:S(2)}) collective-permute-start(bf16[256,1536]{1,0:T(8,128)(2,1)S(1)} %pad_maximum_fusion.refs_0_), channel_id=1, source_target_pairs={{0,4},{1,3},{2,6},{3,1},{4,0},{5,7},{6,2},{7,5},{8,12},{9,11},{10,... | collective-permute-start | bytes 2359304 | tf_op jit(solution)/shard_map/ppermute | solution.py:504
  75.8 16.7 %copy-start.5 = (bf16[256,1024]{1,0:T(8,128)(2,1)}, bf16[256,1024]{1,0:T(8,128)(2,1)S(1)}, u32[]{:S(2)}) copy-start(bf16[256,1024]{1,0:T(8,128)(2,1)S(1)} %constant_dynamic-update-slice_fusion.refs_2_) | copy-start | bytes 1572868
  75.8 9.2 %collective-permute-start.11 = (bf16[256,1024]{1,0:T(8,128)(2,1)S(1)}, bf16[256,1024]{1,0:T(8,128)(2,1)S(1)}, u32[]{:S(2)}, u32[]{:S(2)}) collective-permute-start(bf16[256,1024]{1,0:T(8,128)(2,1)S(1)} %constant_dynamic-update-slice_fusion.refs_2_), channel_id=1, source_target_pairs={{0,4},{1,3},{2,6},{3,1},{4,0},{5,7},{6,2},{7,5},{8,12},{9,11},{10,... | collective-permute-start | bytes 1572872 | tf_op jit(solution)/shard_map/ppermute | solution.py:504
  76.8 10.4 %collective-permute-start.14 = (bf16[256,1024]{1,0:T(8,128)(2,1)S(1)}, bf16[256,1024]{1,0:T(8,128)(2,1)S(1)}, u32[]{:S(2)}, u32[]{:S(2)}) collective-permute-start(bf16[256,1024]{1,0:T(8,128)(2,1)S(1)} %constant_dynamic-update-slice_fusion.refs_2_), channel_id=1, source_target_pairs={{0,1},{1,0},{2,3},{3,2},{4,5},{5,4},{6,7},{7,6},{8,9},{9,8},{10,11... | collective-permute-start | bytes 1572872 | tf_op jit(solution)/shard_map/ppermute | solution.py:504
  79.7 10.2 %collective-permute-start.13 = (bf16[256,1536]{1,0:T(8,128)(2,1)S(1)}, bf16[256,1536]{1,0:T(8,128)(2,1)}, u32[]{:S(2)}, u32[]{:S(2)}) collective-permute-start(bf16[256,1536]{1,0:T(8,128)(2,1)S(1)} %pad_maximum_fusion.1.refs_1_), channel_id=1, source_target_pairs={{0,1},{1,0},{2,3},{3,2},{4,5},{5,4},{6,7},{7,6},{8,9},{9,8},{10,11... | collective-permute-start | bytes 2359304 | tf_op jit(solution)/shard_map/ppermute | solution.py:504
  85.1 7.4 %copy-start.12 = (bf16[256,1024]{1,0:T(8,128)(2,1)}, bf16[256,1024]{1,0:T(8,128)(2,1)S(1)}, u32[]{:S(2)}) copy-start(bf16[256,1024]{1,0:T(8,128)(2,1)S(1)} %collective-permute-done.11.refs_5_) | copy-start | bytes 1572868
  85.1 4.8 %collective-permute-start.12 = (bf16[256,1536]{1,0:T(8,128)(2,1)S(1)}, bf16[256,1536]{1,0:T(8,128)(2,1)}, u32[]{:S(2)}, u32[]{:S(2)}) collective-permute-start(bf16[256,1536]{1,0:T(8,128)(2,1)S(1)} %pad_maximum_fusion.refs_0_), channel_id=1, source_target_pairs={{0,1},{1,0},{2,3},{3,2},{4,5},{5,4},{6,7},{7,6},{8,9},{9,8},{10,11... | collective-permute-start | bytes 2359304 | tf_op jit(solution)/shard_map/ppermute | solution.py:504
  86.7 5.8 %copy-start.11 = (bf16[256,1536]{1,0:T(8,128)(2,1)}, bf16[256,1536]{1,0:T(8,128)(2,1)S(1)}, u32[]{:S(2)}) copy-start(bf16[256,1536]{1,0:T(8,128)(2,1)S(1)} %collective-permute-done.10.refs_4_) | copy-start | bytes 2359300
  86.7 5.8 %collective-permute-start.16 = (bf16[256,1536]{1,0:T(8,128)(2,1)S(1)}, bf16[256,1536]{1,0:T(8,128)(2,1)}, u32[]{:S(2)}, u32[]{:S(2)}) collective-permute-start(bf16[256,1536]{1,0:T(8,128)(2,1)S(1)} %collective-permute-done.10.refs_4_), channel_id=1, source_target_pairs={{0,1},{1,0},{2,3},{3,2},{4,5},{5,4},{6,7},{7,6},{8,9},{9,8},{10,11... | collective-permute-start | bytes 2359304 | tf_op jit(solution)/shard_map/ppermute | solution.py:504
  86.7 5.7 %collective-permute-start.15 = (bf16[256,1536]{1,0:T(8,128)(2,1)}, bf16[256,1536]{1,0:T(8,128)(2,1)}, u32[]{:S(2)}, u32[]{:S(2)}) collective-permute-start(bf16[256,1536]{1,0:T(8,128)(2,1)} %collective-permute-done.9.refs_3_), channel_id=1, source_target_pairs={{0,1},{1,0},{2,3},{3,2},{4,5},{5,4},{6,7},{7,6},{8,9},{9,8},{10,11... | collective-permute-start | bytes 2359304 | tf_op jit(solution)/shard_map/ppermute | solution.py:504
  87.2 0.8 copy-start.13
  88.0 4.5 %collective-permute-start.17 = (bf16[256,1024]{1,0:T(8,128)(2,1)S(1)}, bf16[256,1024]{1,0:T(8,128)(2,1)}, u32[]{:S(2)}, u32[]{:S(2)}) collective-permute-start(bf16[256,1024]{1,0:T(8,128)(2,1)S(1)} %collective-permute-done.11.refs_5_), channel_id=1, source_target_pairs={{0,1},{1,0},{2,3},{3,2},{4,5},{5,4},{6,7},{7,6},{8,9},{9,8},{10,11... | collective-permute-start | bytes 1572872 | tf_op jit(solution)/shard_map/ppermute | solution.py:504
  194.8 30.1 %copy-start.9 = (f32[1,1024]{1,0:T(1,128)S(1)}, f32[1,1024]{1,0:T(1,128)}, u32[]{:S(2)}) copy-start(f32[1,1024]{1,0:T(1,128)} %get-tuple-element.52) | copy-start | bytes 12292
  194.8 30.1 %copy-start.4 = (f32[1,4096]{1,0:T(1,128)S(1)}, f32[1,4096]{1,0:T(1,128)}, u32[]{:S(2)}) copy-start(f32[1,4096]{1,0:T(1,128)} %get-tuple-element.53) | copy-start | bytes 49156
  194.8 30.1 %copy-start.8 = (f32[1,1024]{1,0:T(1,128)S(1)}, f32[1,1024]{1,0:T(1,128)}, u32[]{:S(2)}) copy-start(f32[1,1024]{1,0:T(1,128)} %get-tuple-element.54) | copy-start | bytes 12292
  194.8 30.1 %copy-start.7 = (f32[1,1024]{1,0:T(1,128)S(1)}, f32[1,1024]{1,0:T(1,128)}, u32[]{:S(2)}) copy-start(f32[1,1024]{1,0:T(1,128)} %get-tuple-element.55) | copy-start | bytes 12292
  194.9 30.1 %copy-start.6 = (f32[1,1024]{1,0:T(1,128)S(1)}, f32[1,1024]{1,0:T(1,128)}, u32[]{:S(2)}) copy-start(f32[1,1024]{1,0:T(1,128)} %get-tuple-element.56) | copy-start | bytes 12292
  225.0 1.3 collective-permute-start.18
  226.2 4.0 %collective-permute-start.19 = (f32[10240]{0:T(1024)S(1)}, f32[10240]{0:T(1024)S(1)}, u32[]{:S(2)}, u32[]{:S(2)}) collective-permute-start(f32[10240]{0:T(1024)S(1)} %add.15), channel_id=1, source_target_pairs={{0,2},{1,3},{2,0},{3,1},{4,6},{5,7},{6,4},{7,5},{8,10},{9,11},{10,... | collective-permute-start | bytes 122888 | tf_op jit(solution)/shard_map/ppermute | solution.py:504
  230.3 4.0 %collective-permute-start.20 = (f32[10240]{0:T(1024)S(1)}, f32[10240]{0:T(1024)S(1)}, u32[]{:S(2)}, u32[]{:S(2)}) collective-permute-start(f32[10240]{0:T(1024)S(1)} %add.16), channel_id=1, source_target_pairs={{0,4},{1,5},{2,6},{3,7},{4,0},{5,1},{6,2},{7,3},{8,12},{9,13},{10,... | collective-permute-start | bytes 122888 | tf_op jit(solution)/shard_map/ppermute | solution.py:504
  234.3 4.0 %collective-permute-start.21 = (f32[10240]{0:T(1024)S(1)}, f32[10240]{0:T(1024)S(1)}, u32[]{:S(2)}, u32[]{:S(2)}) collective-permute-start(f32[10240]{0:T(1024)S(1)} %add.17), channel_id=1, source_target_pairs={{0,8},{1,9},{2,10},{3,11},{4,12},{5,13},{6,14},{7,15},{8,0},{9,1},... | collective-permute-start | bytes 122888 | tf_op jit(solution)/shard_map/ppermute | solution.py:504
  238.3 5.3 %collective-permute-start.22 = (f32[10240]{0:T(1024)S(1)}, f32[10240]{0:T(1024)S(1)}, u32[]{:S(2)}, u32[]{:S(2)}) collective-permute-start(f32[10240]{0:T(1024)S(1)} %add.18), channel_id=1, source_target_pairs={{0,16},{1,17},{2,18},{3,19},{4,20},{5,21},{6,22},{7,23},{8,24},{9,... | collective-permute-start | bytes 122888 | tf_op jit(solution)/shard_map/ppermute | solution.py:504
Sparse Core Ops, SparseCore 0:
  10.9 131.9 all-gather.2

commit v3 on v2

--- a/solution.py
+++ b/solution.py
@@ -102,33 +102,36 @@
     q_out[...] = ((dot(x, weight(0)) + qb[...]).astype(BF).astype(F32) * HEAD_DIM ** (-0.5)).astype(BF)
     k_out[...] = dot(x, weight(1)).astype(BF)
     v_out[...] = (dot(x, weight(2)) + vb[...]).astype(BF)
-    for pair in range(width // 128):
+    groups = ((short_spans, short_lengths, short_p), (long_spans, long_lengths, long_p))
+    pairs = range(width // 128)
+    jobs = []
+    for pair in pairs:
         lanes = slice(128 * pair, 128 * pair + 128)
-        v_t = flip(v_out[:, lanes])
-        for which, spans, refs, probs in (
-            (0, short_spans, short_lengths, short_p),
-            (1, long_spans, long_lengths, long_p),
-        ):
+        for spans, refs, probs in groups:
             for seq, (start, length) in enumerate(spans):
                 k2 = k_out[start : start + length, lanes]
-                rows = lax.broadcasted_iota(jnp.int32, (length, 1), 0)
-                usable = rows < refs[seq]
-                block = min(length, 256)
+                usable = lax.broadcasted_iota(jnp.int32, (length, 1), 0) < refs[seq]
+                block = min(length, 512)
                 for half in range(2):
-                    k_head = head_lanes(k2, half)
-                    v_head = v_t[HEAD_DIM * half : HEAD_DIM * half + HEAD_DIM, start : start + length]
                     for at in range(0, length, block):
-                        scores = dot_t(k_head, q_out[start + at : start + at + block, lanes])
-                        scores = jnp.where(usable, scores, -1e30)
-                        top = jnp.max(scores, axis=0, keepdims=True)
-                        powers = jnp.exp(scores - top)
-                        total = jnp.sum(powers, axis=0, keepdims=True)
-                        prob = (powers * (1.0 / total)).astype(BF)
-                        probs[seq, 2 * pair + half, :, at : at + block] = prob
-                        feature = 128 * pair + HEAD_DIM * half
-                        mixed_t[feature : feature + HEAD_DIM, start + at : start + at + block] = dot(v_head, prob)
+                        jobs.append(dict(pair=pair, probs=probs, seq=seq, start=start, length=length, usable=usable, half=half, at=at, block=block, lanes=lanes,
+                            scores=dot_t(head_lanes(k2, half), q_out[start + at : start + at + block, lanes])))
+    for job in jobs:
+        scores = jnp.where(job["usable"], job["scores"], -1e30)
+        top = jnp.max(scores, axis=0, keepdims=True)
+        powers = jnp.exp(scores - top)
+        total = jnp.sum(powers, axis=0, keepdims=True)
+        job["prob"] = (powers * (1.0 / total)).astype(BF)
+        job["probs"][job["seq"], 2 * job["pair"] + job["half"], :, job["at"] : job["at"] + job["block"]] = job["prob"]
+
+    flipped = {pair: flip(v_out[:, 128 * pair : 128 * pair + 128]) for pair in pairs}
+    for job in jobs:
+        feature = 128 * job["pair"] + HEAD_DIM * job["half"]
+        v_head = flipped[job["pair"]][HEAD_DIM * job["half"] : HEAD_DIM * job["half"] + HEAD_DIM, job["start"] : job["start"] + job["length"]]
+        mixed_t[feature : feature + HEAD_DIM, job["start"] + job["at"] : job["start"] + job["at"] + job["block"]] = dot(v_head, job["prob"])
+    for pair in pairs:
         offset = pl.multiple_of(step * width + 128 * pair, 128)
-        mixed[:, pl.ds(offset, 128)] = flip(mixed_t[lanes, :]).astype(BF)
+        mixed[:, pl.ds(offset, 128)] = flip(mixed_t[128 * pair : 128 * pair + 128, :]).astype(BF)
 
     @pl.when(step == steps - 1)
     def _():
@@ -373,32 +376,45 @@
     width = q.shape[1]
     short_spans, long_spans = sequences(*shape)
     scale = HEAD_DIM ** (-0.5)
+    jobs = []
     for pair in range(width // 128):
         lanes = slice(128 * pair, 128 * pair + 128)
-        gm_t = flip(gm[:, lanes]).astype(F32)
-        k_t = flip(k[:, lanes])
-        product = gm_t * mixed_t[lanes, :]
-        delta = [jnp.sum(product[HEAD_DIM * h : HEAD_DIM * h + HEAD_DIM], axis=0, keepdims=True) for h in range(2)]
         for spans, probs in ((short_spans, short_p), (long_spans, long_p)):
             for seq, (start, length) in enumerate(spans):
                 here = slice(start, start + length)
-                gm2, v2, q2 = gm[here, lanes], v[here, lanes], q[here, lanes]
-                grad_value = grad_key = None
-                grad_query_t = []
                 for half in range(2):
-                    prob = probs[seq, 2 * pair + half]
-                    grad_p = dot_t(head_lanes(v2, half), gm2)
-                    grad_s = (prob.astype(F32) * (grad_p - delta[half][:, here])).astype(BF)
-                    dv = dot(prob, head_lanes(gm2, half))
-                    dk = dot(grad_s, head_lanes(q2, half))
-                    grad_value = dv if half == 0 else grad_value + dv
-                    grad_key = dk if half == 0 else grad_key + dk
-                    grad_query_t.append(dot(k_t[HEAD_DIM * half : HEAD_DIM * half + HEAD_DIM, here], grad_s))
-                grad_packed[here, 128 * pair : 128 * pair + 128] = (
-                    flip(jnp.concatenate(grad_query_t, axis=0)) * scale
-                ).astype(BF)
-                grad_packed[here, width + 128 * pair : width + 128 * pair + 128] = grad_key.astype(BF)
-                grad_packed[here, 2 * width + 128 * pair : 2 * width + 128 * pair + 128] = grad_value.astype(BF)
+                    jobs.append(dict(
+                        pair=pair, here=here, lanes=lanes, half=half, probs=probs, seq=seq,
+                        grad_p=dot_t(head_lanes(v[here, lanes], half), gm[here, lanes]),
+                    ))
+    flipped, delta = {}, {}
+    for pair in range(width // 128):
+        lanes = slice(128 * pair, 128 * pair + 128)
+        flipped[pair] = flip(k[:, lanes])
+        product = flip(gm[:, lanes]).astype(F32) * mixed_t[lanes, :]
+        for half in range(2):
+            delta[pair, half] = jnp.sum(product[HEAD_DIM * half : HEAD_DIM * half + HEAD_DIM], axis=0, keepdims=True)
+    for job in jobs:
+        pair, half = job["pair"], job["half"]
+        prob = job["probs"][job["seq"], 2 * pair + half].astype(F32)
+        job["grad_s"] = (prob * (job["grad_p"] - delta[pair, half][:, job["here"]])).astype(BF)
+    for first, second in zip(jobs[0::2], jobs[1::2]):
+        pair, here, lanes = first["pair"], first["here"], first["lanes"]
+        grad_value = grad_key = None
+        grad_query_t = []
+        for job in (first, second):
+            half = job["half"]
+            prob = job["probs"][job["seq"], 2 * pair + half]
+            dv = dot(prob, head_lanes(gm[here, lanes], half))
+            dk = dot(job["grad_s"], head_lanes(q[here, lanes], half))
+            grad_value = dv if half == 0 else grad_value + dv
+            grad_key = dk if half == 0 else grad_key + dk
+            grad_query_t.append(dot(flipped[pair][HEAD_DIM * half : HEAD_DIM * half + HEAD_DIM, here], job["grad_s"]))
+        grad_packed[here, 128 * pair : 128 * pair + 128] = (
+            flip(jnp.concatenate(grad_query_t, axis=0)) * scale
+        ).astype(BF)
+        grad_packed[here, width + 128 * pair : width + 128 * pair + 128] = grad_key.astype(BF)
+        grad_packed[here, 2 * width + 128 * pair : 2 * width + 128 * pair + 128] = grad_value.astype(BF)
     query_sum[...] = jnp.sum(grad_packed[:, :width].astype(F32), axis=0, keepdims=True)
     value_sum[...] = jnp.sum(grad_packed[:, 2 * width :].astype(F32), axis=0, keepdims=True)
     part = (

time: 252 us -> 249 us (0.988)
  Pallas kernels: 125 us -> 102 us
  waiting for transfers between devices: 74.9 us -> 94.4 us
    all_gather x1, waiting for transfers between devices: 5.91 us -> 25.4 us  [gather_weights(): feed = lax.all_gather(feed, 'dp', axis=0, tiled=False)]
    pallas_call x1, Pallas kernels: 44.5 us -> 24.9 us  [attention_forward(): pl.pallas_call(partial(attention_forward_kernel, shape, weights['slots'])...]
    pallas_call x1, Pallas kernels: 28.6 us -> 25.4 us  [attention_backward(): pl.pallas_call(partial(attention_backward_kernel, shape), grid=(steps,),...]
  transfers between devices with their start and end apart: 24 -> 24, of which waited for: 14 -> 14; matrix products, arithmetic and copies ran while one was open for 1% -> 1% of each run, Pallas kernels for 18% -> 10%
where the time goes in v3:
time: 249 us; the launch traced here: 248 us
  Pallas kernels  102 us (41%)
  waiting for transfers between devices  94.4 us (38%)
  starting transfers between devices  28.9 us (12%)
  between operations  15 us (6%)
  local copies, waits for them, and re-layouts  5.63 us (2%)
    ppermute x23, waiting for transfers between devices, exchange(): return lax.ppermute(block, 'dp', [(i, i ^ mask(i)) for i in range(count)])  68.9 us
    pallas_call x1, Pallas kernels, feed_forward_and_back(): pl.pallas_call(partial(feed_kernel, shape, steps), grid=(2 * steps + 1,),...  51.9 us
    ppermute x23, starting transfers between devices, exchange(): return lax.ppermute(block, 'dp', [(i, i ^ mask(i)) for i in range(count)])  28.9 us
    all_gather x1, waiting for transfers between devices, gather_weights(): feed = lax.all_gather(feed, 'dp', axis=0, tiled=False)  25.4 us
    pallas_call x1, Pallas kernels, attention_backward(): pl.pallas_call(partial(attention_backward_kernel, shape), grid=(steps,),...  25.4 us
    pallas_call x1, Pallas kernels, attention_forward(): pl.pallas_call(partial(attention_forward_kernel, shape, weights['slots'])...  24.9 us
  transfers between devices with their start and end apart: 24, of which 14 were waited for; matrix products, arithmetic and copies ran while one was open for 1% of the time, Pallas kernels for 10%

profile of v3, /device:TPU:0, one launch (start us, length us, event | category | flops | bytes accessed | tf_op | source)
XLA Modules:
  0.0 248.3 jit_solution(1775987088656152371)
XLA Ops:
  7.2 1.0 copy.42
  8.3 1.8 pad_maximum_fusion.2
  10.1 4.1 %collective-permute-start.3 = (bf16[32,1536]{1,0:T(8,128)(2,1)S(1)}, bf16[32,1536]{1,0:T(8,128)(2,1)S(1)}, u32[]{:S(2)}, u32[]{:S(2)}) collective-permute-start(bf16[32,1536]{1,0:T(8,128)(2,1)S(1)} %pad_maximum_fusion.10), channel_id=1, source_target_pairs={{0,16},{1,17},{2,18},{3,19},{4,20},{5,21},{6,22},{7,23},{8,24},{9,... | collective-permute-start | bytes 294920 | tf_op jit(solution)/shard_map/ppermute | solution.py:520
  14.2 0.1 collective-permute-start.6
  14.3 2.9 %collective-permute-start = (bf16[32,1536]{1,0:T(8,128)(2,1)S(1)}, bf16[32,1536]{1,0:T(8,128)(2,1)S(1)}, u32[]{:S(2)}, u32[]{:S(2)}) collective-permute-start(bf16[32,1536]{1,0:T(8,128)(2,1)S(1)} %pad_maximum_fusion.9), channel_id=1, source_target_pairs={{0,16},{1,17},{2,18},{3,19},{4,20},{5,21},{6,22},{7,23},{8,24},{9,... | collective-permute-start | bytes 294920 | tf_op jit(solution)/shard_map/ppermute | solution.py:520
  17.2 7.6 %collective-permute-done.6 = bf16[32,1024]{1,0:T(8,128)(2,1)S(1)} collective-permute-done((bf16[32,1024]{1,0:T(8,128)(2,1)S(1)}, bf16[32,1024]{1,0:T(8,128)(2,1)S(1)}, u32[]{:S(2)}, u32[]{:S(2)}) %collective-permute-start.6) | collective-permute-done | bytes 65568 | tf_op jit(solution)/shard_map/ppermute | solution.py:520
  24.9 1.8 collective-permute-start.7
  26.7 0.4 collective-permute-start.4
  27.1 1.8 collective-permute-start.1
  28.9 3.6 %collective-permute-done.4 = bf16[64,1536]{1,0:T(8,128)(2,1)S(1)} collective-permute-done((bf16[64,1536]{1,0:T(8,128)(2,1)S(1)}, bf16[64,1536]{1,0:T(8,128)(2,1)S(1)}, u32[]{:S(2)}, u32[]{:S(2)}) %collective-permute-start.4) | collective-permute-done | bytes 196640 | tf_op jit(solution)/shard_map/ppermute | solution.py:520
  32.5 1.3 collective-permute-start.5
  33.8 0.8 collective-permute-done.1
  34.6 2.7 %collective-permute-start.2 = (bf16[128,1536]{1,0:T(8,128)(2,1)S(1)}, bf16[128,1536]{1,0:T(8,128)(2,1)S(1)}, u32[]{:S(2)}, u32[]{:S(2)}) collective-permute-start(bf16[128,1536]{1,0:T(8,128)(2,1)S(1)} %pad_maximum_fusion.3), channel_id=1, source_target_pairs={{0,8},{1,9},{2,10},{3,11},{4,12},{5,13},{6,14},{7,15},{8,0},{9,1},... | collective-permute-start | bytes 1179656 | tf_op jit(solution)/shard_map/ppermute | solution.py:520
  37.3 0.1 collective-permute-start.8
  37.4 9.3 %collective-permute-done.5 = bf16[128,1536]{1,0:T(8,128)(2,1)S(1)} collective-permute-done((bf16[128,1536]{1,0:T(8,128)(2,1)S(1)}, bf16[128,1536]{1,0:T(8,128)(2,1)S(1)}, u32[]{:S(2)}, u32[]{:S(2)}) %collective-permute-start.5) | collective-permute-done | bytes 393248 | tf_op jit(solution)/shard_map/ppermute | solution.py:520
  46.7 1.4 collective-permute-start.10
  48.1 18.5 %collective-permute-done.2 = bf16[128,1536]{1,0:T(8,128)(2,1)S(1)} collective-permute-done((bf16[128,1536]{1,0:T(8,128)(2,1)S(1)}, bf16[128,1536]{1,0:T(8,128)(2,1)S(1)}, u32[]{:S(2)}, u32[]{:S(2)}) %collective-permute-start.2) | collective-permute-done | bytes 393248 | tf_op jit(solution)/shard_map/ppermute | solution.py:520
  66.7 1.3 collective-permute-start.9
  68.0 7.8 %collective-permute-done.8 = bf16[128,1024]{1,0:T(8,128)(2,1)S(1)} collective-permute-done((bf16[128,1024]{1,0:T(8,128)(2,1)S(1)}, bf16[128,1024]{1,0:T(8,128)(2,1)S(1)}, u32[]{:S(2)}, u32[]{:S(2)}) %collective-permute-start.8) | collective-permute-done | bytes 262176 | tf_op jit(solution)/shard_map/ppermute | solution.py:520
  75.8 0.9 collective-permute-start.11
  76.8 2.9 %collective-permute-start.14 = (bf16[256,1024]{1,0:T(8,128)(2,1)S(1)}, bf16[256,1024]{1,0:T(8,128)(2,1)S(1)}, u32[]{:S(2)}, u32[]{:S(2)}) collective-permute-start(bf16[256,1024]{1,0:T(8,128)(2,1)S(1)} %constant_dynamic-update-slice_fusion.refs_2_), channel_id=1, source_target_pairs={{0,1},{1,0},{2,3},{3,2},{4,5},{5,4},{6,7},{7,6},{8,9},{9,8},{10,11... | collective-permute-start | bytes 1572872 | tf_op jit(solution)/shard_map/ppermute | solution.py:520
  79.7 5.4 %collective-permute-done.11.refs_5_ = bf16[256,1024]{1,0:T(8,128)(2,1)S(1)} collective-permute-done((bf16[256,1024]{1,0:T(8,128)(2,1)S(1)}, bf16[256,1024]{1,0:T(8,128)(2,1)S(1)}, u32[]{:S(2)}, u32[]{:S(2)}) %collective-permute-start.11) | collective-permute-done | bytes 524320 | tf_op jit(solution)/shard_map/ppermute | solution.py:520
  85.1 1.6 collective-permute-start.12
  86.7 0.1 collective-permute-start.16
  86.7 0.4 collective-permute-start.15
  87.2 0.8 copy-done.13
  88.0 0.1 collective-permute-start.17
  88.8 0.1 fusion
  88.9 1.0 copy.37.keep
  89.9 2.6 %collective-permute-done.17.refs_11_ = bf16[256,1024]{1,0:T(8,128)(2,1)} collective-permute-done((bf16[256,1024]{1,0:T(8,128)(2,1)S(1)}, bf16[256,1024]{1,0:T(8,128)(2,1)}, u32[]{:S(2)}, u32[]{:S(2)}) %collective-permute-start.17) | collective-permute-done | bytes 524320 | tf_op jit(solution)/shard_map/ppermute | solution.py:520
  92.5 24.9 %attention_forward.1 = (bf16[896,1024]{1,0:T(8,128)(2,1)}, bf16[896,1024]{1,0:T(8,128)(2,1)}, bf16[896,1024]{1,0:T(8,128)(2,1)}, bf16[3,16,128,128]{3,2,1,0:T(8,...) custom-call(s32[1]{0:T(128)} %bitcast.1.me, ...), custom_call_target="tpu_custom_call" | custom-call | flops 35999997952 | bytes 40000000 | tf_op jit(solution)/shard_map/attention_forward/pallas_call | solution.py:161
  117.4 25.4 %all-gather.3.cloned.1.call-done = bf16[8192,1024]{1,0:T(8,128)(2,1)} async-done(((bf16[256,1024]{1,0:T(8,128)(2,1)}), bf16[8192,1024]{1,0:T(8,128)(2,1)}) %all-gather.3.cloned.1.call-update) | async-done | bytes 16777232 | tf_op jit(solution)/shard_map/all_gather | solution.py:570
  142.9 51.9 %feed_forward_and_back.1 = (bf16[384,1024]{1,0:T(8,128)(2,1)}, bf16[512,1024]{1,0:T(8,128)(2,1)}, bf16[896,1024]{1,0:T(8,128)(2,1)}, f32[896,1024]{1,0:T(8,128)}...) custom-call(f32[896,1]{1,0:T(8,128)} %copy.37.keep, ...), custom_call_target="tpu_custom_call" | custom-call | flops 65000001536 | bytes 60000000 | tf_op jit(solution)/shard_map/feed_forward_and_back/pallas_call | solution.py:338
  194.9 25.4 %attention_backward.1 = (bf16[384,1024]{1,0:T(8,128)(2,1)}, bf16[512,1024]{1,0:T(8,128)(2,1)}, f32[1,1024]{1,0:T(1,128)}, f32[1,1024]{1,0:T(1,128)}) custom-call(s32[3]{0:T(128)} %short_lengths.3, s32[1]{0:T(128)} %copy.53.long_lengths, bf16[896,1024]{1,0:T(8,128)(2,1)} %get-tuple-element.38.q, bf16[896,1024]{1,0:T(8,128)(2,1)} %get-tuple-element.39.k, ...), custom_call_target="tpu_custom_call" | custom-call | tf_op jit(solution)/shard_map/attention_backward/pallas_call | solution.py:455
  220.2 0.7 constant_dynamic-update-slice_fusion.10
  220.9 0.7 constant_dynamic-update-slice_fusion.9
  221.7 0.3 collective-permute-start.18
  222.0 1.0 collective-permute-done.18
  223.0 1.3 collective-permute-start.19
  224.3 2.7 %collective-permute-done.19 = f32[10240]{0:T(1024)S(1)} collective-permute-done((f32[10240]{0:T(1024)S(1)}, f32[10240]{0:T(1024)S(1)}, u32[]{:S(2)}, u32[]{:S(2)}) %collective-permute-start.19) | collective-permute-done | bytes 40992 | tf_op jit(solution)/shard_map/ppermute | solution.py:520
  227.0 1.5 collective-permute-start.20
  228.5 2.5 %collective-permute-done.20 = f32[10240]{0:T(1024)S(1)} collective-permute-done((f32[10240]{0:T(1024)S(1)}, f32[10240]{0:T(1024)S(1)}, u32[]{:S(2)}, u32[]{:S(2)}) %collective-permute-start.20) | collective-permute-done | bytes 40992 | tf_op jit(solution)/shard_map/ppermute | solution.py:520
  231.0 0.4 collective-permute-start.21
  231.4 3.6 %collective-permute-done.21 = f32[10240]{0:T(1024)S(1)} collective-permute-done((f32[10240]{0:T(1024)S(1)}, f32[10240]{0:T(1024)S(1)}, u32[]{:S(2)}, u32[]{:S(2)}) %collective-permute-start.21) | collective-permute-done | bytes 40992 | tf_op jit(solution)/shard_map/ppermute | solution.py:520
  235.0 1.6 collective-permute-start.22
  236.6 3.6 %collective-permute-done.22 = f32[10240]{0:T(1024)S(1)} collective-permute-done((f32[10240]{0:T(1024)S(1)}, f32[10240]{0:T(1024)S(1)}, u32[]{:S(2)}, u32[]{:S(2)}) %collective-permute-start.22) | collective-permute-done | bytes 40992 | tf_op jit(solution)/shard_map/ppermute | solution.py:520
  240.2 0.6 fusion.2
  240.8 0.6 slice.55
  (69 shorter events, 0.5 us)
Async XLA Ops:
  7.2 2.9 %copy-start.3 = (bf16[32,3072]{1,0:T(8,128)(2,1)S(1)}, bf16[32,3072]{1,0:T(8,128)(2,1)}, u32[]{:S(2)}) copy-start(bf16[32,3072]{1,0:T(8,128)(2,1)} %param.25) | copy-start | bytes 589828
  7.2 7.0 %copy-start.2 = (bf16[32,1024]{1,0:T(8,128)(2,1)S(1)}, bf16[32,1024]{1,0:T(8,128)(2,1)}, u32[]{:S(2)}) copy-start(bf16[32,1024]{1,0:T(8,128)(2,1)} %param.26) | copy-start | bytes 196612
  7.2 135.7 %all-gather.3.cloned.1.call-start = ((), (), s32[]{:S(2)}) async-start(), calls=%async_computation | async-start | bytes 17301504 | tf_op jit(solution)/shard_map/all_gather | solution.py:570
  10.1 16.5 %collective-permute-start.3 = (bf16[32,1536]{1,0:T(8,128)(2,1)S(1)}, bf16[32,1536]{1,0:T(8,128)(2,1)S(1)}, u32[]{:S(2)}, u32[]{:S(2)}) collective-permute-start(bf16[32,1536]{1,0:T(8,128)(2,1)S(1)} %pad_maximum_fusion.10), channel_id=1, source_target_pairs={{0,16},{1,17},{2,18},{3,19},{4,20},{5,21},{6,22},{7,23},{8,24},{9,... | collective-permute-start | bytes 294920 | tf_op jit(solution)/shard_map/ppermute | solution.py:520
  14.2 10.6 %collective-permute-start.6 = (bf16[32,1024]{1,0:T(8,128)(2,1)S(1)}, bf16[32,1024]{1,0:T(8,128)(2,1)S(1)}, u32[]{:S(2)}, u32[]{:S(2)}) collective-permute-start(bf16[32,1024]{1,0:T(8,128)(2,1)S(1)} %copy-done.2), channel_id=1, source_target_pairs={{0,16},{1,17},{2,18},{3,19},{4,20},{5,21},{6,22},{7,23},{8,24},{9,... | collective-permute-start | bytes 196616 | tf_op jit(solution)/shard_map/ppermute | solution.py:520
  14.3 12.7 %collective-permute-start = (bf16[32,1536]{1,0:T(8,128)(2,1)S(1)}, bf16[32,1536]{1,0:T(8,128)(2,1)S(1)}, u32[]{:S(2)}, u32[]{:S(2)}) collective-permute-start(bf16[32,1536]{1,0:T(8,128)(2,1)S(1)} %pad_maximum_fusion.9), channel_id=1, source_target_pairs={{0,16},{1,17},{2,18},{3,19},{4,20},{5,21},{6,22},{7,23},{8,24},{9,... | collective-permute-start | bytes 294920 | tf_op jit(solution)/shard_map/ppermute | solution.py:520
  24.9 12.3 %collective-permute-start.7 = (bf16[64,1024]{1,0:T(8,128)(2,1)S(1)}, bf16[64,1024]{1,0:T(8,128)(2,1)S(1)}, u32[]{:S(2)}, u32[]{:S(2)}) collective-permute-start(bf16[64,1024]{1,0:T(8,128)(2,1)S(1)} %pad_maximum_fusion.8), channel_id=1, source_target_pairs={{0,2},{1,5},{2,0},{3,7},{4,6},{5,1},{6,4},{7,3},{8,10},{9,13},{10,... | collective-permute-start | bytes 393224 | tf_op jit(solution)/shard_map/ppermute | solution.py:520
  26.7 5.7 %collective-permute-start.4 = (bf16[64,1536]{1,0:T(8,128)(2,1)S(1)}, bf16[64,1536]{1,0:T(8,128)(2,1)S(1)}, u32[]{:S(2)}, u32[]{:S(2)}) collective-permute-start(bf16[64,1536]{1,0:T(8,128)(2,1)S(1)} %pad_maximum_fusion.7), channel_id=1, source_target_pairs={{0,2},{1,5},{2,0},{3,7},{4,6},{5,1},{6,4},{7,3},{8,10},{9,13},{10,... | collective-permute-start | bytes 589832 | tf_op jit(solution)/shard_map/ppermute | solution.py:520
  27.1 7.4 %collective-permute-start.1 = (bf16[64,1536]{1,0:T(8,128)(2,1)S(1)}, bf16[64,1536]{1,0:T(8,128)(2,1)S(1)}, u32[]{:S(2)}, u32[]{:S(2)}) collective-permute-start(bf16[64,1536]{1,0:T(8,128)(2,1)S(1)} %pad_maximum_fusion.6), channel_id=1, source_target_pairs={{0,2},{1,5},{2,0},{3,7},{4,6},{5,1},{6,4},{7,3},{8,10},{9,13},{10,... | collective-permute-start | bytes 589832 | tf_op jit(solution)/shard_map/ppermute | solution.py:520
  32.5 14.2 %collective-permute-start.5 = (bf16[128,1536]{1,0:T(8,128)(2,1)S(1)}, bf16[128,1536]{1,0:T(8,128)(2,1)S(1)}, u32[]{:S(2)}, u32[]{:S(2)}) collective-permute-start(bf16[128,1536]{1,0:T(8,128)(2,1)S(1)} %pad_maximum_fusion.4), channel_id=1, source_target_pairs={{0,8},{1,9},{2,10},{3,11},{4,12},{5,13},{6,14},{7,15},{8,0},{9,1},... | collective-permute-start | bytes 1179656 | tf_op jit(solution)/shard_map/ppermute | solution.py:520
  34.6 32.0 %collective-permute-start.2 = (bf16[128,1536]{1,0:T(8,128)(2,1)S(1)}, bf16[128,1536]{1,0:T(8,128)(2,1)S(1)}, u32[]{:S(2)}, u32[]{:S(2)}) collective-permute-start(bf16[128,1536]{1,0:T(8,128)(2,1)S(1)} %pad_maximum_fusion.3), channel_id=1, source_target_pairs={{0,8},{1,9},{2,10},{3,11},{4,12},{5,13},{6,14},{7,15},{8,0},{9,1},... | collective-permute-start | bytes 1179656 | tf_op jit(solution)/shard_map/ppermute | solution.py:520
  37.3 38.5 %collective-permute-start.8 = (bf16[128,1024]{1,0:T(8,128)(2,1)S(1)}, bf16[128,1024]{1,0:T(8,128)(2,1)S(1)}, u32[]{:S(2)}, u32[]{:S(2)}) collective-permute-start(bf16[128,1024]{1,0:T(8,128)(2,1)S(1)} %pad_maximum_fusion.5), channel_id=1, source_target_pairs={{0,8},{1,9},{2,10},{3,11},{4,12},{5,13},{6,14},{7,15},{8,0},{9,1},... | collective-permute-start | bytes 786440 | tf_op jit(solution)/shard_map/ppermute | solution.py:520
  46.7 45.8 %copy-start = (bf16[256,1536]{1,0:T(8,128)(2,1)}, bf16[256,1536]{1,0:T(8,128)(2,1)S(1)}, u32[]{:S(2)}) copy-start(bf16[256,1536]{1,0:T(8,128)(2,1)S(1)} %pad_maximum_fusion.1.refs_1_) | copy-start | bytes 2359300
  46.7 42.1 %copy-start.10 = (s32[3]{0:T(128)S(1)}, s32[3]{0:T(128)}, u32[]{:S(2)}) copy-start(s32[3]{0:T(128)} %short_lengths.3) | copy-start | bytes 40
  46.7 40.0 %collective-permute-start.10 = (bf16[256,1536]{1,0:T(8,128)(2,1)S(1)}, bf16[256,1536]{1,0:T(8,128)(2,1)S(1)}, u32[]{:S(2)}, u32[]{:S(2)}) collective-permute-start(bf16[256,1536]{1,0:T(8,128)(2,1)S(1)} %pad_maximum_fusion.1.refs_1_), channel_id=1, source_target_pairs={{0,4},{1,3},{2,6},{3,1},{4,0},{5,7},{6,2},{7,5},{8,12},{9,11},{10,... | collective-permute-start | bytes 2359304 | tf_op jit(solution)/shard_map/ppermute | solution.py:520
  66.7 25.8 %copy-start.1 = (bf16[256,1536]{1,0:T(8,128)(2,1)}, bf16[256,1536]{1,0:T(8,128)(2,1)S(1)}, u32[]{:S(2)}) copy-start(bf16[256,1536]{1,0:T(8,128)(2,1)S(1)} %pad_maximum_fusion.refs_0_) | copy-start | bytes 2359300
  66.7 20.1 %collective-permute-start.9 = (bf16[256,1536]{1,0:T(8,128)(2,1)S(1)}, bf16[256,1536]{1,0:T(8,128)(2,1)}, u32[]{:S(2)}, u32[]{:S(2)}) collective-permute-start(bf16[256,1536]{1,0:T(8,128)(2,1)S(1)} %pad_maximum_fusion.refs_0_), channel_id=1, source_target_pairs={{0,4},{1,3},{2,6},{3,1},{4,0},{5,7},{6,2},{7,5},{8,12},{9,11},{10,... | collective-permute-start | bytes 2359304 | tf_op jit(solution)/shard_map/ppermute | solution.py:520
  75.8 16.7 %copy-start.5 = (bf16[256,1024]{1,0:T(8,128)(2,1)}, bf16[256,1024]{1,0:T(8,128)(2,1)S(1)}, u32[]{:S(2)}) copy-start(bf16[256,1024]{1,0:T(8,128)(2,1)S(1)} %constant_dynamic-update-slice_fusion.refs_2_) | copy-start | bytes 1572868
  75.8 9.2 %collective-permute-start.11 = (bf16[256,1024]{1,0:T(8,128)(2,1)S(1)}, bf16[256,1024]{1,0:T(8,128)(2,1)S(1)}, u32[]{:S(2)}, u32[]{:S(2)}) collective-permute-start(bf16[256,1024]{1,0:T(8,128)(2,1)S(1)} %constant_dynamic-update-slice_fusion.refs_2_), channel_id=1, source_target_pairs={{0,4},{1,3},{2,6},{3,1},{4,0},{5,7},{6,2},{7,5},{8,12},{9,11},{10,... | collective-permute-start | bytes 1572872 | tf_op jit(solution)/shard_map/ppermute | solution.py:520
  76.8 10.4 %collective-permute-start.14 = (bf16[256,1024]{1,0:T(8,128)(2,1)S(1)}, bf16[256,1024]{1,0:T(8,128)(2,1)S(1)}, u32[]{:S(2)}, u32[]{:S(2)}) collective-permute-start(bf16[256,1024]{1,0:T(8,128)(2,1)S(1)} %constant_dynamic-update-slice_fusion.refs_2_), channel_id=1, source_target_pairs={{0,1},{1,0},{2,3},{3,2},{4,5},{5,4},{6,7},{7,6},{8,9},{9,8},{10,11... | collective-permute-start | bytes 1572872 | tf_op jit(solution)/shard_map/ppermute | solution.py:520
  79.7 10.2 %collective-permute-start.13 = (bf16[256,1536]{1,0:T(8,128)(2,1)S(1)}, bf16[256,1536]{1,0:T(8,128)(2,1)}, u32[]{:S(2)}, u32[]{:S(2)}) collective-permute-start(bf16[256,1536]{1,0:T(8,128)(2,1)S(1)} %pad_maximum_fusion.1.refs_1_), channel_id=1, source_target_pairs={{0,1},{1,0},{2,3},{3,2},{4,5},{5,4},{6,7},{7,6},{8,9},{9,8},{10,11... | collective-permute-start | bytes 2359304 | tf_op jit(solution)/shard_map/ppermute | solution.py:520
  85.1 7.4 %copy-start.12 = (bf16[256,1024]{1,0:T(8,128)(2,1)}, bf16[256,1024]{1,0:T(8,128)(2,1)S(1)}, u32[]{:S(2)}) copy-start(bf16[256,1024]{1,0:T(8,128)(2,1)S(1)} %collective-permute-done.11.refs_5_) | copy-start | bytes 1572868
  85.1 4.8 %collective-permute-start.12 = (bf16[256,1536]{1,0:T(8,128)(2,1)S(1)}, bf16[256,1536]{1,0:T(8,128)(2,1)}, u32[]{:S(2)}, u32[]{:S(2)}) collective-permute-start(bf16[256,1536]{1,0:T(8,128)(2,1)S(1)} %pad_maximum_fusion.refs_0_), channel_id=1, source_target_pairs={{0,1},{1,0},{2,3},{3,2},{4,5},{5,4},{6,7},{7,6},{8,9},{9,8},{10,11... | collective-permute-start | bytes 2359304 | tf_op jit(solution)/shard_map/ppermute | solution.py:520
  86.7 5.8 %copy-start.11 = (bf16[256,1536]{1,0:T(8,128)(2,1)}, bf16[256,1536]{1,0:T(8,128)(2,1)S(1)}, u32[]{:S(2)}) copy-start(bf16[256,1536]{1,0:T(8,128)(2,1)S(1)} %collective-permute-done.10.refs_4_) | copy-start | bytes 2359300
  86.7 5.8 %collective-permute-start.16 = (bf16[256,1536]{1,0:T(8,128)(2,1)S(1)}, bf16[256,1536]{1,0:T(8,128)(2,1)}, u32[]{:S(2)}, u32[]{:S(2)}) collective-permute-start(bf16[256,1536]{1,0:T(8,128)(2,1)S(1)} %collective-permute-done.10.refs_4_), channel_id=1, source_target_pairs={{0,1},{1,0},{2,3},{3,2},{4,5},{5,4},{6,7},{7,6},{8,9},{9,8},{10,11... | collective-permute-start | bytes 2359304 | tf_op jit(solution)/shard_map/ppermute | solution.py:520
  86.7 5.7 %collective-permute-start.15 = (bf16[256,1536]{1,0:T(8,128)(2,1)}, bf16[256,1536]{1,0:T(8,128)(2,1)}, u32[]{:S(2)}, u32[]{:S(2)}) collective-permute-start(bf16[256,1536]{1,0:T(8,128)(2,1)} %collective-permute-done.9.refs_3_), channel_id=1, source_target_pairs={{0,1},{1,0},{2,3},{3,2},{4,5},{5,4},{6,7},{7,6},{8,9},{9,8},{10,11... | collective-permute-start | bytes 2359304 | tf_op jit(solution)/shard_map/ppermute | solution.py:520
  87.2 0.8 copy-start.13
  88.0 4.5 %collective-permute-start.17 = (bf16[256,1024]{1,0:T(8,128)(2,1)S(1)}, bf16[256,1024]{1,0:T(8,128)(2,1)}, u32[]{:S(2)}, u32[]{:S(2)}) collective-permute-start(bf16[256,1024]{1,0:T(8,128)(2,1)S(1)} %collective-permute-done.11.refs_5_), channel_id=1, source_target_pairs={{0,1},{1,0},{2,3},{3,2},{4,5},{5,4},{6,7},{7,6},{8,9},{9,8},{10,11... | collective-permute-start | bytes 1572872 | tf_op jit(solution)/shard_map/ppermute | solution.py:520
  194.8 26.8 %copy-start.9 = (f32[1,1024]{1,0:T(1,128)S(1)}, f32[1,1024]{1,0:T(1,128)}, u32[]{:S(2)}) copy-start(f32[1,1024]{1,0:T(1,128)} %get-tuple-element.52) | copy-start | bytes 12292
  194.8 26.8 %copy-start.4 = (f32[1,4096]{1,0:T(1,128)S(1)}, f32[1,4096]{1,0:T(1,128)}, u32[]{:S(2)}) copy-start(f32[1,4096]{1,0:T(1,128)} %get-tuple-element.53) | copy-start | bytes 49156
  194.8 26.8 %copy-start.8 = (f32[1,1024]{1,0:T(1,128)S(1)}, f32[1,1024]{1,0:T(1,128)}, u32[]{:S(2)}) copy-start(f32[1,1024]{1,0:T(1,128)} %get-tuple-element.54) | copy-start | bytes 12292
  194.8 26.8 %copy-start.7 = (f32[1,1024]{1,0:T(1,128)S(1)}, f32[1,1024]{1,0:T(1,128)}, u32[]{:S(2)}) copy-start(f32[1,1024]{1,0:T(1,128)} %get-tuple-element.55) | copy-start | bytes 12292
  194.9 26.8 %copy-start.6 = (f32[1,1024]{1,0:T(1,128)S(1)}, f32[1,1024]{1,0:T(1,128)}, u32[]{:S(2)}) copy-start(f32[1,1024]{1,0:T(1,128)} %get-tuple-element.56) | copy-start | bytes 12292
  221.7 1.3 collective-permute-start.18
  223.0 4.0 %collective-permute-start.19 = (f32[10240]{0:T(1024)S(1)}, f32[10240]{0:T(1024)S(1)}, u32[]{:S(2)}, u32[]{:S(2)}) collective-permute-start(f32[10240]{0:T(1024)S(1)} %add.15), channel_id=1, source_target_pairs={{0,2},{1,3},{2,0},{3,1},{4,6},{5,7},{6,4},{7,5},{8,10},{9,11},{10,... | collective-permute-start | bytes 122888 | tf_op jit(solution)/shard_map/ppermute | solution.py:520
  227.0 4.0 %collective-permute-start.20 = (f32[10240]{0:T(1024)S(1)}, f32[10240]{0:T(1024)S(1)}, u32[]{:S(2)}, u32[]{:S(2)}) collective-permute-start(f32[10240]{0:T(1024)S(1)} %add.16), channel_id=1, source_target_pairs={{0,4},{1,5},{2,6},{3,7},{4,0},{5,1},{6,2},{7,3},{8,12},{9,13},{10,... | collective-permute-start | bytes 122888 | tf_op jit(solution)/shard_map/ppermute | solution.py:520
  231.0 4.0 %collective-permute-start.21 = (f32[10240]{0:T(1024)S(1)}, f32[10240]{0:T(1024)S(1)}, u32[]{:S(2)}, u32[]{:S(2)}) collective-permute-start(f32[10240]{0:T(1024)S(1)} %add.17), channel_id=1, source_target_pairs={{0,8},{1,9},{2,10},{3,11},{4,12},{5,13},{6,14},{7,15},{8,0},{9,1},... | collective-permute-start | bytes 122888 | tf_op jit(solution)/shard_map/ppermute | solution.py:520
  235.0 5.2 %collective-permute-start.22 = (f32[10240]{0:T(1024)S(1)}, f32[10240]{0:T(1024)S(1)}, u32[]{:S(2)}, u32[]{:S(2)}) collective-permute-start(f32[10240]{0:T(1024)S(1)} %add.18), channel_id=1, source_target_pairs={{0,16},{1,17},{2,18},{3,19},{4,20},{5,21},{6,22},{7,23},{8,24},{9,... | collective-permute-start | bytes 122888 | tf_op jit(solution)/shard_map/ppermute | solution.py:520
Sparse Core Ops, SparseCore 0:
  10.9 131.9 all-gather.2

commit v4 on v3

--- a/solution.py
+++ b/solution.py
@@ -13,6 +13,7 @@
 F32 = jnp.float32
 VMEM_BYTES = 60 * 1024 * 1024
 FEED_BLOCK = 1024
+TAIL_VMEM_BYTES = 63 * 1024 * 1024
 
 
 def dot(left, right):
@@ -57,7 +58,8 @@
 ):
     pieces, refs = refs[: 3 * len(slots)], refs[3 * len(slots) :]
     (
-        qb, vb, ob, q_out, k_out, v_out, short_p, long_p, mixed_t, xhat_out, rstd_out, packed_out, output_out,
+        qb, vb, ob, gain1, beta1, q_out, k_out, v_out, short_p, long_p, mixed_t, xhat_out, rstd_out, first_out,
+        packed_out, output_out,
         x_all, mixed, packed, wo, in_sems, out_sems,
     ) = refs
     step = pl.program_id(0)
@@ -139,8 +141,10 @@
         center = first_sum - jnp.mean(first_sum, axis=-1, keepdims=True)
         spread = jnp.mean(center * center, axis=-1, keepdims=True)
         rstd = lax.rsqrt(spread + 1e-06)
-        xhat_out[...] = center * rstd
+        xhat = center * rstd
+        xhat_out[...] = xhat
         rstd_out[...] = rstd
+        first_out[...] = (xhat * gain1[...] + beta1[...]).astype(BF)
         for keep in keeps:
             keep.wait()
 
@@ -163,14 +167,14 @@
         grid=(steps,),
         in_specs=[
             smem, smem, smem, whole(xs[0].shape), whole(xs[1].shape),
-            *[anywhere] * len(weights["pieces"]), row_block, row_block, whole((1, width)),
+            *[anywhere] * len(weights["pieces"]), row_block, row_block, *[whole((1, width))] * 3,
         ],
         out_specs=[
             out_col, out_col, out_col,
             pl.BlockSpec((short_seqs, heads, short_len, short_len), lambda j: (0, j, 0, 0)),
             pl.BlockSpec((long_seqs, heads, long_len, long_len), lambda j: (0, j, 0, 0)),
             pl.BlockSpec((block, rows), lambda j: (j, 0)),
-            whole((rows, width)), whole((rows, 1)), anywhere, anywhere,
+            whole((rows, width)), whole((rows, 1)), whole((rows, width)), anywhere, anywhere,
         ],
         out_shape=[
             jax.ShapeDtypeStruct((rows, width), BF),
@@ -181,6 +185,7 @@
             jax.ShapeDtypeStruct((width, rows), F32),
             jax.ShapeDtypeStruct((rows, width), F32),
             jax.ShapeDtypeStruct((rows, 1), F32),
+            jax.ShapeDtypeStruct((rows, width), BF),
             jax.ShapeDtypeStruct((2, width, half_width), BF),
             jax.ShapeDtypeStruct((width, width), BF),
         ],
@@ -195,6 +200,7 @@
     )(
         weights["me"], *lengths, *xs, *weights["pieces"],
         vectors["query_bias"], vectors["value_bias"], vectors["output_bias"],
+        vectors["first_gain"], vectors["first_beta"],
     )
 
 
@@ -227,22 +233,65 @@
     return jnp.sum(block.reshape(block.shape[0] // 8, 8, block.shape[1]), axis=0)
 
 
-def feed_kernel(
-    shape, steps, keep, xhat, rstd, short_ct, long_ct, wi, wd, wo, inner_bias,
-    gain1, beta1, gain2, beta2, down_bias,
-    short_out, long_out, grad_mixed, grad_first_sum, second_beta_sum, down_sum, inner_sum, first_beta_sum, output_sum,
-    total, low, value, slope, sums,
+def tail_kernel(
+    shape, steps, keep, rstd, first, wi, wd, inner_bias, gain1, beta1, gain2, beta2, down_bias,
+    xhat_in, short_ct, long_ct, wo_in, q_in, k_in, v_in, short_p_in, long_p_in, mixed_t_in, packed_in,
+    short_out, long_out, short_grad, long_grad, sums_out,
+    total, low, value, slope, sums, xhat, ct, wo, short_p, long_p, mixed_t, packed, gm, sems, load_sems,
 ):
     step = pl.program_id(0)
     short_seqs, short_len, long_seqs, long_len = shape
     base = short_seqs * short_len
-    rows, width = xhat.shape
+    rows, width = total.shape
+    units = steps * value.shape[2]
+    part = packed.shape[3]
+    attention_steps = width // part
+    heads = part // HEAD_DIM
+    first_attention = 2 * steps + 1
+    turn = step - first_attention
+    slot = lax.rem(jnp.maximum(turn, 0), 2)
     chunk = 128
     wide = lambda ref: ref[...].reshape(width, -1)
     tall = lambda ref: ref[...].reshape(-1, width)
+    short_spans, long_spans = sequences(*shape)
+
+    early = [
+        pltpu.make_async_copy(short_ct, ct.at[:base], sems.at[0]),
+        pltpu.make_async_copy(long_ct, ct.at[base:], sems.at[1]),
+        pltpu.make_async_copy(xhat_in, xhat, sems.at[2]),
+        pltpu.make_async_copy(wo_in, wo, sems.at[3]),
+    ]
+    outs = [
+        pltpu.make_async_copy(ct.at[:base], short_out, sems.at[4]),
+        pltpu.make_async_copy(ct.at[base:], long_out, sems.at[5]),
+    ]
+    grads = [
+        pltpu.make_async_copy(low.at[:base], short_grad, sems.at[6]),
+        pltpu.make_async_copy(low.at[base:], long_grad, sems.at[7]),
+    ]
+
+    def loads(at, into):
+        columns = pl.ds(pl.multiple_of(at * part, part), part)
+        side = at // (attention_steps // 2)
+        within = lax.rem(at, attention_steps // 2)
+        third = packed_in.shape[2] // 3
+        pairs = [(ref.at[:, columns], slope.at[3 - into, :, part * i : part * i + part]) for i, ref in enumerate((q_in, k_in, v_in))]
+        pairs += [
+            (short_p_in.at[:, pl.ds(at * heads, heads)], short_p.at[into]),
+            (long_p_in.at[:, pl.ds(at * heads, heads)], long_p.at[into]),
+            (mixed_t_in.at[columns], mixed_t.at[into]),
+        ]
+        pairs += [
+            (
+                packed_in.at[side, :, pl.ds(pl.multiple_of(i * third + within * part, part), part)],
+                packed.at[into, i],
+            )
+            for i in range(3)
+        ]
+        return [pltpu.make_async_copy(a, b, load_sems.at[into, i]) for i, (a, b) in enumerate(pairs)]
 
     def first_part():
-        value[lax.rem(step, 2)] = dot(low[...], wide(wi)) + inner_bias[...]
+        value[lax.rem(step, 2)] = dot(first[...], wide(wi)) + inner_bias[...]
 
     def second_part():
         act, slp = gelu_and_slope(value[lax.rem(step + 1, 2)])
@@ -251,68 +300,70 @@
 
     @pl.when(step == 0)
     def _():
+        for copy in early:
+            copy.start()
+        first_part()
+        total[...] = jnp.broadcast_to(down_bias[...], total.shape)
+
+    @pl.when((step > 0) & (step < steps))
+    def _():
+        first_part()
+        second_part()
+
+    @pl.when(step == steps)
+    def _():
+        for copy in early[:3]:
+            copy.wait()
+        second_part()
+        sums[...] = jnp.zeros_like(sums)
+
         def body(i, _):
             here = pl.ds(pl.multiple_of(i * chunk, chunk), chunk)
-            first = xhat[here, :] * gain1[...] + beta1[...]
-            low[here, :] = first.astype(BF)
-            total[here, :] = first + down_bias[...]
+            second = total[here, :] + (xhat[here, :] * gain1[...] + beta1[...])
+            center = second - jnp.mean(second, axis=-1, keepdims=True)
+            spread = jnp.mean(center * center, axis=-1, keepdims=True)
+            rstd2 = lax.rsqrt(spread + 1e-06)
+            xhat2 = center * rstd2
+            usable = keep[here, :]
+            grad_out = ct[here, :].astype(F32) * usable
+            ct[here, :] = ((xhat2 * gain2[...] + beta2[...]) * usable).astype(BF)
+            grad_second = norm_gradient(grad_out, xhat2, rstd2, gain2[...])
+            rounded = grad_second.astype(BF)
+            low[here, :] = rounded
+            total[here, :] = grad_second
+            sums[0] += fold(grad_out)
+            sums[1] += fold(rounded.astype(F32))
             return 0
 
         lax.fori_loop(0, rows // chunk, body, 0)
-        first_part()
-
-    @pl.when((step > 0) & (step < steps))
-    def _():
-        first_part()
-        second_part()
-
-    @pl.when(step == steps)
-    def _():
-        second_part()
-        sums[...] = jnp.zeros_like(sums)
-
-        def rows_of(source, out, start):
-            def body(i, _):
-                there = pl.ds(pl.multiple_of(i * chunk, chunk), chunk)
-                here = pl.ds(pl.multiple_of(start + i * chunk, chunk), chunk)
-                second = total[here, :]
-                center = second - jnp.mean(second, axis=-1, keepdims=True)
-                spread = jnp.mean(center * center, axis=-1, keepdims=True)
-                rstd2 = lax.rsqrt(spread + 1e-06)
-                xhat2 = center * rstd2
-                usable = keep[here, :]
-                out[there, :] = ((xhat2 * gain2[...] + beta2[...]) * usable).astype(BF)
-                grad_out = source[there, :].astype(F32) * usable
-                grad_second = norm_gradient(grad_out, xhat2, rstd2, gain2[...])
-                rounded = grad_second.astype(BF)
-                low[here, :] = rounded
-                total[here, :] = grad_second
-                sums[0] += fold(grad_out)
-                sums[1] += fold(rounded.astype(F32))
-                return 0
-
-            lax.fori_loop(0, source.shape[0] // chunk, body, 0)
-
-        rows_of(short_ct, short_out, 0)
-        rows_of(long_ct, long_out, base)
-        second_beta_sum[...] = jnp.sum(sums[0], axis=0, keepdims=True)
-        down_sum[...] = jnp.sum(sums[1], axis=0, keepdims=True)
-
-    @pl.when(step > steps)
+        for copy in outs:
+            copy.start()
+        sums_out[:, 5 * width + units : 6 * width + units] = jnp.sum(sums[0], axis=0, keepdims=True)
+        sums_out[:, 3 * width + units : 4 * width + units] = jnp.sum(sums[1], axis=0, keepdims=True)
+
+    @pl.when((step > steps) & (step <= 2 * steps))
     def _():
         grad_inner = (dot_t(low[...], tall(wd)) * slope[2 * steps - step].astype(F32)).astype(BF)
-        inner_sum[...] = jnp.sum(grad_inner.astype(F32), axis=0, keepdims=True)
+        place = pl.multiple_of(3 * width + (2 * steps - step) * wd.shape[0] * wd.shape[1], 128)
+        sums_out[:, pl.ds(place, value.shape[2])] = jnp.sum(grad_inner.astype(F32), axis=0, keepdims=True)
         total[...] += dot_t(grad_inner, wide(wi))
 
+    @pl.when(step == 2 * steps - 1)
+    def _():
+        for copy in loads(0, 0):
+            copy.start()
+
     @pl.when(step == 2 * steps)
     def _():
+        for copy in loads(1, 1):
+            copy.start()
         sums[...] = jnp.zeros_like(sums)
 
         def body(i, _):
             here = pl.ds(pl.multiple_of(i * chunk, chunk), chunk)
             grad_first = total[here, :]
             result = norm_gradient(grad_first, xhat[here, :], rstd[here, :], gain1[...])
-            grad_first_sum[here, :] = result
+            total[here, :] = result
             branch = result.astype(BF)
             low[here, :] = branch
             sums[0] += fold(grad_first)
@@ -320,157 +371,132 @@
             return 0
 
         lax.fori_loop(0, rows // chunk, body, 0)
-        first_beta_sum[...] = jnp.sum(sums[0], axis=0, keepdims=True)
-        output_sum[...] = jnp.sum(sums[1], axis=0, keepdims=True)
-        grad_mixed[...] = dot_t(low[...], wo[...]).astype(BF)
-
-
-def feed_forward_and_back(shape, keep, xhat, rstd, cts, feed_w, output_w, vectors, block=FEED_BLOCK):
+        sums_out[:, 4 * width + units : 5 * width + units] = jnp.sum(sums[0], axis=0, keepdims=True)
+        sums_out[:, 2 * width : 3 * width] = jnp.sum(sums[1], axis=0, keepdims=True)
+        early[3].wait()
+        gm[...] = dot_t(low[...], wo[...]).astype(BF)
+
+    @pl.when(turn >= 0)
+    def _():
+        for copy in loads(turn, slot):
+            copy.wait()
+        scale = HEAD_DIM ** (-0.5)
+        own = 3 - slot
+        q = lambda here, lanes: slope[own, here, lanes]
+        k = lambda here, lanes: slope[own, here, slice(part + lanes.start, part + lanes.stop)]
+        v = lambda here, lanes: slope[own, here, slice(2 * part + lanes.start, 2 * part + lanes.stop)]
+        grad = lambda here, lanes: slope[1, here, slice(3 * part + lanes.start, 3 * part + lanes.stop)]
+        slope[1, :, 3 * part : 4 * part] = gm[:, pl.ds(pl.multiple_of(turn * part, part), part)]
+        everything = slice(0, rows)
+        jobs = []
+        for pair in range(part // 128):
+            lanes = slice(128 * pair, 128 * pair + 128)
+            for spans, probs in ((short_spans, short_p), (long_spans, long_p)):
+                for seq, (start, length) in enumerate(spans):
+                    here = slice(start, start + length)
+                    for half in range(2):
+                        jobs.append(dict(
+                            pair=pair, here=here, lanes=lanes, half=half, probs=probs, seq=seq,
+                            grad_p=dot_t(head_lanes(v(here, lanes), half), grad(here, lanes)),
+                        ))
+        flipped, delta = {}, {}
+        for pair in range(part // 128):
+            lanes = slice(128 * pair, 128 * pair + 128)
+            flipped[pair] = flip(k(everything, lanes))
+            product = flip(grad(everything, lanes)).astype(F32) * mixed_t[slot, lanes, :]
+            for half in range(2):
+                delta[pair, half] = jnp.sum(product[HEAD_DIM * half : HEAD_DIM * half + HEAD_DIM], axis=0, keepdims=True)
+        for job in jobs:
+            pair, half = job["pair"], job["half"]
+            prob = job["probs"][slot, job["seq"], 2 * pair + half].astype(F32)
+            job["grad_s"] = (prob * (job["grad_p"] - delta[pair, half][:, job["here"]])).astype(BF)
+        for one, two in zip(jobs[0::2], jobs[1::2]):
+            pair, here, lanes = one["pair"], one["here"], one["lanes"]
+            grad_value = grad_key = None
+            grad_query_t = []
+            for job in (one, two):
+                half = job["half"]
+                prob = job["probs"][slot, job["seq"], 2 * pair + half]
+                dv = dot(prob, head_lanes(grad(here, lanes), half))
+                dk = dot(job["grad_s"], head_lanes(q(here, lanes), half))
+                grad_value = dv if half == 0 else grad_value + dv
+                grad_key = dk if half == 0 else grad_key + dk
+                grad_query_t.append(dot(flipped[pair][HEAD_DIM * half : HEAD_DIM * half + HEAD_DIM, here], job["grad_s"]))
+            slope[1, here, 128 * pair : 128 * pair + 128] = (flip(jnp.concatenate(grad_query_t, axis=0)) * scale).astype(BF)
+            slope[1, here, part + 128 * pair : part + 128 * pair + 128] = grad_key.astype(BF)
+            slope[1, here, 2 * part + 128 * pair : 2 * part + 128 * pair + 128] = grad_value.astype(BF)
+        place = pl.multiple_of(turn * part, part)
+        sums_out[:, pl.ds(place, part)] = jnp.sum(slope[1, :, :part].astype(F32), axis=0, keepdims=True)
+        sums_out[:, pl.ds(width + place, part)] = jnp.sum(slope[1, :, 2 * part : 3 * part].astype(F32), axis=0, keepdims=True)
+        total[...] += (
+            dot_t(slope[1, :, :part], packed[slot, 0])
+            + dot_t(slope[1, :, part : 2 * part], packed[slot, 1])
+            + dot_t(slope[1, :, 2 * part : 3 * part], packed[slot, 2])
+        )
+
+    @pl.when((turn >= 0) & (turn < attention_steps - 2))
+    def _():
+        for copy in loads(turn + 2, slot):
+            copy.start()
+
+    @pl.when(turn == attention_steps - 1)
+    def _():
+        low[...] = (total[...] * keep[...]).astype(BF)
+        for copy in grads:
+            copy.start()
+        for copy in outs + grads:
+            copy.wait()
+
+
+def feed_and_attention_backward(shape, keep, attention, cts, feed_w, vectors, block=FEED_BLOCK):
+    q, k, v, short_p, long_p, mixed_t, xhat, rstd, first, packed_w, output_w = attention
+    short_seqs, short_len, long_seqs, long_len = shape
     rows, width = xhat.shape
+    base = short_seqs * short_len
     units = vectors["inner_bias"].shape[1]
     steps = units // block
-    whole = lambda shp: pl.BlockSpec(shp, lambda j: (0,) * len(shp))
+    part = 256
+    heads = part // HEAD_DIM
+    once = pl.Buffered(1)
+    whole = lambda shp: pl.BlockSpec(shp, lambda j: (0,) * len(shp), pipeline_mode=once)
     vec = whole((1, width))
-    back = lambda j: 2 * steps - j
+    anywhere = pl.BlockSpec(memory_space=pl.ANY)
+    back = lambda j: jnp.maximum(2 * steps - j, 0)
     inner_turn = lambda j: jnp.where(j <= steps, jnp.minimum(j, steps - 1), back(j))
     down_turn = lambda j: jnp.where(j <= steps, jnp.maximum(j - 1, 0), back(j))
-    vector_out = jax.ShapeDtypeStruct((1, width), F32)
+    total_width = 6 * width + units
     return pl.pallas_call(
-        partial(feed_kernel, shape, steps),
-        grid=(2 * steps + 1,),
+        partial(tail_kernel, shape, steps),
+        grid=(2 * steps + 1 + width // part,),
         in_specs=[
-            whole((rows, 1)), whole((rows, width)), whole((rows, 1)), whole(cts[0].shape), whole(cts[1].shape),
-            inner_block(feed_w, block, inner_turn), down_block(feed_w, block, down_turn), whole((width, width)),
+            whole((rows, 1)), whole((rows, 1)), whole((rows, width)),
+            inner_block(feed_w, block, inner_turn), down_block(feed_w, block, down_turn),
             pl.BlockSpec((1, block), lambda j: (0, jnp.minimum(j, steps - 1))), vec, vec, vec, vec, vec,
-        ],
-        out_specs=[
-            whole(cts[0].shape), whole(cts[1].shape), whole((rows, width)), whole((rows, width)),
-            vec, vec, pl.BlockSpec((1, block), lambda j: (0, jnp.minimum(back(j), steps - 1))), vec, vec,
-        ],
+            *[anywhere] * 11,
+        ],
+        out_specs=[anywhere] * 4 + [pl.BlockSpec((1, total_width), lambda j: (0, 0))],
         out_shape=[
             jax.ShapeDtypeStruct(cts[0].shape, BF), jax.ShapeDtypeStruct(cts[1].shape, BF),
-            jax.ShapeDtypeStruct((rows, width), BF), jax.ShapeDtypeStruct((rows, width), F32),
-            vector_out, vector_out, jax.ShapeDtypeStruct((1, units), F32), vector_out, vector_out,
+            jax.ShapeDtypeStruct(cts[0].shape, BF), jax.ShapeDtypeStruct(cts[1].shape, BF),
+            jax.ShapeDtypeStruct((1, total_width), F32),
         ],
         scratch_shapes=[
             pltpu.VMEM((rows, width), F32), pltpu.VMEM((rows, width), BF), pltpu.VMEM((2, rows, block), F32),
             pltpu.VMEM((steps, rows, block), BF), pltpu.VMEM((2, 8, width), F32),
-        ],
-        compiler_params=pltpu.CompilerParams(vmem_limit_bytes=VMEM_BYTES),
-        cost_estimate=pl.CostEstimate(flops=65 * 10**9, bytes_accessed=60 * 10**6, transcendentals=4 * 10**6),
-        name="feed_forward_and_back",
+            pltpu.VMEM((rows, width), F32), pltpu.VMEM((rows, width), BF), pltpu.VMEM((width, width), BF),
+            pltpu.VMEM((2, short_seqs, heads, short_len, short_len), BF),
+            pltpu.VMEM((2, long_seqs, heads, long_len, long_len), BF),
+            pltpu.VMEM((2, part, rows), F32), pltpu.VMEM((2, 3, width, part), BF), pltpu.VMEM((rows, width), BF),
+            pltpu.SemaphoreType.DMA((8,)), pltpu.SemaphoreType.DMA((2, 9)),
+        ],
+        compiler_params=pltpu.CompilerParams(vmem_limit_bytes=TAIL_VMEM_BYTES),
+        cost_estimate=pl.CostEstimate(flops=85 * 10**9, bytes_accessed=90 * 10**6, transcendentals=4 * 10**6),
+        name="feed_and_attention_backward",
     )(
-        keep, xhat, rstd, *cts, feed_w, feed_w, output_w, vectors["inner_bias"],
+        keep, rstd, first, feed_w, feed_w, vectors["inner_bias"],
         vectors["first_gain"], vectors["first_beta"], vectors["second_gain"], vectors["second_beta"], vectors["down_bias"],
+        xhat, *cts, output_w, q, k, v, short_p, long_p, mixed_t, packed_w,
     )
-
-
-def attention_backward_kernel(
-    shape, short_lengths, long_lengths, q, k, v, gm, short_p, long_p, mixed_t, wq, wk, wv, grad_first_sum,
-    short_grad, long_grad, query_sum, value_sum, grad_packed, total,
-):
-    step = pl.program_id(0)
-    steps = pl.num_programs(0)
-    short_seqs, short_len, long_seqs, long_len = shape
-    base = short_seqs * short_len
-    width = q.shape[1]
-    short_spans, long_spans = sequences(*shape)
-    scale = HEAD_DIM ** (-0.5)
-    jobs = []
-    for pair in range(width // 128):
-        lanes = slice(128 * pair, 128 * pair + 128)
-        for spans, probs in ((short_spans, short_p), (long_spans, long_p)):
-            for seq, (start, length) in enumerate(spans):
-                here = slice(start, start + length)
-                for half in range(2):
-                    jobs.append(dict(
-                        pair=pair, here=here, lanes=lanes, half=half, probs=probs, seq=seq,
-                        grad_p=dot_t(head_lanes(v[here, lanes], half), gm[here, lanes]),
-                    ))
-    flipped, delta = {}, {}
-    for pair in range(width // 128):
-        lanes = slice(128 * pair, 128 * pair + 128)
-        flipped[pair] = flip(k[:, lanes])
-        product = flip(gm[:, lanes]).astype(F32) * mixed_t[lanes, :]
-        for half in range(2):
-            delta[pair, half] = jnp.sum(product[HEAD_DIM * half : HEAD_DIM * half + HEAD_DIM], axis=0, keepdims=True)
-    for job in jobs:
-        pair, half = job["pair"], job["half"]
-        prob = job["probs"][job["seq"], 2 * pair + half].astype(F32)
-        job["grad_s"] = (prob * (job["grad_p"] - delta[pair, half][:, job["here"]])).astype(BF)
-    for first, second in zip(jobs[0::2], jobs[1::2]):
-        pair, here, lanes = first["pair"], first["here"], first["lanes"]
-        grad_value = grad_key = None
-        grad_query_t = []
-        for job in (first, second):
-            half = job["half"]
-            prob = job["probs"][job["seq"], 2 * pair + half]
-            dv = dot(prob, head_lanes(gm[here, lanes], half))
-            dk = dot(job["grad_s"], head_lanes(q[here, lanes], half))
-            grad_value = dv if half == 0 else grad_value + dv
-            grad_key = dk if half == 0 else grad_key + dk
-            grad_query_t.append(dot(flipped[pair][HEAD_DIM * half : HEAD_DIM * half + HEAD_DIM, here], job["grad_s"]))
-        grad_packed[here, 128 * pair : 128 * pair + 128] = (
-            flip(jnp.concatenate(grad_query_t, axis=0)) * scale
-        ).astype(BF)
-        grad_packed[here, width + 128 * pair : width + 128 * pair + 128] = grad_key.astype(BF)
-        grad_packed[here, 2 * width + 128 * pair : 2 * width + 128 * pair + 128] = grad_value.astype(BF)
-    query_sum[...] = jnp.sum(grad_packed[:, :width].astype(F32), axis=0, keepdims=True)
-    value_sum[...] = jnp.sum(grad_packed[:, 2 * width :].astype(F32), axis=0, keepdims=True)
-    part = (
-        dot_t(grad_packed[:, :width], wq[0])
-        + dot_t(grad_packed[:, width : 2 * width], wk[0])
-        + dot_t(grad_packed[:, 2 * width :], wv[0])
-    )
-
-    @pl.when(step == 0)
-    def _():
-        total[...] = grad_first_sum[...] + part
-
-    @pl.when(step > 0)
-    def _():
-        total[...] += part
-
-    @pl.when(step == steps - 1)
-    def _():
-        keep = row_mask(short_lengths, long_lengths, shape)
-        result = (total[...] * keep).astype(BF)
-        short_grad[...] = result[:base]
-        long_grad[...] = result[base:]
-
-
-def attention_backward(shape, lengths, q, k, v, gm, short_p, long_p, mixed_t, packed_w, grad_first_sum):
-    short_seqs, short_len, long_seqs, long_len = shape
-    rows, width = q.shape
-    block = 256
-    heads = block // HEAD_DIM
-    steps = width // block
-    base = short_seqs * short_len
-    whole = lambda shp: pl.BlockSpec(shp, lambda j: (0,) * len(shp))
-    smem = pl.BlockSpec(memory_space=pltpu.SMEM)
-    half = steps // 2
-    column = lambda off: pl.BlockSpec((1, width, block), lambda j: (j // half, 0, lax.rem(j, half) + off * half))
-    col = pl.BlockSpec((rows, block), lambda j: (0, j))
-    vec = pl.BlockSpec((1, block), lambda j: (0, j))
-    return pl.pallas_call(
-        partial(attention_backward_kernel, shape),
-        grid=(steps,),
-        in_specs=[
-            smem, smem, col, col, col, col,
-            pl.BlockSpec((short_seqs, heads, short_len, short_len), lambda j: (0, j, 0, 0)),
-            pl.BlockSpec((long_seqs, heads, long_len, long_len), lambda j: (0, j, 0, 0)),
-            pl.BlockSpec((block, rows), lambda j: (j, 0)),
-            column(0), column(1), column(2), whole((rows, width)),
-        ],
-        out_specs=[whole((base, width)), whole((rows - base, width)), vec, vec],
-        out_shape=[
-            jax.ShapeDtypeStruct((base, width), BF), jax.ShapeDtypeStruct((rows - base, width), BF),
-            jax.ShapeDtypeStruct((1, width), F32), jax.ShapeDtypeStruct((1, width), F32),
-        ],
-        scratch_shapes=[pltpu.VMEM((rows, 3 * block), BF), pltpu.VMEM((rows, width), F32)],
-        compiler_params=pltpu.CompilerParams(vmem_limit_bytes=VMEM_BYTES),
-        name="attention_backward",
-    )(*lengths, q, k, v, gm, short_p, long_p, mixed_t, packed_w, packed_w, packed_w, grad_first_sum)
 
 
 def local(
@@ -490,20 +516,15 @@
     xs = (short_input.reshape(-1, width), long_input.reshape(-1, width))
     cts = (short_cotangent.reshape(-1, width), long_cotangent.reshape(-1, width))
     weights = gather_weights(packed_weight, output_weight, inner_weight, down_weight)
-    q, k, v, short_p, long_p, mixed_t, xhat, rstd, packed_w, output_w = attention_forward(shape, lengths, xs, weights, vectors)
+    attention = attention_forward(shape, lengths, xs, weights, vectors)
     keep = jnp.concatenate([
         (jnp.arange(item.shape[1])[None, :] < length[:, None]).reshape(-1, 1)
         for item, length in ((short_input, short_lengths), (long_input, long_lengths))
     ], axis=0).astype(F32)
-    (
-        short_out, long_out, gm, grad_first_sum, second_beta_sum, down_sum, inner_sum, first_beta_sum, output_sum,
-    ) = feed_forward_and_back(shape, keep, xhat, rstd, cts, weights["feed"], output_w, vectors)
-    short_grad, long_grad, query_sum, value_sum = attention_backward(
-        shape, lengths, q, k, v, gm, short_p, long_p, mixed_t, packed_w, grad_first_sum
+    short_out, long_out, short_grad, long_grad, sums = feed_and_attention_backward(
+        shape, keep, attention, cts, weights["feed"], vectors
     )
-    sums = sum_all(jnp.concatenate(
-        [query_sum, value_sum, output_sum, inner_sum, down_sum, first_beta_sum, second_beta_sum], axis=1
-    ).reshape(-1))
+    sums = sum_all(sums).reshape(-1)
     outs = []
     at = 0
     for size in (width, width, width, inner_bias.shape[0], width, width, width):

time: 249 us -> 240 us (0.964)
  Pallas kernels: 102 us -> 94.3 us
    pallas_call x2 -> x1, Pallas kernels: 77.3 us -> 68.6 us  [feed_and_attention_backward(): pl.pallas_call(partial(tail_kernel, shape, steps), grid=(2 * steps + 1 +...]
  transfers between devices with their start and end apart: 24 -> 24, of which waited for: 14 -> 14; matrix products, arithmetic and copies ran while one was open for 1% -> 1% of each run, Pallas kernels for 10% -> 11%
where the time goes in v4:
time: 240 us
  Pallas kernels  94.3 us (39%)
  waiting for transfers between devices  94.2 us (39%)
  starting transfers between devices  28.9 us (12%)
  between operations  14.9 us (6%)
  local copies, waits for them, and re-layouts  4.17 us (2%)
  other arithmetic  3.1 us (1%)
    ppermute x23, waiting for transfers between devices, exchange(): return lax.ppermute(block, 'dp', [(i, i ^ mask(i)) for i in range(count)])  69.4 us
    pallas_call x1, Pallas kernels, feed_and_attention_backward(): pl.pallas_call(partial(tail_kernel, shape, steps), grid=(2 * steps + 1 +...  68.6 us
    ppermute x23, starting transfers between devices, exchange(): return lax.ppermute(block, 'dp', [(i, i ^ mask(i)) for i in range(count)])  28.9 us
    pallas_call x1, Pallas kernels, attention_forward(): pl.pallas_call(partial(attention_forward_kernel, shape, weights['slots'])...  25.6 us
    all_gather x1, waiting for transfers between devices, gather_weights(): feed = lax.all_gather(feed, 'dp', axis=0, tiled=False)  24.8 us
  transfers between devices with their start and end apart: 24, of which 14 were waited for; matrix products, arithmetic and copies ran while one was open for 1% of the time, Pallas kernels for 11%

profile of v4, /device:TPU:0, one launch (start us, length us, event | category | flops | bytes accessed | tf_op | source)
XLA Modules:
  0.0 239.6 jit_solution(13257672779558622488)
XLA Ops:
  7.2 1.0 copy.42
  8.3 1.8 pad_maximum_fusion.2
  10.1 4.1 %collective-permute-start.3 = (bf16[32,1536]{1,0:T(8,128)(2,1)S(1)}, bf16[32,1536]{1,0:T(8,128)(2,1)S(1)}, u32[]{:S(2)}, u32[]{:S(2)}) collective-permute-start(bf16[32,1536]{1,0:T(8,128)(2,1)S(1)} %pad_maximum_fusion.10), channel_id=1, source_target_pairs={{0,16},{1,17},{2,18},{3,19},{4,20},{5,21},{6,22},{7,23},{8,24},{9,... | collective-permute-start | bytes 294920 | tf_op jit(solution)/shard_map/ppermute | solution.py:541
  14.2 0.1 collective-permute-start.6
  14.3 2.9 %collective-permute-start = (bf16[32,1536]{1,0:T(8,128)(2,1)S(1)}, bf16[32,1536]{1,0:T(8,128)(2,1)S(1)}, u32[]{:S(2)}, u32[]{:S(2)}) collective-permute-start(bf16[32,1536]{1,0:T(8,128)(2,1)S(1)} %pad_maximum_fusion.9), channel_id=1, source_target_pairs={{0,16},{1,17},{2,18},{3,19},{4,20},{5,21},{6,22},{7,23},{8,24},{9,... | collective-permute-start | bytes 294920 | tf_op jit(solution)/shard_map/ppermute | solution.py:541
  17.3 7.6 %collective-permute-done.6 = bf16[32,1024]{1,0:T(8,128)(2,1)S(1)} collective-permute-done((bf16[32,1024]{1,0:T(8,128)(2,1)S(1)}, bf16[32,1024]{1,0:T(8,128)(2,1)S(1)}, u32[]{:S(2)}, u32[]{:S(2)}) %collective-permute-start.6) | collective-permute-done | bytes 65568 | tf_op jit(solution)/shard_map/ppermute | solution.py:541
  24.9 1.8 collective-permute-start.7
  26.7 0.4 collective-permute-start.4
  27.1 1.8 collective-permute-start.1
  28.9 3.6 %collective-permute-done.4 = bf16[64,1536]{1,0:T(8,128)(2,1)S(1)} collective-permute-done((bf16[64,1536]{1,0:T(8,128)(2,1)S(1)}, bf16[64,1536]{1,0:T(8,128)(2,1)S(1)}, u32[]{:S(2)}, u32[]{:S(2)}) %collective-permute-start.4) | collective-permute-done | bytes 196640 | tf_op jit(solution)/shard_map/ppermute | solution.py:541
  32.5 1.3 collective-permute-start.5
  33.8 0.8 collective-permute-done.1
  34.6 2.7 %collective-permute-start.2 = (bf16[128,1536]{1,0:T(8,128)(2,1)S(1)}, bf16[128,1536]{1,0:T(8,128)(2,1)S(1)}, u32[]{:S(2)}, u32[]{:S(2)}) collective-permute-start(bf16[128,1536]{1,0:T(8,128)(2,1)S(1)} %pad_maximum_fusion.3), channel_id=1, source_target_pairs={{0,8},{1,9},{2,10},{3,11},{4,12},{5,13},{6,14},{7,15},{8,0},{9,1},... | collective-permute-start | bytes 1179656 | tf_op jit(solution)/shard_map/ppermute | solution.py:541
  37.3 0.1 collective-permute-start.8
  37.4 9.3 %collective-permute-done.5 = bf16[128,1536]{1,0:T(8,128)(2,1)S(1)} collective-permute-done((bf16[128,1536]{1,0:T(8,128)(2,1)S(1)}, bf16[128,1536]{1,0:T(8,128)(2,1)S(1)}, u32[]{:S(2)}, u32[]{:S(2)}) %collective-permute-start.5) | collective-permute-done | bytes 393248 | tf_op jit(solution)/shard_map/ppermute | solution.py:541
  46.6 0.1 pad_maximum_fusion.1.refs_1_
  46.7 1.4 collective-permute-start.10
  48.1 18.5 %collective-permute-done.2 = bf16[128,1536]{1,0:T(8,128)(2,1)S(1)} collective-permute-done((bf16[128,1536]{1,0:T(8,128)(2,1)S(1)}, bf16[128,1536]{1,0:T(8,128)(2,1)S(1)}, u32[]{:S(2)}, u32[]{:S(2)}) %collective-permute-start.2) | collective-permute-done | bytes 393248 | tf_op jit(solution)/shard_map/ppermute | solution.py:541
  66.7 0.1 pad_maximum_fusion.refs_0_
  66.7 1.3 collective-permute-start.9
  68.0 8.0 %collective-permute-done.8 = bf16[128,1024]{1,0:T(8,128)(2,1)S(1)} collective-permute-done((bf16[128,1024]{1,0:T(8,128)(2,1)S(1)}, bf16[128,1024]{1,0:T(8,128)(2,1)S(1)}, u32[]{:S(2)}, u32[]{:S(2)}) %collective-permute-start.8) | collective-permute-done | bytes 262176 | tf_op jit(solution)/shard_map/ppermute | solution.py:541
  76.0 0.8 collective-permute-start.11
  76.8 3.0 %collective-permute-start.14 = (bf16[256,1024]{1,0:T(8,128)(2,1)S(1)}, bf16[256,1024]{1,0:T(8,128)(2,1)S(1)}, u32[]{:S(2)}, u32[]{:S(2)}) collective-permute-start(bf16[256,1024]{1,0:T(8,128)(2,1)S(1)} %constant_dynamic-update-slice_fusion.refs_2_), channel_id=1, source_target_pairs={{0,1},{1,0},{2,3},{3,2},{4,5},{5,4},{6,7},{7,6},{8,9},{9,8},{10,11... | collective-permute-start | bytes 1572872 | tf_op jit(solution)/shard_map/ppermute | solution.py:541
  79.7 5.5 %collective-permute-done.11.refs_5_ = bf16[256,1024]{1,0:T(8,128)(2,1)S(1)} collective-permute-done((bf16[256,1024]{1,0:T(8,128)(2,1)S(1)}, bf16[256,1024]{1,0:T(8,128)(2,1)S(1)}, u32[]{:S(2)}, u32[]{:S(2)}) %collective-permute-start.11) | collective-permute-done | bytes 524320 | tf_op jit(solution)/shard_map/ppermute | solution.py:541
  85.2 1.4 collective-permute-start.12
  86.6 0.1 collective-permute-start.16
  86.7 0.4 collective-permute-start.15
  87.2 0.8 copy-done.7
  88.0 0.1 collective-permute-start.17
  88.7 0.1 fusion
  88.8 1.0 copy.37.keep
  89.8 2.6 %collective-permute-done.17.refs_11_ = bf16[256,1024]{1,0:T(8,128)(2,1)} collective-permute-done((bf16[256,1024]{1,0:T(8,128)(2,1)S(1)}, bf16[256,1024]{1,0:T(8,128)(2,1)}, u32[]{:S(2)}, u32[]{:S(2)}) %collective-permute-start.17) | collective-permute-done | bytes 524320 | tf_op jit(solution)/shard_map/ppermute | solution.py:541
  92.5 25.6 %attention_forward.1 = (bf16[896,1024]{1,0:T(8,128)(2,1)}, bf16[896,1024]{1,0:T(8,128)(2,1)}, bf16[896,1024]{1,0:T(8,128)(2,1)}, bf16[3,16,128,128]{3,2,1,0:T(8,...) custom-call(s32[1]{0:T(128)} %bitcast.1.me, ...), custom_call_target="tpu_custom_call" | custom-call | flops 35999997952 | bytes 40000000 | tf_op jit(solution)/shard_map/attention_forward/pallas_call | solution.py:165
  118.1 24.8 %all-gather.3.cloned.1.call-done = bf16[8192,1024]{1,0:T(8,128)(2,1)} async-done(((bf16[256,1024]{1,0:T(8,128)(2,1)}), bf16[8192,1024]{1,0:T(8,128)(2,1)}) %all-gather.3.cloned.1.call-update) | async-done | bytes 16777232 | tf_op jit(solution)/shard_map/all_gather | solution.py:591
  142.9 68.6 %feed_and_attention_backward.1 = (bf16[384,1024]{1,0:T(8,128)(2,1)}, bf16[512,1024]{1,0:T(8,128)(2,1)}, bf16[384,1024]{1,0:T(8,128)(2,1)}, bf16[512,1024]{1,0:T(8,128)(2,1)}, f32[1,10240]{1,0:T(1,128)}) custom-call(f32[896,1]{1,0:T(8,128)} %copy.37.keep, f32[896,1]{1,0:T(8,128)} %get-tuple-element.27.rstd, bf16[896,1024]{1,0:T(8,128)(2,1)} %get-tuple-element.28.first, ...), custom_call_target="tpu_custom_call" | custom-call | flops 85000003584 | bytes 90000000 | tf_op jit(solution)/shard_map/feed_and_attention_backward/pallas_call | solution.py:468
  211.5 0.3 collective-permute-start.18
  211.9 1.2 collective-permute-done.18
  213.0 0.8 add.15
  213.9 1.3 collective-permute-start.19
  215.2 2.7 %collective-permute-done.19 = f32[1,10240]{1,0:T(1,128)S(1)} collective-permute-done((f32[1,10240]{1,0:T(1,128)S(1)}, f32[1,10240]{1,0:T(1,128)S(1)}, u32[]{:S(2)}, u32[]{:S(2)}) %collective-permute-start.19) | collective-permute-done | bytes 40992 | tf_op jit(solution)/shard_map/ppermute | solution.py:541
  218.0 1.5 collective-permute-start.20
  219.5 2.5 %collective-permute-done.20 = f32[1,10240]{1,0:T(1,128)S(1)} collective-permute-done((f32[1,10240]{1,0:T(1,128)S(1)}, f32[1,10240]{1,0:T(1,128)S(1)}, u32[]{:S(2)}, u32[]{:S(2)}) %collective-permute-start.20) | collective-permute-done | bytes 40992 | tf_op jit(solution)/shard_map/ppermute | solution.py:541
  222.1 0.5 collective-permute-start.21
  222.6 3.6 %collective-permute-done.21 = f32[1,10240]{1,0:T(1,128)S(1)} collective-permute-done((f32[1,10240]{1,0:T(1,128)S(1)}, f32[1,10240]{1,0:T(1,128)S(1)}, u32[]{:S(2)}, u32[]{:S(2)}) %collective-permute-start.21) | collective-permute-done | bytes 40992 | tf_op jit(solution)/shard_map/ppermute | solution.py:541
  226.2 1.8 collective-permute-start.22
  228.0 3.5 %collective-permute-done.22 = f32[1,10240]{1,0:T(1,128)S(1)} collective-permute-done((f32[1,10240]{1,0:T(1,128)S(1)}, f32[1,10240]{1,0:T(1,128)S(1)}, u32[]{:S(2)}, u32[]{:S(2)}) %collective-permute-start.22) | collective-permute-done | bytes 40992 | tf_op jit(solution)/shard_map/ppermute | solution.py:541
  231.5 0.6 fusion.2
  232.1 0.6 slice.83
  (51 shorter events, 0.5 us)
Async XLA Ops:
  7.2 2.9 %copy-start.3 = (bf16[32,3072]{1,0:T(8,128)(2,1)S(1)}, bf16[32,3072]{1,0:T(8,128)(2,1)}, u32[]{:S(2)}) copy-start(bf16[32,3072]{1,0:T(8,128)(2,1)} %param.25) | copy-start | bytes 589828
  7.2 7.1 %copy-start.2 = (bf16[32,1024]{1,0:T(8,128)(2,1)S(1)}, bf16[32,1024]{1,0:T(8,128)(2,1)}, u32[]{:S(2)}) copy-start(bf16[32,1024]{1,0:T(8,128)(2,1)} %param.26) | copy-start | bytes 196612
  7.2 135.7 %all-gather.3.cloned.1.call-start = ((), (), s32[]{:S(2)}) async-start(), calls=%async_computation | async-start | bytes 17301504 | tf_op jit(solution)/shard_map/all_gather | solution.py:591
  10.1 16.5 %collective-permute-start.3 = (bf16[32,1536]{1,0:T(8,128)(2,1)S(1)}, bf16[32,1536]{1,0:T(8,128)(2,1)S(1)}, u32[]{:S(2)}, u32[]{:S(2)}) collective-permute-start(bf16[32,1536]{1,0:T(8,128)(2,1)S(1)} %pad_maximum_fusion.10), channel_id=1, source_target_pairs={{0,16},{1,17},{2,18},{3,19},{4,20},{5,21},{6,22},{7,23},{8,24},{9,... | collective-permute-start | bytes 294920 | tf_op jit(solution)/shard_map/ppermute | solution.py:541
  14.2 10.6 %collective-permute-start.6 = (bf16[32,1024]{1,0:T(8,128)(2,1)S(1)}, bf16[32,1024]{1,0:T(8,128)(2,1)S(1)}, u32[]{:S(2)}, u32[]{:S(2)}) collective-permute-start(bf16[32,1024]{1,0:T(8,128)(2,1)S(1)} %copy-done.2), channel_id=1, source_target_pairs={{0,16},{1,17},{2,18},{3,19},{4,20},{5,21},{6,22},{7,23},{8,24},{9,... | collective-permute-start | bytes 196616 | tf_op jit(solution)/shard_map/ppermute | solution.py:541
  14.3 12.7 %collective-permute-start = (bf16[32,1536]{1,0:T(8,128)(2,1)S(1)}, bf16[32,1536]{1,0:T(8,128)(2,1)S(1)}, u32[]{:S(2)}, u32[]{:S(2)}) collective-permute-start(bf16[32,1536]{1,0:T(8,128)(2,1)S(1)} %pad_maximum_fusion.9), channel_id=1, source_target_pairs={{0,16},{1,17},{2,18},{3,19},{4,20},{5,21},{6,22},{7,23},{8,24},{9,... | collective-permute-start | bytes 294920 | tf_op jit(solution)/shard_map/ppermute | solution.py:541
  24.9 12.3 %collective-permute-start.7 = (bf16[64,1024]{1,0:T(8,128)(2,1)S(1)}, bf16[64,1024]{1,0:T(8,128)(2,1)S(1)}, u32[]{:S(2)}, u32[]{:S(2)}) collective-permute-start(bf16[64,1024]{1,0:T(8,128)(2,1)S(1)} %pad_maximum_fusion.8), channel_id=1, source_target_pairs={{0,2},{1,5},{2,0},{3,7},{4,6},{5,1},{6,4},{7,3},{8,10},{9,13},{10,... | collective-permute-start | bytes 393224 | tf_op jit(solution)/shard_map/ppermute | solution.py:541
  26.7 5.7 %collective-permute-start.4 = (bf16[64,1536]{1,0:T(8,128)(2,1)S(1)}, bf16[64,1536]{1,0:T(8,128)(2,1)S(1)}, u32[]{:S(2)}, u32[]{:S(2)}) collective-permute-start(bf16[64,1536]{1,0:T(8,128)(2,1)S(1)} %pad_maximum_fusion.7), channel_id=1, source_target_pairs={{0,2},{1,5},{2,0},{3,7},{4,6},{5,1},{6,4},{7,3},{8,10},{9,13},{10,... | collective-permute-start | bytes 589832 | tf_op jit(solution)/shard_map/ppermute | solution.py:541
  27.1 7.4 %collective-permute-start.1 = (bf16[64,1536]{1,0:T(8,128)(2,1)S(1)}, bf16[64,1536]{1,0:T(8,128)(2,1)S(1)}, u32[]{:S(2)}, u32[]{:S(2)}) collective-permute-start(bf16[64,1536]{1,0:T(8,128)(2,1)S(1)} %pad_maximum_fusion.6), channel_id=1, source_target_pairs={{0,2},{1,5},{2,0},{3,7},{4,6},{5,1},{6,4},{7,3},{8,10},{9,13},{10,... | collective-permute-start | bytes 589832 | tf_op jit(solution)/shard_map/ppermute | solution.py:541
  32.5 14.2 %collective-permute-start.5 = (bf16[128,1536]{1,0:T(8,128)(2,1)S(1)}, bf16[128,1536]{1,0:T(8,128)(2,1)S(1)}, u32[]{:S(2)}, u32[]{:S(2)}) collective-permute-start(bf16[128,1536]{1,0:T(8,128)(2,1)S(1)} %pad_maximum_fusion.4), channel_id=1, source_target_pairs={{0,8},{1,9},{2,10},{3,11},{4,12},{5,13},{6,14},{7,15},{8,0},{9,1},... | collective-permute-start | bytes 1179656 | tf_op jit(solution)/shard_map/ppermute | solution.py:541
  34.6 32.1 %collective-permute-start.2 = (bf16[128,1536]{1,0:T(8,128)(2,1)S(1)}, bf16[128,1536]{1,0:T(8,128)(2,1)S(1)}, u32[]{:S(2)}, u32[]{:S(2)}) collective-permute-start(bf16[128,1536]{1,0:T(8,128)(2,1)S(1)} %pad_maximum_fusion.3), channel_id=1, source_target_pairs={{0,8},{1,9},{2,10},{3,11},{4,12},{5,13},{6,14},{7,15},{8,0},{9,1},... | collective-permute-start | bytes 1179656 | tf_op jit(solution)/shard_map/ppermute | solution.py:541
  37.3 38.7 %collective-permute-start.8 = (bf16[128,1024]{1,0:T(8,128)(2,1)S(1)}, bf16[128,1024]{1,0:T(8,128)(2,1)S(1)}, u32[]{:S(2)}, u32[]{:S(2)}) collective-permute-start(bf16[128,1024]{1,0:T(8,128)(2,1)S(1)} %pad_maximum_fusion.5), channel_id=1, source_target_pairs={{0,8},{1,9},{2,10},{3,11},{4,12},{5,13},{6,14},{7,15},{8,0},{9,1},... | collective-permute-start | bytes 786440 | tf_op jit(solution)/shard_map/ppermute | solution.py:541
  46.7 45.8 %copy-start = (bf16[256,1536]{1,0:T(8,128)(2,1)}, bf16[256,1536]{1,0:T(8,128)(2,1)S(1)}, u32[]{:S(2)}) copy-start(bf16[256,1536]{1,0:T(8,128)(2,1)S(1)} %pad_maximum_fusion.1.refs_1_) | copy-start | bytes 2359300
  46.7 42.0 %copy-start.8 = (s32[3]{0:T(128)S(1)}, s32[3]{0:T(128)}, u32[]{:S(2)}) copy-start(s32[3]{0:T(128)} %short_lengths.1) | copy-start | bytes 40
  46.7 39.9 %collective-permute-start.10 = (bf16[256,1536]{1,0:T(8,128)(2,1)S(1)}, bf16[256,1536]{1,0:T(8,128)(2,1)S(1)}, u32[]{:S(2)}, u32[]{:S(2)}) collective-permute-start(bf16[256,1536]{1,0:T(8,128)(2,1)S(1)} %pad_maximum_fusion.1.refs_1_), channel_id=1, source_target_pairs={{0,4},{1,3},{2,6},{3,1},{4,0},{5,7},{6,2},{7,5},{8,12},{9,11},{10,... | collective-permute-start | bytes 2359304 | tf_op jit(solution)/shard_map/ppermute | solution.py:541
  66.7 25.7 %copy-start.1 = (bf16[256,1536]{1,0:T(8,128)(2,1)}, bf16[256,1536]{1,0:T(8,128)(2,1)S(1)}, u32[]{:S(2)}) copy-start(bf16[256,1536]{1,0:T(8,128)(2,1)S(1)} %pad_maximum_fusion.refs_0_) | copy-start | bytes 2359300
  66.7 20.0 %collective-permute-start.9 = (bf16[256,1536]{1,0:T(8,128)(2,1)S(1)}, bf16[256,1536]{1,0:T(8,128)(2,1)}, u32[]{:S(2)}, u32[]{:S(2)}) collective-permute-start(bf16[256,1536]{1,0:T(8,128)(2,1)S(1)} %pad_maximum_fusion.refs_0_), channel_id=1, source_target_pairs={{0,4},{1,3},{2,6},{3,1},{4,0},{5,7},{6,2},{7,5},{8,12},{9,11},{10,... | collective-permute-start | bytes 2359304 | tf_op jit(solution)/shard_map/ppermute | solution.py:541
  76.0 16.5 %copy-start.4 = (bf16[256,1024]{1,0:T(8,128)(2,1)}, bf16[256,1024]{1,0:T(8,128)(2,1)S(1)}, u32[]{:S(2)}) copy-start(bf16[256,1024]{1,0:T(8,128)(2,1)S(1)} %constant_dynamic-update-slice_fusion.refs_2_) | copy-start | bytes 1572868
  76.0 9.2 %collective-permute-start.11 = (bf16[256,1024]{1,0:T(8,128)(2,1)S(1)}, bf16[256,1024]{1,0:T(8,128)(2,1)S(1)}, u32[]{:S(2)}, u32[]{:S(2)}) collective-permute-start(bf16[256,1024]{1,0:T(8,128)(2,1)S(1)} %constant_dynamic-update-slice_fusion.refs_2_), channel_id=1, source_target_pairs={{0,4},{1,3},{2,6},{3,1},{4,0},{5,7},{6,2},{7,5},{8,12},{9,11},{10,... | collective-permute-start | bytes 1572872 | tf_op jit(solution)/shard_map/ppermute | solution.py:541
  76.8 10.4 %collective-permute-start.14 = (bf16[256,1024]{1,0:T(8,128)(2,1)S(1)}, bf16[256,1024]{1,0:T(8,128)(2,1)S(1)}, u32[]{:S(2)}, u32[]{:S(2)}) collective-permute-start(bf16[256,1024]{1,0:T(8,128)(2,1)S(1)} %constant_dynamic-update-slice_fusion.refs_2_), channel_id=1, source_target_pairs={{0,1},{1,0},{2,3},{3,2},{4,5},{5,4},{6,7},{7,6},{8,9},{9,8},{10,11... | collective-permute-start | bytes 1572872 | tf_op jit(solution)/shard_map/ppermute | solution.py:541
  79.7 10.1 %collective-permute-start.13 = (bf16[256,1536]{1,0:T(8,128)(2,1)S(1)}, bf16[256,1536]{1,0:T(8,128)(2,1)}, u32[]{:S(2)}, u32[]{:S(2)}) collective-permute-start(bf16[256,1536]{1,0:T(8,128)(2,1)S(1)} %pad_maximum_fusion.1.refs_1_), channel_id=1, source_target_pairs={{0,1},{1,0},{2,3},{3,2},{4,5},{5,4},{6,7},{7,6},{8,9},{9,8},{10,11... | collective-permute-start | bytes 2359304 | tf_op jit(solution)/shard_map/ppermute | solution.py:541
  85.2 7.2 %copy-start.6 = (bf16[256,1024]{1,0:T(8,128)(2,1)}, bf16[256,1024]{1,0:T(8,128)(2,1)S(1)}, u32[]{:S(2)}) copy-start(bf16[256,1024]{1,0:T(8,128)(2,1)S(1)} %collective-permute-done.11.refs_5_) | copy-start | bytes 1572868
  85.2 4.6 %collective-permute-start.12 = (bf16[256,1536]{1,0:T(8,128)(2,1)S(1)}, bf16[256,1536]{1,0:T(8,128)(2,1)}, u32[]{:S(2)}, u32[]{:S(2)}) collective-permute-start(bf16[256,1536]{1,0:T(8,128)(2,1)S(1)} %pad_maximum_fusion.refs_0_), channel_id=1, source_target_pairs={{0,1},{1,0},{2,3},{3,2},{4,5},{5,4},{6,7},{7,6},{8,9},{9,8},{10,11... | collective-permute-start | bytes 2359304 | tf_op jit(solution)/shard_map/ppermute | solution.py:541
  86.6 5.8 %copy-start.5 = (bf16[256,1536]{1,0:T(8,128)(2,1)}, bf16[256,1536]{1,0:T(8,128)(2,1)S(1)}, u32[]{:S(2)}) copy-start(bf16[256,1536]{1,0:T(8,128)(2,1)S(1)} %collective-permute-done.10.refs_4_) | copy-start | bytes 2359300
  86.6 5.8 %collective-permute-start.16 = (bf16[256,1536]{1,0:T(8,128)(2,1)S(1)}, bf16[256,1536]{1,0:T(8,128)(2,1)}, u32[]{:S(2)}, u32[]{:S(2)}) collective-permute-start(bf16[256,1536]{1,0:T(8,128)(2,1)S(1)} %collective-permute-done.10.refs_4_), channel_id=1, source_target_pairs={{0,1},{1,0},{2,3},{3,2},{4,5},{5,4},{6,7},{7,6},{8,9},{9,8},{10,11... | collective-permute-start | bytes 2359304 | tf_op jit(solution)/shard_map/ppermute | solution.py:541
  86.7 5.7 %collective-permute-start.15 = (bf16[256,1536]{1,0:T(8,128)(2,1)}, bf16[256,1536]{1,0:T(8,128)(2,1)}, u32[]{:S(2)}, u32[]{:S(2)}) collective-permute-start(bf16[256,1536]{1,0:T(8,128)(2,1)} %collective-permute-done.9.refs_3_), channel_id=1, source_target_pairs={{0,1},{1,0},{2,3},{3,2},{4,5},{5,4},{6,7},{7,6},{8,9},{9,8},{10,11... | collective-permute-start | bytes 2359304 | tf_op jit(solution)/shard_map/ppermute | solution.py:541
  87.2 0.8 copy-start.7
  88.0 4.5 %collective-permute-start.17 = (bf16[256,1024]{1,0:T(8,128)(2,1)S(1)}, bf16[256,1024]{1,0:T(8,128)(2,1)}, u32[]{:S(2)}, u32[]{:S(2)}) collective-permute-start(bf16[256,1024]{1,0:T(8,128)(2,1)S(1)} %collective-permute-done.11.refs_5_), channel_id=1, source_target_pairs={{0,1},{1,0},{2,3},{3,2},{4,5},{5,4},{6,7},{7,6},{8,9},{9,8},{10,11... | collective-permute-start | bytes 1572872 | tf_op jit(solution)/shard_map/ppermute | solution.py:541
  211.5 1.5 collective-permute-start.18
  213.9 4.1 %collective-permute-start.19 = (f32[1,10240]{1,0:T(1,128)S(1)}, f32[1,10240]{1,0:T(1,128)S(1)}, u32[]{:S(2)}, u32[]{:S(2)}) collective-permute-start(f32[1,10240]{1,0:T(1,128)S(1)} %add.15), channel_id=1, source_target_pairs={{0,2},{1,3},{2,0},{3,1},{4,6},{5,7},{6,4},{7,5},{8,10},{9,11},{10,... | collective-permute-start | bytes 122888 | tf_op jit(solution)/shard_map/ppermute | solution.py:541
  218.0 4.1 %collective-permute-start.20 = (f32[1,10240]{1,0:T(1,128)S(1)}, f32[1,10240]{1,0:T(1,128)S(1)}, u32[]{:S(2)}, u32[]{:S(2)}) collective-permute-start(f32[1,10240]{1,0:T(1,128)S(1)} %add.16), channel_id=1, source_target_pairs={{0,4},{1,5},{2,6},{3,7},{4,0},{5,1},{6,2},{7,3},{8,12},{9,13},{10,... | collective-permute-start | bytes 122888 | tf_op jit(solution)/shard_map/ppermute | solution.py:541
  222.1 4.1 %collective-permute-start.21 = (f32[1,10240]{1,0:T(1,128)S(1)}, f32[1,10240]{1,0:T(1,128)S(1)}, u32[]{:S(2)}, u32[]{:S(2)}) collective-permute-start(f32[1,10240]{1,0:T(1,128)S(1)} %add.17), channel_id=1, source_target_pairs={{0,8},{1,9},{2,10},{3,11},{4,12},{5,13},{6,14},{7,15},{8,0},{9,1},... | collective-permute-start | bytes 122888 | tf_op jit(solution)/shard_map/ppermute | solution.py:541
  226.2 5.2 %collective-permute-start.22 = (f32[1,10240]{1,0:T(1,128)S(1)}, f32[1,10240]{1,0:T(1,128)S(1)}, u32[]{:S(2)}, u32[]{:S(2)}) collective-permute-start(f32[1,10240]{1,0:T(1,128)S(1)} %add.18), channel_id=1, source_target_pairs={{0,16},{1,17},{2,18},{3,19},{4,20},{5,21},{6,22},{7,23},{8,24},{9,... | collective-permute-start | bytes 122888 | tf_op jit(solution)/shard_map/ppermute | solution.py:541
Sparse Core Ops, SparseCore 0:
  10.9 131.9 all-gather.2

commit v5 on v4

--- a/solution.py
+++ b/solution.py
@@ -574,6 +574,22 @@
     ]
 
 
+def pack_kernel(inner, down, out):
+    tall, width = inner.shape[0], down.shape[1]
+    blocks = inner.shape[1] // width
+    for i in range(blocks):
+        out[i * tall : (i + 1) * tall, :] = inner[:, i * width : (i + 1) * width]
+    out[blocks * tall :, :] = down[...]
+
+
+def pack_rows(inner, down):
+    width = down.shape[1]
+    rows = inner.shape[1] // width * inner.shape[0] + down.shape[0]
+    return pl.pallas_call(
+        pack_kernel, out_shape=jax.ShapeDtypeStruct((rows, width), inner.dtype), name="pack_rows"
+    )(inner, down)
+
+
 def gather_weights(packed, output, inner, down):
     count = lax.axis_size("dp")
     width = output.shape[1]
@@ -585,10 +601,7 @@
     tall = inner.shape[0]
     blocks = inner.shape[1] // width
     if count == 32:
-        feed = jnp.concatenate(
-            [inner.reshape(tall, blocks, width).transpose(1, 0, 2).reshape(blocks * tall, width), down], axis=0
-        )
-        feed = lax.all_gather(feed, "dp", axis=0, tiled=False)
+        feed = lax.all_gather(pack_rows(inner, down), "dp", axis=0, tiled=False)
         gathered = [gather_by_exchange(part) for part in parts]
         return dict(
             me=lax.axis_index("dp").reshape(1).astype(jnp.int32), slots=exchange_slots(),
@@ -610,10 +623,17 @@
     count = lax.axis_size("dp")
     if count & (count - 1):
         return lax.psum(vector, "dp")
-    bit = 1
+    vector = vector + exchange(vector, lambda i: 1) if count > 1 else vector
+    bit = 2
     while bit < count:
-        vector = vector + exchange(vector, lambda i: bit)
-        bit *= 2
+        near = exchange(vector, lambda i: bit)
+        if 2 * bit < count:
+            far = exchange(vector, lambda i: 2 * bit)
+            both = exchange(vector, lambda i: 3 * bit)
+            vector = (vector + near) + (far + both)
+        else:
+            vector = vector + near
+        bit *= 4
     return vector
 
 

time: 240 us -> 237 us (0.988)
  waiting for transfers between devices: 94.2 us -> 89 us
  starting transfers between devices: 28.9 us -> 31.7 us
    all_gather x1, waiting for transfers between devices: 24.8 us -> 18 us  [gather_weights(): feed = lax.all_gather(pack_rows(inner, down), 'dp', axis=0, tiled=False)]
    ppermute x23 -> x25, starting transfers between devices: 28.9 us -> 31.7 us  [exchange(): return lax.ppermute(block, 'dp', [(i, i ^ mask(i)) for i in range(count)])]
    ppermute x23 -> x25, waiting for transfers between devices: 69.4 us -> 71 us  [exchange(): return lax.ppermute(block, 'dp', [(i, i ^ mask(i)) for i in range(count)])]
  transfers between devices with their start and end apart: 24 -> 26, of which waited for: 14 -> 16; matrix products, arithmetic and copies ran while one was open for 1% -> 1% of each run, Pallas kernels for 11% -> 11%
where the time goes in v5:
time: 237 us; the launch traced here: 236 us
  Pallas kernels  96.2 us (41%)
  waiting for transfers between devices  89 us (38%)
  starting transfers between devices  31.7 us (13%)
  between operations  14.9 us (6%)
  local copies, waits for them, and re-layouts  3.15 us (1%)
    ppermute x25, waiting for transfers between devices, exchange(): return lax.ppermute(block, 'dp', [(i, i ^ mask(i)) for i in range(count)])  71 us
    pallas_call x1, Pallas kernels, feed_and_attention_backward(): pl.pallas_call(partial(tail_kernel, shape, steps), grid=(2 * steps + 1 +...  68.6 us
    ppermute x25, starting transfers between devices, exchange(): return lax.ppermute(block, 'dp', [(i, i ^ mask(i)) for i in range(count)])  31.7 us
    pallas_call x1, Pallas kernels, attention_forward(): pl.pallas_call(partial(attention_forward_kernel, shape, weights['slots'])...  25.6 us
    all_gather x1, waiting for transfers between devices, gather_weights(): feed = lax.all_gather(pack_rows(inner, down), 'dp', axis=0, tiled=False)  18 us
  transfers between devices with their start and end apart: 26, of which 16 were waited for; matrix products, arithmetic and copies ran while one was open for 1% of the time, Pallas kernels for 11%

profile of v5, /device:TPU:0, one launch (start us, length us, event | category | flops | bytes accessed | tf_op | source)
XLA Modules:
  0.0 236.3 jit_solution(17215831415904066044)
XLA Ops:
  7.2 1.9 pack_rows.1
  9.3 4.1 %collective-permute-start.3 = (bf16[32,1536]{1,0:T(8,128)(2,1)S(1)}, bf16[32,1536]{1,0:T(8,128)(2,1)S(1)}, u32[]{:S(2)}, u32[]{:S(2)}) collective-permute-start(bf16[32,1536]{1,0:T(8,128)(2,1)S(1)} %pad_maximum_fusion.9), channel_id=1, source_target_pairs={{0,16},{1,17},{2,18},{3,19},{4,20},{5,21},{6,22},{7,23},{8,24},{9,... | collective-permute-start | bytes 294920 | tf_op jit(solution)/shard_map/ppermute | solution.py:541
  13.4 0.1 collective-permute-start.6
  13.5 2.9 %collective-permute-start = (bf16[32,1536]{1,0:T(8,128)(2,1)S(1)}, bf16[32,1536]{1,0:T(8,128)(2,1)S(1)}, u32[]{:S(2)}, u32[]{:S(2)}) collective-permute-start(bf16[32,1536]{1,0:T(8,128)(2,1)S(1)} %pad_maximum_fusion.8), channel_id=1, source_target_pairs={{0,16},{1,17},{2,18},{3,19},{4,20},{5,21},{6,22},{7,23},{8,24},{9,... | collective-permute-start | bytes 294920 | tf_op jit(solution)/shard_map/ppermute | solution.py:541
  16.4 7.6 %collective-permute-done.6 = bf16[32,1024]{1,0:T(8,128)(2,1)S(1)} collective-permute-done((bf16[32,1024]{1,0:T(8,128)(2,1)S(1)}, bf16[32,1024]{1,0:T(8,128)(2,1)S(1)}, u32[]{:S(2)}, u32[]{:S(2)}) %collective-permute-start.6) | collective-permute-done | bytes 65568 | tf_op jit(solution)/shard_map/ppermute | solution.py:541
  24.0 1.8 collective-permute-start.7
  25.8 0.4 collective-permute-start.4
  26.2 1.8 collective-permute-start.1
  28.0 4.2 %collective-permute-done.4 = bf16[64,1536]{1,0:T(8,128)(2,1)S(1)} collective-permute-done((bf16[64,1536]{1,0:T(8,128)(2,1)S(1)}, bf16[64,1536]{1,0:T(8,128)(2,1)S(1)}, u32[]{:S(2)}, u32[]{:S(2)}) %collective-permute-start.4) | collective-permute-done | bytes 196640 | tf_op jit(solution)/shard_map/ppermute | solution.py:541
  32.2 1.6 collective-permute-start.5
  33.8 0.5 collective-permute-done.1
  34.3 1.6 collective-permute-start.2
  35.9 0.6 collective-permute-start.8
  36.5 10.7 %collective-permute-done.5 = bf16[128,1536]{1,0:T(8,128)(2,1)S(1)} collective-permute-done((bf16[128,1536]{1,0:T(8,128)(2,1)S(1)}, bf16[128,1536]{1,0:T(8,128)(2,1)S(1)}, u32[]{:S(2)}, u32[]{:S(2)}) %collective-permute-start.5) | collective-permute-done | bytes 393248 | tf_op jit(solution)/shard_map/ppermute | solution.py:541
  47.3 1.1 collective-permute-start.10
  48.4 20.0 %collective-permute-done.2 = bf16[128,1536]{1,0:T(8,128)(2,1)S(1)} collective-permute-done((bf16[128,1536]{1,0:T(8,128)(2,1)S(1)}, bf16[128,1536]{1,0:T(8,128)(2,1)S(1)}, u32[]{:S(2)}, u32[]{:S(2)}) %collective-permute-start.2) | collective-permute-done | bytes 393248 | tf_op jit(solution)/shard_map/ppermute | solution.py:541
  68.5 0.6 collective-permute-start.9
  69.1 10.6 %collective-permute-done.8 = bf16[128,1024]{1,0:T(8,128)(2,1)S(1)} collective-permute-done((bf16[128,1024]{1,0:T(8,128)(2,1)S(1)}, bf16[128,1024]{1,0:T(8,128)(2,1)S(1)}, u32[]{:S(2)}, u32[]{:S(2)}) %collective-permute-start.8) | collective-permute-done | bytes 262176 | tf_op jit(solution)/shard_map/ppermute | solution.py:541
  79.7 3.8 %collective-permute-start.14 = (bf16[256,1024]{1,0:T(8,128)(2,1)S(1)}, bf16[256,1024]{1,0:T(8,128)(2,1)S(1)}, u32[]{:S(2)}, u32[]{:S(2)}) collective-permute-start(bf16[256,1024]{1,0:T(8,128)(2,1)S(1)} %constant_dynamic-update-slice_fusion.refs_2_), channel_id=1, source_target_pairs={{0,1},{1,0},{2,3},{3,2},{4,5},{5,4},{6,7},{7,6},{8,9},{9,8},{10,11... | collective-permute-start | bytes 1572872 | tf_op jit(solution)/shard_map/ppermute | solution.py:541
  83.6 5.3 %collective-permute-done.11.refs_5_ = bf16[256,1024]{1,0:T(8,128)(2,1)S(1)} collective-permute-done((bf16[256,1024]{1,0:T(8,128)(2,1)S(1)}, bf16[256,1024]{1,0:T(8,128)(2,1)S(1)}, u32[]{:S(2)}, u32[]{:S(2)}) %collective-permute-start.11) | collective-permute-done | bytes 524320 | tf_op jit(solution)/shard_map/ppermute | solution.py:541
  88.9 2.4 %collective-permute-start.12 = (bf16[256,1536]{1,0:T(8,128)(2,1)S(1)}, bf16[256,1536]{1,0:T(8,128)(2,1)}, u32[]{:S(2)}, u32[]{:S(2)}) collective-permute-start(bf16[256,1536]{1,0:T(8,128)(2,1)S(1)} %pad_maximum_fusion.refs_0_), channel_id=1, source_target_pairs={{0,1},{1,0},{2,3},{3,2},{4,5},{5,4},{6,7},{7,6},{8,9},{9,8},{10,11... | collective-permute-start | bytes 2359304 | tf_op jit(solution)/shard_map/ppermute | solution.py:541
  91.3 0.1 collective-permute-start.16
  91.4 0.4 collective-permute-start.15
  91.9 0.8 copy-done.7
  92.7 0.1 collective-permute-start.17
  93.4 0.1 fusion
  93.5 1.0 copy.33.keep
  94.5 0.8 collective-permute-done.12.refs_6_
  95.4 3.1 %collective-permute-done.17.refs_11_ = bf16[256,1024]{1,0:T(8,128)(2,1)} collective-permute-done((bf16[256,1024]{1,0:T(8,128)(2,1)S(1)}, bf16[256,1024]{1,0:T(8,128)(2,1)}, u32[]{:S(2)}, u32[]{:S(2)}) %collective-permute-start.17) | collective-permute-done | bytes 524320 | tf_op jit(solution)/shard_map/ppermute | solution.py:541
  98.5 25.6 %attention_forward.1 = (bf16[896,1024]{1,0:T(8,128)(2,1)}, bf16[896,1024]{1,0:T(8,128)(2,1)}, bf16[896,1024]{1,0:T(8,128)(2,1)}, bf16[3,16,128,128]{3,2,1,0:T(8,...) custom-call(s32[1]{0:T(128)} %bitcast.1.me, ...), custom_call_target="tpu_custom_call" | custom-call | flops 35999997952 | bytes 40000000 | tf_op jit(solution)/shard_map/attention_forward/pallas_call | solution.py:165
  124.1 18.0 %all-gather.3.cloned.1.call-done = bf16[8192,1024]{1,0:T(8,128)(2,1)} async-done(((bf16[256,1024]{1,0:T(8,128)(2,1)}), bf16[8192,1024]{1,0:T(8,128)(2,1)}) %all-gather.3.cloned.1.call-update) | async-done | bytes 16777232 | tf_op jit(solution)/shard_map/all_gather | solution.py:604
  142.2 68.6 %feed_and_attention_backward.1 = (bf16[384,1024]{1,0:T(8,128)(2,1)}, bf16[512,1024]{1,0:T(8,128)(2,1)}, bf16[384,1024]{1,0:T(8,128)(2,1)}, bf16[512,1024]{1,0:T(8,128)(2,1)}, f32[1,10240]{1,0:T(1,128)}) custom-call(f32[896,1]{1,0:T(8,128)} %copy.33.keep, f32[896,1]{1,0:T(8,128)} %get-tuple-element.27.rstd, bf16[896,1024]{1,0:T(8,128)(2,1)} %get-tuple-element.28.first, ...), custom_call_target="tpu_custom_call" | custom-call | flops 85000003584 | bytes 90000000 | tf_op jit(solution)/shard_map/feed_and_attention_backward/pallas_call | solution.py:468
  210.8 0.3 collective-permute-start.18
  211.1 1.2 collective-permute-done.18
  212.3 0.8 add.21
  213.1 1.4 collective-permute-start.19
  214.5 0.8 collective-permute-start.20
  215.3 1.4 collective-permute-start.21
  216.7 0.5 collective-permute-done.19
  217.2 1.3 collective-permute-done.20
  218.5 1.7 collective-permute-done.21
  220.3 0.5 collective-permute-start.22
  220.7 1.6 collective-permute-start.23
  222.3 2.4 %collective-permute-start.24 = (f32[1,10240]{1,0:T(1,128)S(1)}, f32[1,10240]{1,0:T(1,128)S(1)}, u32[]{:S(2)}, u32[]{:S(2)}) collective-permute-start(f32[1,10240]{1,0:T(1,128)S(1)} %add_add_fusion.1), channel_id=1, source_target_pairs={{0,24},{1,25},{2,26},{3,27},{4,28},{5,29},{6,30},{7,31},{8,16},{9,... | collective-permute-start | bytes 122888 | tf_op jit(solution)/shard_map/ppermute | solution.py:541
  224.7 1.2 collective-permute-done.23
  225.9 2.2 collective-permute-done.24
  228.2 0.6 fusion.2
  228.8 0.6 slice.83
  (52 shorter events, 0.7 us)
Async XLA Ops:
  7.2 2.0 copy-start.3
  7.2 6.2 %copy-start.2 = (bf16[32,1024]{1,0:T(8,128)(2,1)S(1)}, bf16[32,1024]{1,0:T(8,128)(2,1)}, u32[]{:S(2)}) copy-start(bf16[32,1024]{1,0:T(8,128)(2,1)} %param.26) | copy-start | bytes 196612
  7.2 135.0 %all-gather.3.cloned.1.call-start = ((), (), s32[]{:S(2)}) async-start(), calls=%async_computation | async-start | bytes 17301504 | tf_op jit(solution)/shard_map/all_gather | solution.py:604
  9.3 16.5 %collective-permute-start.3 = (bf16[32,1536]{1,0:T(8,128)(2,1)S(1)}, bf16[32,1536]{1,0:T(8,128)(2,1)S(1)}, u32[]{:S(2)}, u32[]{:S(2)}) collective-permute-start(bf16[32,1536]{1,0:T(8,128)(2,1)S(1)} %pad_maximum_fusion.9), channel_id=1, source_target_pairs={{0,16},{1,17},{2,18},{3,19},{4,20},{5,21},{6,22},{7,23},{8,24},{9,... | collective-permute-start | bytes 294920 | tf_op jit(solution)/shard_map/ppermute | solution.py:541
  13.4 10.6 %collective-permute-start.6 = (bf16[32,1024]{1,0:T(8,128)(2,1)S(1)}, bf16[32,1024]{1,0:T(8,128)(2,1)S(1)}, u32[]{:S(2)}, u32[]{:S(2)}) collective-permute-start(bf16[32,1024]{1,0:T(8,128)(2,1)S(1)} %copy-done.2), channel_id=1, source_target_pairs={{0,16},{1,17},{2,18},{3,19},{4,20},{5,21},{6,22},{7,23},{8,24},{9,... | collective-permute-start | bytes 196616 | tf_op jit(solution)/shard_map/ppermute | solution.py:541
  13.5 12.7 %collective-permute-start = (bf16[32,1536]{1,0:T(8,128)(2,1)S(1)}, bf16[32,1536]{1,0:T(8,128)(2,1)S(1)}, u32[]{:S(2)}, u32[]{:S(2)}) collective-permute-start(bf16[32,1536]{1,0:T(8,128)(2,1)S(1)} %pad_maximum_fusion.8), channel_id=1, source_target_pairs={{0,16},{1,17},{2,18},{3,19},{4,20},{5,21},{6,22},{7,23},{8,24},{9,... | collective-permute-start | bytes 294920 | tf_op jit(solution)/shard_map/ppermute | solution.py:541
  24.0 11.9 %collective-permute-start.7 = (bf16[64,1024]{1,0:T(8,128)(2,1)S(1)}, bf16[64,1024]{1,0:T(8,128)(2,1)S(1)}, u32[]{:S(2)}, u32[]{:S(2)}) collective-permute-start(bf16[64,1024]{1,0:T(8,128)(2,1)S(1)} %pad_maximum_fusion.7), channel_id=1, source_target_pairs={{0,2},{1,5},{2,0},{3,7},{4,6},{5,1},{6,4},{7,3},{8,10},{9,13},{10,... | collective-permute-start | bytes 393224 | tf_op jit(solution)/shard_map/ppermute | solution.py:541
  25.8 6.4 %collective-permute-start.4 = (bf16[64,1536]{1,0:T(8,128)(2,1)S(1)}, bf16[64,1536]{1,0:T(8,128)(2,1)S(1)}, u32[]{:S(2)}, u32[]{:S(2)}) collective-permute-start(bf16[64,1536]{1,0:T(8,128)(2,1)S(1)} %pad_maximum_fusion.6), channel_id=1, source_target_pairs={{0,2},{1,5},{2,0},{3,7},{4,6},{5,1},{6,4},{7,3},{8,10},{9,13},{10,... | collective-permute-start | bytes 589832 | tf_op jit(solution)/shard_map/ppermute | solution.py:541
  26.2 8.1 %collective-permute-start.1 = (bf16[64,1536]{1,0:T(8,128)(2,1)S(1)}, bf16[64,1536]{1,0:T(8,128)(2,1)S(1)}, u32[]{:S(2)}, u32[]{:S(2)}) collective-permute-start(bf16[64,1536]{1,0:T(8,128)(2,1)S(1)} %pad_maximum_fusion.5), channel_id=1, source_target_pairs={{0,2},{1,5},{2,0},{3,7},{4,6},{5,1},{6,4},{7,3},{8,10},{9,13},{10,... | collective-permute-start | bytes 589832 | tf_op jit(solution)/shard_map/ppermute | solution.py:541
  32.2 15.0 %collective-permute-start.5 = (bf16[128,1536]{1,0:T(8,128)(2,1)S(1)}, bf16[128,1536]{1,0:T(8,128)(2,1)S(1)}, u32[]{:S(2)}, u32[]{:S(2)}) collective-permute-start(bf16[128,1536]{1,0:T(8,128)(2,1)S(1)} %pad_maximum_fusion.3), channel_id=1, source_target_pairs={{0,8},{1,9},{2,10},{3,11},{4,12},{5,13},{6,14},{7,15},{8,0},{9,1},... | collective-permute-start | bytes 1179656 | tf_op jit(solution)/shard_map/ppermute | solution.py:541
  34.3 34.1 %collective-permute-start.2 = (bf16[128,1536]{1,0:T(8,128)(2,1)S(1)}, bf16[128,1536]{1,0:T(8,128)(2,1)S(1)}, u32[]{:S(2)}, u32[]{:S(2)}) collective-permute-start(bf16[128,1536]{1,0:T(8,128)(2,1)S(1)} %pad_maximum_fusion.2), channel_id=1, source_target_pairs={{0,8},{1,9},{2,10},{3,11},{4,12},{5,13},{6,14},{7,15},{8,0},{9,1},... | collective-permute-start | bytes 1179656 | tf_op jit(solution)/shard_map/ppermute | solution.py:541
  35.9 43.7 %collective-permute-start.8 = (bf16[128,1024]{1,0:T(8,128)(2,1)S(1)}, bf16[128,1024]{1,0:T(8,128)(2,1)S(1)}, u32[]{:S(2)}, u32[]{:S(2)}) collective-permute-start(bf16[128,1024]{1,0:T(8,128)(2,1)S(1)} %pad_maximum_fusion.4), channel_id=1, source_target_pairs={{0,8},{1,9},{2,10},{3,11},{4,12},{5,13},{6,14},{7,15},{8,0},{9,1},... | collective-permute-start | bytes 786440 | tf_op jit(solution)/shard_map/ppermute | solution.py:541
  47.3 51.2 %copy-start = (bf16[256,1536]{1,0:T(8,128)(2,1)}, bf16[256,1536]{1,0:T(8,128)(2,1)S(1)}, u32[]{:S(2)}) copy-start(bf16[256,1536]{1,0:T(8,128)(2,1)S(1)} %pad_maximum_fusion.1.refs_1_) | copy-start | bytes 2359300
  47.3 46.1 %copy-start.8 = (s32[3]{0:T(128)S(1)}, s32[3]{0:T(128)}, u32[]{:S(2)}) copy-start(s32[3]{0:T(128)} %short_lengths.1) | copy-start | bytes 40
  47.3 44.0 %collective-permute-start.10 = (bf16[256,1536]{1,0:T(8,128)(2,1)S(1)}, bf16[256,1536]{1,0:T(8,128)(2,1)S(1)}, u32[]{:S(2)}, u32[]{:S(2)}) collective-permute-start(bf16[256,1536]{1,0:T(8,128)(2,1)S(1)} %pad_maximum_fusion.1.refs_1_), channel_id=1, source_target_pairs={{0,4},{1,3},{2,6},{3,1},{4,0},{5,7},{6,2},{7,5},{8,12},{9,11},{10,... | collective-permute-start | bytes 2359304 | tf_op jit(solution)/shard_map/ppermute | solution.py:541
  68.4 30.0 %copy-start.1 = (bf16[256,1536]{1,0:T(8,128)(2,1)}, bf16[256,1536]{1,0:T(8,128)(2,1)S(1)}, u32[]{:S(2)}) copy-start(bf16[256,1536]{1,0:T(8,128)(2,1)S(1)} %pad_maximum_fusion.refs_0_) | copy-start | bytes 2359300
  68.5 23.0 %collective-permute-start.9 = (bf16[256,1536]{1,0:T(8,128)(2,1)S(1)}, bf16[256,1536]{1,0:T(8,128)(2,1)}, u32[]{:S(2)}, u32[]{:S(2)}) collective-permute-start(bf16[256,1536]{1,0:T(8,128)(2,1)S(1)} %pad_maximum_fusion.refs_0_), channel_id=1, source_target_pairs={{0,4},{1,3},{2,6},{3,1},{4,0},{5,7},{6,2},{7,5},{8,12},{9,11},{10,... | collective-permute-start | bytes 2359304 | tf_op jit(solution)/shard_map/ppermute | solution.py:541
  79.7 18.8 %copy-start.4 = (bf16[256,1024]{1,0:T(8,128)(2,1)}, bf16[256,1024]{1,0:T(8,128)(2,1)S(1)}, u32[]{:S(2)}) copy-start(bf16[256,1024]{1,0:T(8,128)(2,1)S(1)} %constant_dynamic-update-slice_fusion.refs_2_) | copy-start | bytes 1572868
  79.7 9.2 %collective-permute-start.11 = (bf16[256,1024]{1,0:T(8,128)(2,1)S(1)}, bf16[256,1024]{1,0:T(8,128)(2,1)S(1)}, u32[]{:S(2)}, u32[]{:S(2)}) collective-permute-start(bf16[256,1024]{1,0:T(8,128)(2,1)S(1)} %constant_dynamic-update-slice_fusion.refs_2_), channel_id=1, source_target_pairs={{0,4},{1,3},{2,6},{3,1},{4,0},{5,7},{6,2},{7,5},{8,12},{9,11},{10,... | collective-permute-start | bytes 1572872 | tf_op jit(solution)/shard_map/ppermute | solution.py:541
  79.7 12.1 %collective-permute-start.14 = (bf16[256,1024]{1,0:T(8,128)(2,1)S(1)}, bf16[256,1024]{1,0:T(8,128)(2,1)S(1)}, u32[]{:S(2)}, u32[]{:S(2)}) collective-permute-start(bf16[256,1024]{1,0:T(8,128)(2,1)S(1)} %constant_dynamic-update-slice_fusion.refs_2_), channel_id=1, source_target_pairs={{0,1},{1,0},{2,3},{3,2},{4,5},{5,4},{6,7},{7,6},{8,9},{9,8},{10,11... | collective-permute-start | bytes 1572872 | tf_op jit(solution)/shard_map/ppermute | solution.py:541
  83.6 10.9 %collective-permute-start.13 = (bf16[256,1536]{1,0:T(8,128)(2,1)S(1)}, bf16[256,1536]{1,0:T(8,128)(2,1)}, u32[]{:S(2)}, u32[]{:S(2)}) collective-permute-start(bf16[256,1536]{1,0:T(8,128)(2,1)S(1)} %pad_maximum_fusion.1.refs_1_), channel_id=1, source_target_pairs={{0,1},{1,0},{2,3},{3,2},{4,5},{5,4},{6,7},{7,6},{8,9},{9,8},{10,11... | collective-permute-start | bytes 2359304 | tf_op jit(solution)/shard_map/ppermute | solution.py:541
  88.9 9.6 %copy-start.6 = (bf16[256,1024]{1,0:T(8,128)(2,1)}, bf16[256,1024]{1,0:T(8,128)(2,1)S(1)}, u32[]{:S(2)}) copy-start(bf16[256,1024]{1,0:T(8,128)(2,1)S(1)} %collective-permute-done.11.refs_5_) | copy-start | bytes 1572868
  88.9 6.4 %collective-permute-start.12 = (bf16[256,1536]{1,0:T(8,128)(2,1)S(1)}, bf16[256,1536]{1,0:T(8,128)(2,1)}, u32[]{:S(2)}, u32[]{:S(2)}) collective-permute-start(bf16[256,1536]{1,0:T(8,128)(2,1)S(1)} %pad_maximum_fusion.refs_0_), channel_id=1, source_target_pairs={{0,1},{1,0},{2,3},{3,2},{4,5},{5,4},{6,7},{7,6},{8,9},{9,8},{10,11... | collective-permute-start | bytes 2359304 | tf_op jit(solution)/shard_map/ppermute | solution.py:541
  91.3 7.2 %copy-start.5 = (bf16[256,1536]{1,0:T(8,128)(2,1)}, bf16[256,1536]{1,0:T(8,128)(2,1)S(1)}, u32[]{:S(2)}) copy-start(bf16[256,1536]{1,0:T(8,128)(2,1)S(1)} %collective-permute-done.10.refs_4_) | copy-start | bytes 2359300
  91.3 7.1 %collective-permute-start.16 = (bf16[256,1536]{1,0:T(8,128)(2,1)S(1)}, bf16[256,1536]{1,0:T(8,128)(2,1)}, u32[]{:S(2)}, u32[]{:S(2)}) collective-permute-start(bf16[256,1536]{1,0:T(8,128)(2,1)S(1)} %collective-permute-done.10.refs_4_), channel_id=1, source_target_pairs={{0,1},{1,0},{2,3},{3,2},{4,5},{5,4},{6,7},{7,6},{8,9},{9,8},{10,11... | collective-permute-start | bytes 2359304 | tf_op jit(solution)/shard_map/ppermute | solution.py:541
  91.4 7.1 %collective-permute-start.15 = (bf16[256,1536]{1,0:T(8,128)(2,1)}, bf16[256,1536]{1,0:T(8,128)(2,1)}, u32[]{:S(2)}, u32[]{:S(2)}) collective-permute-start(bf16[256,1536]{1,0:T(8,128)(2,1)} %collective-permute-done.9.refs_3_), channel_id=1, source_target_pairs={{0,1},{1,0},{2,3},{3,2},{4,5},{5,4},{6,7},{7,6},{8,9},{9,8},{10,11... | collective-permute-start | bytes 2359304 | tf_op jit(solution)/shard_map/ppermute | solution.py:541
  91.9 0.8 copy-start.7
  92.7 5.8 %collective-permute-start.17 = (bf16[256,1024]{1,0:T(8,128)(2,1)S(1)}, bf16[256,1024]{1,0:T(8,128)(2,1)}, u32[]{:S(2)}, u32[]{:S(2)}) collective-permute-start(bf16[256,1024]{1,0:T(8,128)(2,1)S(1)} %collective-permute-done.11.refs_5_), channel_id=1, source_target_pairs={{0,1},{1,0},{2,3},{3,2},{4,5},{5,4},{6,7},{7,6},{8,9},{9,8},{10,11... | collective-permute-start | bytes 1572872 | tf_op jit(solution)/shard_map/ppermute | solution.py:541
  210.8 1.5 collective-permute-start.18
  213.1 4.1 %collective-permute-start.19 = (f32[1,10240]{1,0:T(1,128)S(1)}, f32[1,10240]{1,0:T(1,128)S(1)}, u32[]{:S(2)}, u32[]{:S(2)}) collective-permute-start(f32[1,10240]{1,0:T(1,128)S(1)} %add.21), channel_id=1, source_target_pairs={{0,2},{1,3},{2,0},{3,1},{4,6},{5,7},{6,4},{7,5},{8,10},{9,11},{10,... | collective-permute-start | bytes 122888 | tf_op jit(solution)/shard_map/ppermute | solution.py:541
  214.5 4.0 %collective-permute-start.20 = (f32[1,10240]{1,0:T(1,128)S(1)}, f32[1,10240]{1,0:T(1,128)S(1)}, u32[]{:S(2)}, u32[]{:S(2)}) collective-permute-start(f32[1,10240]{1,0:T(1,128)S(1)} %add.21), channel_id=1, source_target_pairs={{0,4},{1,5},{2,6},{3,7},{4,0},{5,1},{6,2},{7,3},{8,12},{9,13},{10,... | collective-permute-start | bytes 122888 | tf_op jit(solution)/shard_map/ppermute | solution.py:541
  215.3 4.9 %collective-permute-start.21 = (f32[1,10240]{1,0:T(1,128)S(1)}, f32[1,10240]{1,0:T(1,128)S(1)}, u32[]{:S(2)}, u32[]{:S(2)}) collective-permute-start(f32[1,10240]{1,0:T(1,128)S(1)} %add.21), channel_id=1, source_target_pairs={{0,6},{1,7},{2,4},{3,5},{4,2},{5,3},{6,0},{7,1},{8,14},{9,15},{10,... | collective-permute-start | bytes 122888 | tf_op jit(solution)/shard_map/ppermute | solution.py:541
  220.3 4.5 %collective-permute-start.22 = (f32[1,10240]{1,0:T(1,128)S(1)}, f32[1,10240]{1,0:T(1,128)S(1)}, u32[]{:S(2)}, u32[]{:S(2)}) collective-permute-start(f32[1,10240]{1,0:T(1,128)S(1)} %add_add_fusion.1), channel_id=1, source_target_pairs={{0,8},{1,9},{2,10},{3,11},{4,12},{5,13},{6,14},{7,15},{8,0},{9,1},... | collective-permute-start | bytes 122888 | tf_op jit(solution)/shard_map/ppermute | solution.py:541
  220.7 5.1 %collective-permute-start.23 = (f32[1,10240]{1,0:T(1,128)S(1)}, f32[1,10240]{1,0:T(1,128)S(1)}, u32[]{:S(2)}, u32[]{:S(2)}) collective-permute-start(f32[1,10240]{1,0:T(1,128)S(1)} %add_add_fusion.1), channel_id=1, source_target_pairs={{0,16},{1,17},{2,18},{3,19},{4,20},{5,21},{6,22},{7,23},{8,24},{9,... | collective-permute-start | bytes 122888 | tf_op jit(solution)/shard_map/ppermute | solution.py:541
  222.3 5.8 %collective-permute-start.24 = (f32[1,10240]{1,0:T(1,128)S(1)}, f32[1,10240]{1,0:T(1,128)S(1)}, u32[]{:S(2)}, u32[]{:S(2)}) collective-permute-start(f32[1,10240]{1,0:T(1,128)S(1)} %add_add_fusion.1), channel_id=1, source_target_pairs={{0,24},{1,25},{2,26},{3,27},{4,28},{5,29},{6,30},{7,31},{8,16},{9,... | collective-permute-start | bytes 122888 | tf_op jit(solution)/shard_map/ppermute | solution.py:541
Sparse Core Ops, SparseCore 0:
  10.9 131.2 all-gather.2

commit v6 on v5

--- a/solution.py
+++ b/solution.py
@@ -237,7 +237,7 @@
     shape, steps, keep, rstd, first, wi, wd, inner_bias, gain1, beta1, gain2, beta2, down_bias,
     xhat_in, short_ct, long_ct, wo_in, q_in, k_in, v_in, short_p_in, long_p_in, mixed_t_in, packed_in,
     short_out, long_out, short_grad, long_grad, sums_out,
-    total, low, value, slope, sums, xhat, ct, wo, short_p, long_p, mixed_t, packed, gm, sems, load_sems,
+    total, low, value, slope, sums, inner_fold, xhat, ct, wo, short_p, long_p, mixed_t, packed, gm, sems, load_sems,
 ):
     step = pl.program_id(0)
     short_seqs, short_len, long_seqs, long_len = shape
@@ -341,7 +341,7 @@
         sums_out[:, 5 * width + units : 6 * width + units] = jnp.sum(sums[0], axis=0, keepdims=True)
         sums_out[:, 3 * width + units : 4 * width + units] = jnp.sum(sums[1], axis=0, keepdims=True)
 
-    @pl.when((step > steps) & (step <= 2 * steps))
+    @pl.when((step > steps) & (step < 2 * steps))
     def _():
         grad_inner = (dot_t(low[...], tall(wd)) * slope[2 * steps - step].astype(F32)).astype(BF)
         place = pl.multiple_of(3 * width + (2 * steps - step) * wd.shape[0] * wd.shape[1], 128)
@@ -357,24 +357,36 @@
     def _():
         for copy in loads(1, 1):
             copy.start()
+        early[3].wait()
         sums[...] = jnp.zeros_like(sums)
-
-        def body(i, _):
-            here = pl.ds(pl.multiple_of(i * chunk, chunk), chunk)
-            grad_first = total[here, :]
-            result = norm_gradient(grad_first, xhat[here, :], rstd[here, :], gain1[...])
-            total[here, :] = result
-            branch = result.astype(BF)
-            low[here, :] = branch
-            sums[0] += fold(grad_first)
-            sums[1] += fold(branch.astype(F32))
-            return 0
-
-        lax.fori_loop(0, rows // chunk, body, 0)
+        inner_fold[...] = jnp.zeros_like(inner_fold)
+        chunks = [slice(at, at + rows // 2) for at in range(0, rows, rows // 2)]
+        firsts = {}
+        for turn_of in range(len(chunks) + 2):
+            if turn_of < len(chunks):
+                ahead = chunks[turn_of]
+                grad_active = dot_t(low[ahead], tall(wd))
+            if turn_of >= 2:
+                back_here = chunks[turn_of - 2]
+                mixed_grad = dot_t(low[back_here], wo[...])
+            if 0 < turn_of <= len(chunks):
+                here = chunks[turn_of - 1]
+                grad_first = firsts.pop(turn_of - 1)
+                result = norm_gradient(grad_first, xhat[here], rstd[here], gain1[...])
+                total[here] = result
+                branch = result.astype(BF)
+                low[here] = branch
+                sums[0] += fold(grad_first)
+                sums[1] += fold(branch.astype(F32))
+            if turn_of < len(chunks):
+                grad_inner = (grad_active * slope[0, ahead].astype(F32)).astype(BF)
+                firsts[turn_of] = total[ahead] + dot_t(grad_inner, wide(wi))
+                inner_fold[...] += fold(grad_inner.astype(F32))
+            if turn_of >= 2:
+                gm[back_here] = mixed_grad.astype(BF)
         sums_out[:, 4 * width + units : 5 * width + units] = jnp.sum(sums[0], axis=0, keepdims=True)
         sums_out[:, 2 * width : 3 * width] = jnp.sum(sums[1], axis=0, keepdims=True)
-        early[3].wait()
-        gm[...] = dot_t(low[...], wo[...]).astype(BF)
+        sums_out[:, 3 * width : 3 * width + value.shape[2]] = jnp.sum(inner_fold[...], axis=0, keepdims=True)
 
     @pl.when(turn >= 0)
     def _():
@@ -412,17 +424,23 @@
             job["grad_s"] = (prob * (job["grad_p"] - delta[pair, half][:, job["here"]])).astype(BF)
         for one, two in zip(jobs[0::2], jobs[1::2]):
             pair, here, lanes = one["pair"], one["here"], one["lanes"]
-            grad_value = grad_key = None
-            grad_query_t = []
-            for job in (one, two):
-                half = job["half"]
-                prob = job["probs"][slot, job["seq"], 2 * pair + half]
-                dv = dot(prob, head_lanes(grad(here, lanes), half))
-                dk = dot(job["grad_s"], head_lanes(q(here, lanes), half))
-                grad_value = dv if half == 0 else grad_value + dv
-                grad_key = dk if half == 0 else grad_key + dk
-                grad_query_t.append(dot(flipped[pair][HEAD_DIM * half : HEAD_DIM * half + HEAD_DIM, here], job["grad_s"]))
-            slope[1, here, 128 * pair : 128 * pair + 128] = (flip(jnp.concatenate(grad_query_t, axis=0)) * scale).astype(BF)
+            probs2 = [job["probs"][slot, job["seq"], 2 * pair + job["half"]] for job in (one, two)]
+            grad_value = dot(
+                jnp.concatenate(probs2, axis=1),
+                jnp.concatenate([head_lanes(grad(here, lanes), half) for half in range(2)], axis=0),
+            )
+            grad_key = dot(
+                jnp.concatenate([one["grad_s"], two["grad_s"]], axis=1),
+                jnp.concatenate([head_lanes(q(here, lanes), half) for half in range(2)], axis=0),
+            )
+            k_t = flipped[pair][:, here]
+            first_head = lax.broadcasted_iota(jnp.int32, k_t.shape, 0) < HEAD_DIM
+            zero = jnp.zeros_like(k_t)
+            grad_query_t = dot(
+                jnp.concatenate([jnp.where(first_head, k_t, zero), jnp.where(first_head, zero, k_t)], axis=1),
+                jnp.concatenate([one["grad_s"], two["grad_s"]], axis=0),
+            )
+            slope[1, here, 128 * pair : 128 * pair + 128] = (flip(grad_query_t) * scale).astype(BF)
             slope[1, here, part + 128 * pair : part + 128 * pair + 128] = grad_key.astype(BF)
             slope[1, here, 2 * part + 128 * pair : 2 * part + 128 * pair + 128] = grad_value.astype(BF)
         place = pl.multiple_of(turn * part, part)
@@ -482,7 +500,7 @@
         ],
         scratch_shapes=[
             pltpu.VMEM((rows, width), F32), pltpu.VMEM((rows, width), BF), pltpu.VMEM((2, rows, block), F32),
-            pltpu.VMEM((steps, rows, block), BF), pltpu.VMEM((2, 8, width), F32),
+            pltpu.VMEM((steps, rows, block), BF), pltpu.VMEM((2, 8, width), F32), pltpu.VMEM((8, block), F32),
             pltpu.VMEM((rows, width), F32), pltpu.VMEM((rows, width), BF), pltpu.VMEM((width, width), BF),
             pltpu.VMEM((2, short_seqs, heads, short_len, short_len), BF),
             pltpu.VMEM((2, long_seqs, heads, long_len, long_len), BF),

time: 237 us -> 235 us (level)
  no operation moved by 1% of the time
where the time goes in v6:
time: 235 us
  Pallas kernels  94.4 us (40%)
  waiting for transfers between devices  89 us (38%)
  starting transfers between devices  31.7 us (13%)
  between operations  14.9 us (6%)
  local copies, waits for them, and re-layouts  3.15 us (1%)
    ppermute x25, waiting for transfers between devices, exchange(): return lax.ppermute(block, 'dp', [(i, i ^ mask(i)) for i in range(count)])  71 us
    pallas_call x1, Pallas kernels, feed_and_attention_backward(): pl.pallas_call(partial(tail_kernel, shape, steps), grid=(2 * steps + 1 +...  66.9 us
    ppermute x25, starting transfers between devices, exchange(): return lax.ppermute(block, 'dp', [(i, i ^ mask(i)) for i in range(count)])  31.6 us
    pallas_call x1, Pallas kernels, attention_forward(): pl.pallas_call(partial(attention_forward_kernel, shape, weights['slots'])...  25.6 us
    all_gather x1, waiting for transfers between devices, gather_weights(): feed = lax.all_gather(pack_rows(inner, down), 'dp', axis=0, tiled=False)  18 us
  transfers between devices with their start and end apart: 26, of which 16 were waited for; matrix products, arithmetic and copies ran while one was open for 1% of the time, Pallas kernels for 11%

profile of v6, /device:TPU:0, one launch (start us, length us, event | category | flops | bytes accessed | tf_op | source)
XLA Modules:
  0.0 234.5 jit_solution(7726591423672024152)
XLA Ops:
  7.2 1.9 pack_rows.1
  9.3 4.1 %collective-permute-start.3 = (bf16[32,1536]{1,0:T(8,128)(2,1)S(1)}, bf16[32,1536]{1,0:T(8,128)(2,1)S(1)}, u32[]{:S(2)}, u32[]{:S(2)}) collective-permute-start(bf16[32,1536]{1,0:T(8,128)(2,1)S(1)} %pad_maximum_fusion.9), channel_id=1, source_target_pairs={{0,16},{1,17},{2,18},{3,19},{4,20},{5,21},{6,22},{7,23},{8,24},{9,... | collective-permute-start | bytes 294920 | tf_op jit(solution)/shard_map/ppermute | solution.py:559
  13.4 0.1 collective-permute-start.6
  13.5 2.9 %collective-permute-start = (bf16[32,1536]{1,0:T(8,128)(2,1)S(1)}, bf16[32,1536]{1,0:T(8,128)(2,1)S(1)}, u32[]{:S(2)}, u32[]{:S(2)}) collective-permute-start(bf16[32,1536]{1,0:T(8,128)(2,1)S(1)} %pad_maximum_fusion.8), channel_id=1, source_target_pairs={{0,16},{1,17},{2,18},{3,19},{4,20},{5,21},{6,22},{7,23},{8,24},{9,... | collective-permute-start | bytes 294920 | tf_op jit(solution)/shard_map/ppermute | solution.py:559
  16.4 7.6 %collective-permute-done.6 = bf16[32,1024]{1,0:T(8,128)(2,1)S(1)} collective-permute-done((bf16[32,1024]{1,0:T(8,128)(2,1)S(1)}, bf16[32,1024]{1,0:T(8,128)(2,1)S(1)}, u32[]{:S(2)}, u32[]{:S(2)}) %collective-permute-start.6) | collective-permute-done | bytes 65568 | tf_op jit(solution)/shard_map/ppermute | solution.py:559
  24.0 1.8 collective-permute-start.7
  25.8 0.4 collective-permute-start.4
  26.2 1.8 collective-permute-start.1
  28.0 4.2 %collective-permute-done.4 = bf16[64,1536]{1,0:T(8,128)(2,1)S(1)} collective-permute-done((bf16[64,1536]{1,0:T(8,128)(2,1)S(1)}, bf16[64,1536]{1,0:T(8,128)(2,1)S(1)}, u32[]{:S(2)}, u32[]{:S(2)}) %collective-permute-start.4) | collective-permute-done | bytes 196640 | tf_op jit(solution)/shard_map/ppermute | solution.py:559
  32.2 1.6 collective-permute-start.5
  33.8 0.5 collective-permute-done.1
  34.3 1.6 collective-permute-start.2
  35.9 0.6 collective-permute-start.8
  36.5 10.7 %collective-permute-done.5 = bf16[128,1536]{1,0:T(8,128)(2,1)S(1)} collective-permute-done((bf16[128,1536]{1,0:T(8,128)(2,1)S(1)}, bf16[128,1536]{1,0:T(8,128)(2,1)S(1)}, u32[]{:S(2)}, u32[]{:S(2)}) %collective-permute-start.5) | collective-permute-done | bytes 393248 | tf_op jit(solution)/shard_map/ppermute | solution.py:559
  47.3 1.1 collective-permute-start.10
  48.4 20.0 %collective-permute-done.2 = bf16[128,1536]{1,0:T(8,128)(2,1)S(1)} collective-permute-done((bf16[128,1536]{1,0:T(8,128)(2,1)S(1)}, bf16[128,1536]{1,0:T(8,128)(2,1)S(1)}, u32[]{:S(2)}, u32[]{:S(2)}) %collective-permute-start.2) | collective-permute-done | bytes 393248 | tf_op jit(solution)/shard_map/ppermute | solution.py:559
  68.5 0.6 collective-permute-start.9
  69.1 10.6 %collective-permute-done.8 = bf16[128,1024]{1,0:T(8,128)(2,1)S(1)} collective-permute-done((bf16[128,1024]{1,0:T(8,128)(2,1)S(1)}, bf16[128,1024]{1,0:T(8,128)(2,1)S(1)}, u32[]{:S(2)}, u32[]{:S(2)}) %collective-permute-start.8) | collective-permute-done | bytes 262176 | tf_op jit(solution)/shard_map/ppermute | solution.py:559
  79.7 3.8 %collective-permute-start.14 = (bf16[256,1024]{1,0:T(8,128)(2,1)S(1)}, bf16[256,1024]{1,0:T(8,128)(2,1)S(1)}, u32[]{:S(2)}, u32[]{:S(2)}) collective-permute-start(bf16[256,1024]{1,0:T(8,128)(2,1)S(1)} %constant_dynamic-update-slice_fusion.refs_2_), channel_id=1, source_target_pairs={{0,1},{1,0},{2,3},{3,2},{4,5},{5,4},{6,7},{7,6},{8,9},{9,8},{10,11... | collective-permute-start | bytes 1572872 | tf_op jit(solution)/shard_map/ppermute | solution.py:559
  83.6 5.3 %collective-permute-done.11.refs_5_ = bf16[256,1024]{1,0:T(8,128)(2,1)S(1)} collective-permute-done((bf16[256,1024]{1,0:T(8,128)(2,1)S(1)}, bf16[256,1024]{1,0:T(8,128)(2,1)S(1)}, u32[]{:S(2)}, u32[]{:S(2)}) %collective-permute-start.11) | collective-permute-done | bytes 524320 | tf_op jit(solution)/shard_map/ppermute | solution.py:559
  88.9 2.4 %collective-permute-start.12 = (bf16[256,1536]{1,0:T(8,128)(2,1)S(1)}, bf16[256,1536]{1,0:T(8,128)(2,1)}, u32[]{:S(2)}, u32[]{:S(2)}) collective-permute-start(bf16[256,1536]{1,0:T(8,128)(2,1)S(1)} %pad_maximum_fusion.refs_0_), channel_id=1, source_target_pairs={{0,1},{1,0},{2,3},{3,2},{4,5},{5,4},{6,7},{7,6},{8,9},{9,8},{10,11... | collective-permute-start | bytes 2359304 | tf_op jit(solution)/shard_map/ppermute | solution.py:559
  91.3 0.1 collective-permute-start.16
  91.4 0.4 collective-permute-start.15
  91.9 0.8 copy-done.7
  92.7 0.1 collective-permute-start.17
  93.4 0.1 fusion
  93.5 1.0 copy.33.keep
  94.5 0.8 collective-permute-done.12.refs_6_
  95.4 3.1 %collective-permute-done.17.refs_11_ = bf16[256,1024]{1,0:T(8,128)(2,1)} collective-permute-done((bf16[256,1024]{1,0:T(8,128)(2,1)S(1)}, bf16[256,1024]{1,0:T(8,128)(2,1)}, u32[]{:S(2)}, u32[]{:S(2)}) %collective-permute-start.17) | collective-permute-done | bytes 524320 | tf_op jit(solution)/shard_map/ppermute | solution.py:559
  98.5 25.6 %attention_forward.1 = (bf16[896,1024]{1,0:T(8,128)(2,1)}, bf16[896,1024]{1,0:T(8,128)(2,1)}, bf16[896,1024]{1,0:T(8,128)(2,1)}, bf16[3,16,128,128]{3,2,1,0:T(8,...) custom-call(s32[1]{0:T(128)} %bitcast.1.me, ...), custom_call_target="tpu_custom_call" | custom-call | flops 35999997952 | bytes 40000000 | tf_op jit(solution)/shard_map/attention_forward/pallas_call | solution.py:165
  124.1 18.0 %all-gather.3.cloned.1.call-done = bf16[8192,1024]{1,0:T(8,128)(2,1)} async-done(((bf16[256,1024]{1,0:T(8,128)(2,1)}), bf16[8192,1024]{1,0:T(8,128)(2,1)}) %all-gather.3.cloned.1.call-update) | async-done | bytes 16777232 | tf_op jit(solution)/shard_map/all_gather | solution.py:622
  142.2 66.9 %feed_and_attention_backward.1 = (bf16[384,1024]{1,0:T(8,128)(2,1)}, bf16[512,1024]{1,0:T(8,128)(2,1)}, bf16[384,1024]{1,0:T(8,128)(2,1)}, bf16[512,1024]{1,0:T(8,128)(2,1)}, f32[1,10240]{1,0:T(1,128)}) custom-call(f32[896,1]{1,0:T(8,128)} %copy.33.keep, f32[896,1]{1,0:T(8,128)} %get-tuple-element.27.rstd, bf16[896,1024]{1,0:T(8,128)(2,1)} %get-tuple-element.28.first, ...), custom_call_target="tpu_custom_call" | custom-call | flops 85000003584 | bytes 90000000 | tf_op jit(solution)/shard_map/feed_and_attention_backward/pallas_call | solution.py:486
  209.1 0.3 collective-permute-start.18
  209.4 1.2 collective-permute-done.18
  210.6 0.8 add.21
  211.4 1.4 collective-permute-start.19
  212.8 0.8 collective-permute-start.20
  213.5 1.4 collective-permute-start.21
  214.9 0.5 collective-permute-done.19
  215.4 1.3 collective-permute-done.20
  216.8 1.7 collective-permute-done.21
  218.5 0.5 collective-permute-start.22
  219.0 1.6 collective-permute-start.23
  220.6 2.4 %collective-permute-start.24 = (f32[1,10240]{1,0:T(1,128)S(1)}, f32[1,10240]{1,0:T(1,128)S(1)}, u32[]{:S(2)}, u32[]{:S(2)}) collective-permute-start(f32[1,10240]{1,0:T(1,128)S(1)} %add_add_fusion.1), channel_id=1, source_target_pairs={{0,24},{1,25},{2,26},{3,27},{4,28},{5,29},{6,30},{7,31},{8,16},{9,... | collective-permute-start | bytes 122888 | tf_op jit(solution)/shard_map/ppermute | solution.py:559
  223.0 1.2 collective-permute-done.23
  224.1 2.3 collective-permute-done.24
  226.5 0.6 fusion.2
  227.1 0.6 slice.83
  (52 shorter events, 0.7 us)
Async XLA Ops:
  7.2 2.0 copy-start.3
  7.2 6.2 %copy-start.2 = (bf16[32,1024]{1,0:T(8,128)(2,1)S(1)}, bf16[32,1024]{1,0:T(8,128)(2,1)}, u32[]{:S(2)}) copy-start(bf16[32,1024]{1,0:T(8,128)(2,1)} %param.26) | copy-start | bytes 196612
  7.2 135.0 %all-gather.3.cloned.1.call-start = ((), (), s32[]{:S(2)}) async-start(), calls=%async_computation | async-start | bytes 17301504 | tf_op jit(solution)/shard_map/all_gather | solution.py:622
  9.3 16.5 %collective-permute-start.3 = (bf16[32,1536]{1,0:T(8,128)(2,1)S(1)}, bf16[32,1536]{1,0:T(8,128)(2,1)S(1)}, u32[]{:S(2)}, u32[]{:S(2)}) collective-permute-start(bf16[32,1536]{1,0:T(8,128)(2,1)S(1)} %pad_maximum_fusion.9), channel_id=1, source_target_pairs={{0,16},{1,17},{2,18},{3,19},{4,20},{5,21},{6,22},{7,23},{8,24},{9,... | collective-permute-start | bytes 294920 | tf_op jit(solution)/shard_map/ppermute | solution.py:559
  13.4 10.6 %collective-permute-start.6 = (bf16[32,1024]{1,0:T(8,128)(2,1)S(1)}, bf16[32,1024]{1,0:T(8,128)(2,1)S(1)}, u32[]{:S(2)}, u32[]{:S(2)}) collective-permute-start(bf16[32,1024]{1,0:T(8,128)(2,1)S(1)} %copy-done.2), channel_id=1, source_target_pairs={{0,16},{1,17},{2,18},{3,19},{4,20},{5,21},{6,22},{7,23},{8,24},{9,... | collective-permute-start | bytes 196616 | tf_op jit(solution)/shard_map/ppermute | solution.py:559
  13.5 12.7 %collective-permute-start = (bf16[32,1536]{1,0:T(8,128)(2,1)S(1)}, bf16[32,1536]{1,0:T(8,128)(2,1)S(1)}, u32[]{:S(2)}, u32[]{:S(2)}) collective-permute-start(bf16[32,1536]{1,0:T(8,128)(2,1)S(1)} %pad_maximum_fusion.8), channel_id=1, source_target_pairs={{0,16},{1,17},{2,18},{3,19},{4,20},{5,21},{6,22},{7,23},{8,24},{9,... | collective-permute-start | bytes 294920 | tf_op jit(solution)/shard_map/ppermute | solution.py:559
  24.0 11.9 %collective-permute-start.7 = (bf16[64,1024]{1,0:T(8,128)(2,1)S(1)}, bf16[64,1024]{1,0:T(8,128)(2,1)S(1)}, u32[]{:S(2)}, u32[]{:S(2)}) collective-permute-start(bf16[64,1024]{1,0:T(8,128)(2,1)S(1)} %pad_maximum_fusion.7), channel_id=1, source_target_pairs={{0,2},{1,5},{2,0},{3,7},{4,6},{5,1},{6,4},{7,3},{8,10},{9,13},{10,... | collective-permute-start | bytes 393224 | tf_op jit(solution)/shard_map/ppermute | solution.py:559
  25.8 6.4 %collective-permute-start.4 = (bf16[64,1536]{1,0:T(8,128)(2,1)S(1)}, bf16[64,1536]{1,0:T(8,128)(2,1)S(1)}, u32[]{:S(2)}, u32[]{:S(2)}) collective-permute-start(bf16[64,1536]{1,0:T(8,128)(2,1)S(1)} %pad_maximum_fusion.6), channel_id=1, source_target_pairs={{0,2},{1,5},{2,0},{3,7},{4,6},{5,1},{6,4},{7,3},{8,10},{9,13},{10,... | collective-permute-start | bytes 589832 | tf_op jit(solution)/shard_map/ppermute | solution.py:559
  26.2 8.1 %collective-permute-start.1 = (bf16[64,1536]{1,0:T(8,128)(2,1)S(1)}, bf16[64,1536]{1,0:T(8,128)(2,1)S(1)}, u32[]{:S(2)}, u32[]{:S(2)}) collective-permute-start(bf16[64,1536]{1,0:T(8,128)(2,1)S(1)} %pad_maximum_fusion.5), channel_id=1, source_target_pairs={{0,2},{1,5},{2,0},{3,7},{4,6},{5,1},{6,4},{7,3},{8,10},{9,13},{10,... | collective-permute-start | bytes 589832 | tf_op jit(solution)/shard_map/ppermute | solution.py:559
  32.2 15.0 %collective-permute-start.5 = (bf16[128,1536]{1,0:T(8,128)(2,1)S(1)}, bf16[128,1536]{1,0:T(8,128)(2,1)S(1)}, u32[]{:S(2)}, u32[]{:S(2)}) collective-permute-start(bf16[128,1536]{1,0:T(8,128)(2,1)S(1)} %pad_maximum_fusion.3), channel_id=1, source_target_pairs={{0,8},{1,9},{2,10},{3,11},{4,12},{5,13},{6,14},{7,15},{8,0},{9,1},... | collective-permute-start | bytes 1179656 | tf_op jit(solution)/shard_map/ppermute | solution.py:559
  34.3 34.1 %collective-permute-start.2 = (bf16[128,1536]{1,0:T(8,128)(2,1)S(1)}, bf16[128,1536]{1,0:T(8,128)(2,1)S(1)}, u32[]{:S(2)}, u32[]{:S(2)}) collective-permute-start(bf16[128,1536]{1,0:T(8,128)(2,1)S(1)} %pad_maximum_fusion.2), channel_id=1, source_target_pairs={{0,8},{1,9},{2,10},{3,11},{4,12},{5,13},{6,14},{7,15},{8,0},{9,1},... | collective-permute-start | bytes 1179656 | tf_op jit(solution)/shard_map/ppermute | solution.py:559
  35.9 43.7 %collective-permute-start.8 = (bf16[128,1024]{1,0:T(8,128)(2,1)S(1)}, bf16[128,1024]{1,0:T(8,128)(2,1)S(1)}, u32[]{:S(2)}, u32[]{:S(2)}) collective-permute-start(bf16[128,1024]{1,0:T(8,128)(2,1)S(1)} %pad_maximum_fusion.4), channel_id=1, source_target_pairs={{0,8},{1,9},{2,10},{3,11},{4,12},{5,13},{6,14},{7,15},{8,0},{9,1},... | collective-permute-start | bytes 786440 | tf_op jit(solution)/shard_map/ppermute | solution.py:559
  47.3 51.2 %copy-start = (bf16[256,1536]{1,0:T(8,128)(2,1)}, bf16[256,1536]{1,0:T(8,128)(2,1)S(1)}, u32[]{:S(2)}) copy-start(bf16[256,1536]{1,0:T(8,128)(2,1)S(1)} %pad_maximum_fusion.1.refs_1_) | copy-start | bytes 2359300
  47.3 46.1 %copy-start.8 = (s32[3]{0:T(128)S(1)}, s32[3]{0:T(128)}, u32[]{:S(2)}) copy-start(s32[3]{0:T(128)} %short_lengths.1) | copy-start | bytes 40
  47.3 44.0 %collective-permute-start.10 = (bf16[256,1536]{1,0:T(8,128)(2,1)S(1)}, bf16[256,1536]{1,0:T(8,128)(2,1)S(1)}, u32[]{:S(2)}, u32[]{:S(2)}) collective-permute-start(bf16[256,1536]{1,0:T(8,128)(2,1)S(1)} %pad_maximum_fusion.1.refs_1_), channel_id=1, source_target_pairs={{0,4},{1,3},{2,6},{3,1},{4,0},{5,7},{6,2},{7,5},{8,12},{9,11},{10,... | collective-permute-start | bytes 2359304 | tf_op jit(solution)/shard_map/ppermute | solution.py:559
  68.4 30.0 %copy-start.1 = (bf16[256,1536]{1,0:T(8,128)(2,1)}, bf16[256,1536]{1,0:T(8,128)(2,1)S(1)}, u32[]{:S(2)}) copy-start(bf16[256,1536]{1,0:T(8,128)(2,1)S(1)} %pad_maximum_fusion.refs_0_) | copy-start | bytes 2359300
  68.5 23.0 %collective-permute-start.9 = (bf16[256,1536]{1,0:T(8,128)(2,1)S(1)}, bf16[256,1536]{1,0:T(8,128)(2,1)}, u32[]{:S(2)}, u32[]{:S(2)}) collective-permute-start(bf16[256,1536]{1,0:T(8,128)(2,1)S(1)} %pad_maximum_fusion.refs_0_), channel_id=1, source_target_pairs={{0,4},{1,3},{2,6},{3,1},{4,0},{5,7},{6,2},{7,5},{8,12},{9,11},{10,... | collective-permute-start | bytes 2359304 | tf_op jit(solution)/shard_map/ppermute | solution.py:559
  79.7 18.8 %copy-start.4 = (bf16[256,1024]{1,0:T(8,128)(2,1)}, bf16[256,1024]{1,0:T(8,128)(2,1)S(1)}, u32[]{:S(2)}) copy-start(bf16[256,1024]{1,0:T(8,128)(2,1)S(1)} %constant_dynamic-update-slice_fusion.refs_2_) | copy-start | bytes 1572868
  79.7 9.2 %collective-permute-start.11 = (bf16[256,1024]{1,0:T(8,128)(2,1)S(1)}, bf16[256,1024]{1,0:T(8,128)(2,1)S(1)}, u32[]{:S(2)}, u32[]{:S(2)}) collective-permute-start(bf16[256,1024]{1,0:T(8,128)(2,1)S(1)} %constant_dynamic-update-slice_fusion.refs_2_), channel_id=1, source_target_pairs={{0,4},{1,3},{2,6},{3,1},{4,0},{5,7},{6,2},{7,5},{8,12},{9,11},{10,... | collective-permute-start | bytes 1572872 | tf_op jit(solution)/shard_map/ppermute | solution.py:559
  79.7 12.1 %collective-permute-start.14 = (bf16[256,1024]{1,0:T(8,128)(2,1)S(1)}, bf16[256,1024]{1,0:T(8,128)(2,1)S(1)}, u32[]{:S(2)}, u32[]{:S(2)}) collective-permute-start(bf16[256,1024]{1,0:T(8,128)(2,1)S(1)} %constant_dynamic-update-slice_fusion.refs_2_), channel_id=1, source_target_pairs={{0,1},{1,0},{2,3},{3,2},{4,5},{5,4},{6,7},{7,6},{8,9},{9,8},{10,11... | collective-permute-start | bytes 1572872 | tf_op jit(solution)/shard_map/ppermute | solution.py:559
  83.6 10.9 %collective-permute-start.13 = (bf16[256,1536]{1,0:T(8,128)(2,1)S(1)}, bf16[256,1536]{1,0:T(8,128)(2,1)}, u32[]{:S(2)}, u32[]{:S(2)}) collective-permute-start(bf16[256,1536]{1,0:T(8,128)(2,1)S(1)} %pad_maximum_fusion.1.refs_1_), channel_id=1, source_target_pairs={{0,1},{1,0},{2,3},{3,2},{4,5},{5,4},{6,7},{7,6},{8,9},{9,8},{10,11... | collective-permute-start | bytes 2359304 | tf_op jit(solution)/shard_map/ppermute | solution.py:559
  88.9 9.6 %copy-start.6 = (bf16[256,1024]{1,0:T(8,128)(2,1)}, bf16[256,1024]{1,0:T(8,128)(2,1)S(1)}, u32[]{:S(2)}) copy-start(bf16[256,1024]{1,0:T(8,128)(2,1)S(1)} %collective-permute-done.11.refs_5_) | copy-start | bytes 1572868
  88.9 6.4 %collective-permute-start.12 = (bf16[256,1536]{1,0:T(8,128)(2,1)S(1)}, bf16[256,1536]{1,0:T(8,128)(2,1)}, u32[]{:S(2)}, u32[]{:S(2)}) collective-permute-start(bf16[256,1536]{1,0:T(8,128)(2,1)S(1)} %pad_maximum_fusion.refs_0_), channel_id=1, source_target_pairs={{0,1},{1,0},{2,3},{3,2},{4,5},{5,4},{6,7},{7,6},{8,9},{9,8},{10,11... | collective-permute-start | bytes 2359304 | tf_op jit(solution)/shard_map/ppermute | solution.py:559
  91.3 7.2 %copy-start.5 = (bf16[256,1536]{1,0:T(8,128)(2,1)}, bf16[256,1536]{1,0:T(8,128)(2,1)S(1)}, u32[]{:S(2)}) copy-start(bf16[256,1536]{1,0:T(8,128)(2,1)S(1)} %collective-permute-done.10.refs_4_) | copy-start | bytes 2359300
  91.3 7.1 %collective-permute-start.16 = (bf16[256,1536]{1,0:T(8,128)(2,1)S(1)}, bf16[256,1536]{1,0:T(8,128)(2,1)}, u32[]{:S(2)}, u32[]{:S(2)}) collective-permute-start(bf16[256,1536]{1,0:T(8,128)(2,1)S(1)} %collective-permute-done.10.refs_4_), channel_id=1, source_target_pairs={{0,1},{1,0},{2,3},{3,2},{4,5},{5,4},{6,7},{7,6},{8,9},{9,8},{10,11... | collective-permute-start | bytes 2359304 | tf_op jit(solution)/shard_map/ppermute | solution.py:559
  91.4 7.1 %collective-permute-start.15 = (bf16[256,1536]{1,0:T(8,128)(2,1)}, bf16[256,1536]{1,0:T(8,128)(2,1)}, u32[]{:S(2)}, u32[]{:S(2)}) collective-permute-start(bf16[256,1536]{1,0:T(8,128)(2,1)} %collective-permute-done.9.refs_3_), channel_id=1, source_target_pairs={{0,1},{1,0},{2,3},{3,2},{4,5},{5,4},{6,7},{7,6},{8,9},{9,8},{10,11... | collective-permute-start | bytes 2359304 | tf_op jit(solution)/shard_map/ppermute | solution.py:559
  91.9 0.8 copy-start.7
  92.7 5.8 %collective-permute-start.17 = (bf16[256,1024]{1,0:T(8,128)(2,1)S(1)}, bf16[256,1024]{1,0:T(8,128)(2,1)}, u32[]{:S(2)}, u32[]{:S(2)}) collective-permute-start(bf16[256,1024]{1,0:T(8,128)(2,1)S(1)} %collective-permute-done.11.refs_5_), channel_id=1, source_target_pairs={{0,1},{1,0},{2,3},{3,2},{4,5},{5,4},{6,7},{7,6},{8,9},{9,8},{10,11... | collective-permute-start | bytes 1572872 | tf_op jit(solution)/shard_map/ppermute | solution.py:559
  209.1 1.5 collective-permute-start.18
  211.4 4.1 %collective-permute-start.19 = (f32[1,10240]{1,0:T(1,128)S(1)}, f32[1,10240]{1,0:T(1,128)S(1)}, u32[]{:S(2)}, u32[]{:S(2)}) collective-permute-start(f32[1,10240]{1,0:T(1,128)S(1)} %add.21), channel_id=1, source_target_pairs={{0,2},{1,3},{2,0},{3,1},{4,6},{5,7},{6,4},{7,5},{8,10},{9,11},{10,... | collective-permute-start | bytes 122888 | tf_op jit(solution)/shard_map/ppermute | solution.py:559
  212.8 4.0 %collective-permute-start.20 = (f32[1,10240]{1,0:T(1,128)S(1)}, f32[1,10240]{1,0:T(1,128)S(1)}, u32[]{:S(2)}, u32[]{:S(2)}) collective-permute-start(f32[1,10240]{1,0:T(1,128)S(1)} %add.21), channel_id=1, source_target_pairs={{0,4},{1,5},{2,6},{3,7},{4,0},{5,1},{6,2},{7,3},{8,12},{9,13},{10,... | collective-permute-start | bytes 122888 | tf_op jit(solution)/shard_map/ppermute | solution.py:559
  213.5 4.9 %collective-permute-start.21 = (f32[1,10240]{1,0:T(1,128)S(1)}, f32[1,10240]{1,0:T(1,128)S(1)}, u32[]{:S(2)}, u32[]{:S(2)}) collective-permute-start(f32[1,10240]{1,0:T(1,128)S(1)} %add.21), channel_id=1, source_target_pairs={{0,6},{1,7},{2,4},{3,5},{4,2},{5,3},{6,0},{7,1},{8,14},{9,15},{10,... | collective-permute-start | bytes 122888 | tf_op jit(solution)/shard_map/ppermute | solution.py:559
  218.5 4.5 %collective-permute-start.22 = (f32[1,10240]{1,0:T(1,128)S(1)}, f32[1,10240]{1,0:T(1,128)S(1)}, u32[]{:S(2)}, u32[]{:S(2)}) collective-permute-start(f32[1,10240]{1,0:T(1,128)S(1)} %add_add_fusion.1), channel_id=1, source_target_pairs={{0,8},{1,9},{2,10},{3,11},{4,12},{5,13},{6,14},{7,15},{8,0},{9,1},... | collective-permute-start | bytes 122888 | tf_op jit(solution)/shard_map/ppermute | solution.py:559
  219.0 5.1 %collective-permute-start.23 = (f32[1,10240]{1,0:T(1,128)S(1)}, f32[1,10240]{1,0:T(1,128)S(1)}, u32[]{:S(2)}, u32[]{:S(2)}) collective-permute-start(f32[1,10240]{1,0:T(1,128)S(1)} %add_add_fusion.1), channel_id=1, source_target_pairs={{0,16},{1,17},{2,18},{3,19},{4,20},{5,21},{6,22},{7,23},{8,24},{9,... | collective-permute-start | bytes 122888 | tf_op jit(solution)/shard_map/ppermute | solution.py:559
  220.6 5.8 %collective-permute-start.24 = (f32[1,10240]{1,0:T(1,128)S(1)}, f32[1,10240]{1,0:T(1,128)S(1)}, u32[]{:S(2)}, u32[]{:S(2)}) collective-permute-start(f32[1,10240]{1,0:T(1,128)S(1)} %add_add_fusion.1), channel_id=1, source_target_pairs={{0,24},{1,25},{2,26},{3,27},{4,28},{5,29},{6,30},{7,31},{8,16},{9,... | collective-permute-start | bytes 122888 | tf_op jit(solution)/shard_map/ppermute | solution.py:559
Sparse Core Ops, SparseCore 0:
  10.9 131.2 all-gather.2

commit v7 on v6

--- a/solution.py
+++ b/solution.py
@@ -244,13 +244,13 @@
     base = short_seqs * short_len
     rows, width = total.shape
     units = steps * value.shape[2]
-    part = packed.shape[3]
+    part = packed.shape[2] // 3
     attention_steps = width // part
     heads = part // HEAD_DIM
     first_attention = 2 * steps + 1
     turn = step - first_attention
     slot = lax.rem(jnp.maximum(turn, 0), 2)
-    chunk = 128
+    chunk = 224 if rows % 224 == 0 else 128
     wide = lambda ref: ref[...].reshape(width, -1)
     tall = lambda ref: ref[...].reshape(-1, width)
     short_spans, long_spans = sequences(*shape)
@@ -284,7 +284,7 @@
         pairs += [
             (
                 packed_in.at[side, :, pl.ds(pl.multiple_of(i * third + within * part, part), part)],
-                packed.at[into, i],
+                packed.at[into, :, part * i : part * i + part],
             )
             for i in range(3)
         ]
@@ -446,11 +446,7 @@
         place = pl.multiple_of(turn * part, part)
         sums_out[:, pl.ds(place, part)] = jnp.sum(slope[1, :, :part].astype(F32), axis=0, keepdims=True)
         sums_out[:, pl.ds(width + place, part)] = jnp.sum(slope[1, :, 2 * part : 3 * part].astype(F32), axis=0, keepdims=True)
-        total[...] += (
-            dot_t(slope[1, :, :part], packed[slot, 0])
-            + dot_t(slope[1, :, part : 2 * part], packed[slot, 1])
-            + dot_t(slope[1, :, 2 * part : 3 * part], packed[slot, 2])
-        )
+        total[...] += dot_t(slope[1, :, : 3 * part], packed[slot])
 
     @pl.when((turn >= 0) & (turn < attention_steps - 2))
     def _():
@@ -504,7 +500,7 @@
             pltpu.VMEM((rows, width), F32), pltpu.VMEM((rows, width), BF), pltpu.VMEM((width, width), BF),
             pltpu.VMEM((2, short_seqs, heads, short_len, short_len), BF),
             pltpu.VMEM((2, long_seqs, heads, long_len, long_len), BF),
-            pltpu.VMEM((2, part, rows), F32), pltpu.VMEM((2, 3, width, part), BF), pltpu.VMEM((rows, width), BF),
+            pltpu.VMEM((2, part, rows), F32), pltpu.VMEM((2, width, 3 * part), BF), pltpu.VMEM((rows, width), BF),
             pltpu.SemaphoreType.DMA((8,)), pltpu.SemaphoreType.DMA((2, 9)),
         ],
         compiler_params=pltpu.CompilerParams(vmem_limit_bytes=TAIL_VMEM_BYTES),

time: 235 us -> 234 us (level)
  no operation moved by 1% of the time
where the time goes in v7:
time: 234 us
  Pallas kernels  93.9 us (40%)
  waiting for transfers between devices  89 us (38%)
  starting transfers between devices  31.7 us (14%)
  between operations  14.9 us (6%)
  local copies, waits for them, and re-layouts  3.15 us (1%)
    ppermute x25, waiting for transfers between devices, exchange(): return lax.ppermute(block, 'dp', [(i, i ^ mask(i)) for i in range(count)])  71 us
    pallas_call x1, Pallas kernels, feed_and_attention_backward(): pl.pallas_call(partial(tail_kernel, shape, steps), grid=(2 * steps + 1 +...  66.4 us
    ppermute x25, starting transfers between devices, exchange(): return lax.ppermute(block, 'dp', [(i, i ^ mask(i)) for i in range(count)])  31.6 us
    pallas_call x1, Pallas kernels, attention_forward(): pl.pallas_call(partial(attention_forward_kernel, shape, weights['slots'])...  25.6 us
    all_gather x1, waiting for transfers between devices, gather_weights(): feed = lax.all_gather(pack_rows(inner, down), 'dp', axis=0, tiled=False)  18 us
  transfers between devices with their start and end apart: 26, of which 16 were waited for; matrix products, arithmetic and copies ran while one was open for 1% of the time, Pallas kernels for 11%

profile of v7, /device:TPU:0, one launch (start us, length us, event | category | flops | bytes accessed | tf_op | source)
XLA Modules:
  0.0 234.0 jit_solution(4165846859095407628)
XLA Ops:
  7.2 1.9 pack_rows.1
  9.3 4.1 %collective-permute-start.3 = (bf16[32,1536]{1,0:T(8,128)(2,1)S(1)}, bf16[32,1536]{1,0:T(8,128)(2,1)S(1)}, u32[]{:S(2)}, u32[]{:S(2)}) collective-permute-start(bf16[32,1536]{1,0:T(8,128)(2,1)S(1)} %pad_maximum_fusion.9), channel_id=1, source_target_pairs={{0,16},{1,17},{2,18},{3,19},{4,20},{5,21},{6,22},{7,23},{8,24},{9,... | collective-permute-start | bytes 294920 | tf_op jit(solution)/shard_map/ppermute | solution.py:555
  13.4 0.1 collective-permute-start.6
  13.5 2.9 %collective-permute-start = (bf16[32,1536]{1,0:T(8,128)(2,1)S(1)}, bf16[32,1536]{1,0:T(8,128)(2,1)S(1)}, u32[]{:S(2)}, u32[]{:S(2)}) collective-permute-start(bf16[32,1536]{1,0:T(8,128)(2,1)S(1)} %pad_maximum_fusion.8), channel_id=1, source_target_pairs={{0,16},{1,17},{2,18},{3,19},{4,20},{5,21},{6,22},{7,23},{8,24},{9,... | collective-permute-start | bytes 294920 | tf_op jit(solution)/shard_map/ppermute | solution.py:555
  16.4 7.6 %collective-permute-done.6 = bf16[32,1024]{1,0:T(8,128)(2,1)S(1)} collective-permute-done((bf16[32,1024]{1,0:T(8,128)(2,1)S(1)}, bf16[32,1024]{1,0:T(8,128)(2,1)S(1)}, u32[]{:S(2)}, u32[]{:S(2)}) %collective-permute-start.6) | collective-permute-done | bytes 65568 | tf_op jit(solution)/shard_map/ppermute | solution.py:555
  24.0 1.8 collective-permute-start.7
  25.8 0.4 collective-permute-start.4
  26.2 1.8 collective-permute-start.1
  28.0 4.2 %collective-permute-done.4 = bf16[64,1536]{1,0:T(8,128)(2,1)S(1)} collective-permute-done((bf16[64,1536]{1,0:T(8,128)(2,1)S(1)}, bf16[64,1536]{1,0:T(8,128)(2,1)S(1)}, u32[]{:S(2)}, u32[]{:S(2)}) %collective-permute-start.4) | collective-permute-done | bytes 196640 | tf_op jit(solution)/shard_map/ppermute | solution.py:555
  32.2 1.6 collective-permute-start.5
  33.8 0.5 collective-permute-done.1
  34.3 1.6 collective-permute-start.2
  35.9 0.6 collective-permute-start.8
  36.5 10.7 %collective-permute-done.5 = bf16[128,1536]{1,0:T(8,128)(2,1)S(1)} collective-permute-done((bf16[128,1536]{1,0:T(8,128)(2,1)S(1)}, bf16[128,1536]{1,0:T(8,128)(2,1)S(1)}, u32[]{:S(2)}, u32[]{:S(2)}) %collective-permute-start.5) | collective-permute-done | bytes 393248 | tf_op jit(solution)/shard_map/ppermute | solution.py:555
  47.3 1.1 collective-permute-start.10
  48.4 20.0 %collective-permute-done.2 = bf16[128,1536]{1,0:T(8,128)(2,1)S(1)} collective-permute-done((bf16[128,1536]{1,0:T(8,128)(2,1)S(1)}, bf16[128,1536]{1,0:T(8,128)(2,1)S(1)}, u32[]{:S(2)}, u32[]{:S(2)}) %collective-permute-start.2) | collective-permute-done | bytes 393248 | tf_op jit(solution)/shard_map/ppermute | solution.py:555
  68.5 0.6 collective-permute-start.9
  69.1 10.6 %collective-permute-done.8 = bf16[128,1024]{1,0:T(8,128)(2,1)S(1)} collective-permute-done((bf16[128,1024]{1,0:T(8,128)(2,1)S(1)}, bf16[128,1024]{1,0:T(8,128)(2,1)S(1)}, u32[]{:S(2)}, u32[]{:S(2)}) %collective-permute-start.8) | collective-permute-done | bytes 262176 | tf_op jit(solution)/shard_map/ppermute | solution.py:555
  79.7 3.8 %collective-permute-start.14 = (bf16[256,1024]{1,0:T(8,128)(2,1)S(1)}, bf16[256,1024]{1,0:T(8,128)(2,1)S(1)}, u32[]{:S(2)}, u32[]{:S(2)}) collective-permute-start(bf16[256,1024]{1,0:T(8,128)(2,1)S(1)} %constant_dynamic-update-slice_fusion.refs_2_), channel_id=1, source_target_pairs={{0,1},{1,0},{2,3},{3,2},{4,5},{5,4},{6,7},{7,6},{8,9},{9,8},{10,11... | collective-permute-start | bytes 1572872 | tf_op jit(solution)/shard_map/ppermute | solution.py:555
  83.6 5.3 %collective-permute-done.11.refs_5_ = bf16[256,1024]{1,0:T(8,128)(2,1)S(1)} collective-permute-done((bf16[256,1024]{1,0:T(8,128)(2,1)S(1)}, bf16[256,1024]{1,0:T(8,128)(2,1)S(1)}, u32[]{:S(2)}, u32[]{:S(2)}) %collective-permute-start.11) | collective-permute-done | bytes 524320 | tf_op jit(solution)/shard_map/ppermute | solution.py:555
  88.9 2.4 %collective-permute-start.12 = (bf16[256,1536]{1,0:T(8,128)(2,1)S(1)}, bf16[256,1536]{1,0:T(8,128)(2,1)}, u32[]{:S(2)}, u32[]{:S(2)}) collective-permute-start(bf16[256,1536]{1,0:T(8,128)(2,1)S(1)} %pad_maximum_fusion.refs_0_), channel_id=1, source_target_pairs={{0,1},{1,0},{2,3},{3,2},{4,5},{5,4},{6,7},{7,6},{8,9},{9,8},{10,11... | collective-permute-start | bytes 2359304 | tf_op jit(solution)/shard_map/ppermute | solution.py:555
  91.3 0.1 collective-permute-start.16
  91.4 0.4 collective-permute-start.15
  91.9 0.8 copy-done.7
  92.7 0.1 collective-permute-start.17
  93.4 0.1 fusion
  93.5 1.0 copy.33.keep
  94.5 0.8 collective-permute-done.12.refs_6_
  95.4 3.1 %collective-permute-done.17.refs_11_ = bf16[256,1024]{1,0:T(8,128)(2,1)} collective-permute-done((bf16[256,1024]{1,0:T(8,128)(2,1)S(1)}, bf16[256,1024]{1,0:T(8,128)(2,1)}, u32[]{:S(2)}, u32[]{:S(2)}) %collective-permute-start.17) | collective-permute-done | bytes 524320 | tf_op jit(solution)/shard_map/ppermute | solution.py:555
  98.5 25.6 %attention_forward.1 = (bf16[896,1024]{1,0:T(8,128)(2,1)}, bf16[896,1024]{1,0:T(8,128)(2,1)}, bf16[896,1024]{1,0:T(8,128)(2,1)}, bf16[3,16,128,128]{3,2,1,0:T(8,...) custom-call(s32[1]{0:T(128)} %bitcast.1.me, ...), custom_call_target="tpu_custom_call" | custom-call | flops 35999997952 | bytes 40000000 | tf_op jit(solution)/shard_map/attention_forward/pallas_call | solution.py:165
  124.1 18.0 %all-gather.3.cloned.1.call-done = bf16[8192,1024]{1,0:T(8,128)(2,1)} async-done(((bf16[256,1024]{1,0:T(8,128)(2,1)}), bf16[8192,1024]{1,0:T(8,128)(2,1)}) %all-gather.3.cloned.1.call-update) | async-done | bytes 16777232 | tf_op jit(solution)/shard_map/all_gather | solution.py:618
  142.2 66.4 %feed_and_attention_backward.1 = (bf16[384,1024]{1,0:T(8,128)(2,1)}, bf16[512,1024]{1,0:T(8,128)(2,1)}, bf16[384,1024]{1,0:T(8,128)(2,1)}, bf16[512,1024]{1,0:T(8,128)(2,1)}, f32[1,10240]{1,0:T(1,128)}) custom-call(f32[896,1]{1,0:T(8,128)} %copy.33.keep, f32[896,1]{1,0:T(8,128)} %get-tuple-element.27.rstd, bf16[896,1024]{1,0:T(8,128)(2,1)} %get-tuple-element.28.first, ...), custom_call_target="tpu_custom_call" | custom-call | flops 85000003584 | bytes 90000000 | tf_op jit(solution)/shard_map/feed_and_attention_backward/pallas_call | solution.py:482
  208.5 0.3 collective-permute-start.18
  208.8 1.2 collective-permute-done.18
  210.0 0.8 add.21
  210.9 1.4 collective-permute-start.19
  212.2 0.8 collective-permute-start.20
  213.0 1.4 collective-permute-start.21
  214.4 0.5 collective-permute-done.19
  214.9 1.3 collective-permute-done.20
  216.2 1.7 collective-permute-done.21
  218.0 0.5 collective-permute-start.22
  218.5 1.6 collective-permute-start.23
  220.1 2.4 %collective-permute-start.24 = (f32[1,10240]{1,0:T(1,128)S(1)}, f32[1,10240]{1,0:T(1,128)S(1)}, u32[]{:S(2)}, u32[]{:S(2)}) collective-permute-start(f32[1,10240]{1,0:T(1,128)S(1)} %add_add_fusion.1), channel_id=1, source_target_pairs={{0,24},{1,25},{2,26},{3,27},{4,28},{5,29},{6,30},{7,31},{8,16},{9,... | collective-permute-start | bytes 122888 | tf_op jit(solution)/shard_map/ppermute | solution.py:555
  222.4 1.2 collective-permute-done.23
  223.6 2.3 collective-permute-done.24
  225.9 0.6 fusion.2
  226.6 0.6 slice.83
  (52 shorter events, 0.7 us)
Async XLA Ops:
  7.2 2.0 copy-start.3
  7.2 6.2 %copy-start.2 = (bf16[32,1024]{1,0:T(8,128)(2,1)S(1)}, bf16[32,1024]{1,0:T(8,128)(2,1)}, u32[]{:S(2)}) copy-start(bf16[32,1024]{1,0:T(8,128)(2,1)} %param.26) | copy-start | bytes 196612
  7.2 135.0 %all-gather.3.cloned.1.call-start = ((), (), s32[]{:S(2)}) async-start(), calls=%async_computation | async-start | bytes 17301504 | tf_op jit(solution)/shard_map/all_gather | solution.py:618
  9.3 16.5 %collective-permute-start.3 = (bf16[32,1536]{1,0:T(8,128)(2,1)S(1)}, bf16[32,1536]{1,0:T(8,128)(2,1)S(1)}, u32[]{:S(2)}, u32[]{:S(2)}) collective-permute-start(bf16[32,1536]{1,0:T(8,128)(2,1)S(1)} %pad_maximum_fusion.9), channel_id=1, source_target_pairs={{0,16},{1,17},{2,18},{3,19},{4,20},{5,21},{6,22},{7,23},{8,24},{9,... | collective-permute-start | bytes 294920 | tf_op jit(solution)/shard_map/ppermute | solution.py:555
  13.4 10.6 %collective-permute-start.6 = (bf16[32,1024]{1,0:T(8,128)(2,1)S(1)}, bf16[32,1024]{1,0:T(8,128)(2,1)S(1)}, u32[]{:S(2)}, u32[]{:S(2)}) collective-permute-start(bf16[32,1024]{1,0:T(8,128)(2,1)S(1)} %copy-done.2), channel_id=1, source_target_pairs={{0,16},{1,17},{2,18},{3,19},{4,20},{5,21},{6,22},{7,23},{8,24},{9,... | collective-permute-start | bytes 196616 | tf_op jit(solution)/shard_map/ppermute | solution.py:555
  13.5 12.7 %collective-permute-start = (bf16[32,1536]{1,0:T(8,128)(2,1)S(1)}, bf16[32,1536]{1,0:T(8,128)(2,1)S(1)}, u32[]{:S(2)}, u32[]{:S(2)}) collective-permute-start(bf16[32,1536]{1,0:T(8,128)(2,1)S(1)} %pad_maximum_fusion.8), channel_id=1, source_target_pairs={{0,16},{1,17},{2,18},{3,19},{4,20},{5,21},{6,22},{7,23},{8,24},{9,... | collective-permute-start | bytes 294920 | tf_op jit(solution)/shard_map/ppermute | solution.py:555
  24.0 11.9 %collective-permute-start.7 = (bf16[64,1024]{1,0:T(8,128)(2,1)S(1)}, bf16[64,1024]{1,0:T(8,128)(2,1)S(1)}, u32[]{:S(2)}, u32[]{:S(2)}) collective-permute-start(bf16[64,1024]{1,0:T(8,128)(2,1)S(1)} %pad_maximum_fusion.7), channel_id=1, source_target_pairs={{0,2},{1,5},{2,0},{3,7},{4,6},{5,1},{6,4},{7,3},{8,10},{9,13},{10,... | collective-permute-start | bytes 393224 | tf_op jit(solution)/shard_map/ppermute | solution.py:555
  25.8 6.4 %collective-permute-start.4 = (bf16[64,1536]{1,0:T(8,128)(2,1)S(1)}, bf16[64,1536]{1,0:T(8,128)(2,1)S(1)}, u32[]{:S(2)}, u32[]{:S(2)}) collective-permute-start(bf16[64,1536]{1,0:T(8,128)(2,1)S(1)} %pad_maximum_fusion.6), channel_id=1, source_target_pairs={{0,2},{1,5},{2,0},{3,7},{4,6},{5,1},{6,4},{7,3},{8,10},{9,13},{10,... | collective-permute-start | bytes 589832 | tf_op jit(solution)/shard_map/ppermute | solution.py:555
  26.2 8.1 %collective-permute-start.1 = (bf16[64,1536]{1,0:T(8,128)(2,1)S(1)}, bf16[64,1536]{1,0:T(8,128)(2,1)S(1)}, u32[]{:S(2)}, u32[]{:S(2)}) collective-permute-start(bf16[64,1536]{1,0:T(8,128)(2,1)S(1)} %pad_maximum_fusion.5), channel_id=1, source_target_pairs={{0,2},{1,5},{2,0},{3,7},{4,6},{5,1},{6,4},{7,3},{8,10},{9,13},{10,... | collective-permute-start | bytes 589832 | tf_op jit(solution)/shard_map/ppermute | solution.py:555
  32.2 15.0 %collective-permute-start.5 = (bf16[128,1536]{1,0:T(8,128)(2,1)S(1)}, bf16[128,1536]{1,0:T(8,128)(2,1)S(1)}, u32[]{:S(2)}, u32[]{:S(2)}) collective-permute-start(bf16[128,1536]{1,0:T(8,128)(2,1)S(1)} %pad_maximum_fusion.3), channel_id=1, source_target_pairs={{0,8},{1,9},{2,10},{3,11},{4,12},{5,13},{6,14},{7,15},{8,0},{9,1},... | collective-permute-start | bytes 1179656 | tf_op jit(solution)/shard_map/ppermute | solution.py:555
  34.3 34.1 %collective-permute-start.2 = (bf16[128,1536]{1,0:T(8,128)(2,1)S(1)}, bf16[128,1536]{1,0:T(8,128)(2,1)S(1)}, u32[]{:S(2)}, u32[]{:S(2)}) collective-permute-start(bf16[128,1536]{1,0:T(8,128)(2,1)S(1)} %pad_maximum_fusion.2), channel_id=1, source_target_pairs={{0,8},{1,9},{2,10},{3,11},{4,12},{5,13},{6,14},{7,15},{8,0},{9,1},... | collective-permute-start | bytes 1179656 | tf_op jit(solution)/shard_map/ppermute | solution.py:555
  35.9 43.7 %collective-permute-start.8 = (bf16[128,1024]{1,0:T(8,128)(2,1)S(1)}, bf16[128,1024]{1,0:T(8,128)(2,1)S(1)}, u32[]{:S(2)}, u32[]{:S(2)}) collective-permute-start(bf16[128,1024]{1,0:T(8,128)(2,1)S(1)} %pad_maximum_fusion.4), channel_id=1, source_target_pairs={{0,8},{1,9},{2,10},{3,11},{4,12},{5,13},{6,14},{7,15},{8,0},{9,1},... | collective-permute-start | bytes 786440 | tf_op jit(solution)/shard_map/ppermute | solution.py:555
  47.3 51.2 %copy-start = (bf16[256,1536]{1,0:T(8,128)(2,1)}, bf16[256,1536]{1,0:T(8,128)(2,1)S(1)}, u32[]{:S(2)}) copy-start(bf16[256,1536]{1,0:T(8,128)(2,1)S(1)} %pad_maximum_fusion.1.refs_1_) | copy-start | bytes 2359300
  47.3 46.1 %copy-start.8 = (s32[3]{0:T(128)S(1)}, s32[3]{0:T(128)}, u32[]{:S(2)}) copy-start(s32[3]{0:T(128)} %short_lengths.1) | copy-start | bytes 40
  47.3 44.0 %collective-permute-start.10 = (bf16[256,1536]{1,0:T(8,128)(2,1)S(1)}, bf16[256,1536]{1,0:T(8,128)(2,1)S(1)}, u32[]{:S(2)}, u32[]{:S(2)}) collective-permute-start(bf16[256,1536]{1,0:T(8,128)(2,1)S(1)} %pad_maximum_fusion.1.refs_1_), channel_id=1, source_target_pairs={{0,4},{1,3},{2,6},{3,1},{4,0},{5,7},{6,2},{7,5},{8,12},{9,11},{10,... | collective-permute-start | bytes 2359304 | tf_op jit(solution)/shard_map/ppermute | solution.py:555
  68.4 30.0 %copy-start.1 = (bf16[256,1536]{1,0:T(8,128)(2,1)}, bf16[256,1536]{1,0:T(8,128)(2,1)S(1)}, u32[]{:S(2)}) copy-start(bf16[256,1536]{1,0:T(8,128)(2,1)S(1)} %pad_maximum_fusion.refs_0_) | copy-start | bytes 2359300
  68.5 23.0 %collective-permute-start.9 = (bf16[256,1536]{1,0:T(8,128)(2,1)S(1)}, bf16[256,1536]{1,0:T(8,128)(2,1)}, u32[]{:S(2)}, u32[]{:S(2)}) collective-permute-start(bf16[256,1536]{1,0:T(8,128)(2,1)S(1)} %pad_maximum_fusion.refs_0_), channel_id=1, source_target_pairs={{0,4},{1,3},{2,6},{3,1},{4,0},{5,7},{6,2},{7,5},{8,12},{9,11},{10,... | collective-permute-start | bytes 2359304 | tf_op jit(solution)/shard_map/ppermute | solution.py:555
  79.7 18.8 %copy-start.4 = (bf16[256,1024]{1,0:T(8,128)(2,1)}, bf16[256,1024]{1,0:T(8,128)(2,1)S(1)}, u32[]{:S(2)}) copy-start(bf16[256,1024]{1,0:T(8,128)(2,1)S(1)} %constant_dynamic-update-slice_fusion.refs_2_) | copy-start | bytes 1572868
  79.7 9.2 %collective-permute-start.11 = (bf16[256,1024]{1,0:T(8,128)(2,1)S(1)}, bf16[256,1024]{1,0:T(8,128)(2,1)S(1)}, u32[]{:S(2)}, u32[]{:S(2)}) collective-permute-start(bf16[256,1024]{1,0:T(8,128)(2,1)S(1)} %constant_dynamic-update-slice_fusion.refs_2_), channel_id=1, source_target_pairs={{0,4},{1,3},{2,6},{3,1},{4,0},{5,7},{6,2},{7,5},{8,12},{9,11},{10,... | collective-permute-start | bytes 1572872 | tf_op jit(solution)/shard_map/ppermute | solution.py:555
  79.7 12.1 %collective-permute-start.14 = (bf16[256,1024]{1,0:T(8,128)(2,1)S(1)}, bf16[256,1024]{1,0:T(8,128)(2,1)S(1)}, u32[]{:S(2)}, u32[]{:S(2)}) collective-permute-start(bf16[256,1024]{1,0:T(8,128)(2,1)S(1)} %constant_dynamic-update-slice_fusion.refs_2_), channel_id=1, source_target_pairs={{0,1},{1,0},{2,3},{3,2},{4,5},{5,4},{6,7},{7,6},{8,9},{9,8},{10,11... | collective-permute-start | bytes 1572872 | tf_op jit(solution)/shard_map/ppermute | solution.py:555
  83.6 10.9 %collective-permute-start.13 = (bf16[256,1536]{1,0:T(8,128)(2,1)S(1)}, bf16[256,1536]{1,0:T(8,128)(2,1)}, u32[]{:S(2)}, u32[]{:S(2)}) collective-permute-start(bf16[256,1536]{1,0:T(8,128)(2,1)S(1)} %pad_maximum_fusion.1.refs_1_), channel_id=1, source_target_pairs={{0,1},{1,0},{2,3},{3,2},{4,5},{5,4},{6,7},{7,6},{8,9},{9,8},{10,11... | collective-permute-start | bytes 2359304 | tf_op jit(solution)/shard_map/ppermute | solution.py:555
  88.9 9.6 %copy-start.6 = (bf16[256,1024]{1,0:T(8,128)(2,1)}, bf16[256,1024]{1,0:T(8,128)(2,1)S(1)}, u32[]{:S(2)}) copy-start(bf16[256,1024]{1,0:T(8,128)(2,1)S(1)} %collective-permute-done.11.refs_5_) | copy-start | bytes 1572868
  88.9 6.4 %collective-permute-start.12 = (bf16[256,1536]{1,0:T(8,128)(2,1)S(1)}, bf16[256,1536]{1,0:T(8,128)(2,1)}, u32[]{:S(2)}, u32[]{:S(2)}) collective-permute-start(bf16[256,1536]{1,0:T(8,128)(2,1)S(1)} %pad_maximum_fusion.refs_0_), channel_id=1, source_target_pairs={{0,1},{1,0},{2,3},{3,2},{4,5},{5,4},{6,7},{7,6},{8,9},{9,8},{10,11... | collective-permute-start | bytes 2359304 | tf_op jit(solution)/shard_map/ppermute | solution.py:555
  91.3 7.2 %copy-start.5 = (bf16[256,1536]{1,0:T(8,128)(2,1)}, bf16[256,1536]{1,0:T(8,128)(2,1)S(1)}, u32[]{:S(2)}) copy-start(bf16[256,1536]{1,0:T(8,128)(2,1)S(1)} %collective-permute-done.10.refs_4_) | copy-start | bytes 2359300
  91.3 7.1 %collective-permute-start.16 = (bf16[256,1536]{1,0:T(8,128)(2,1)S(1)}, bf16[256,1536]{1,0:T(8,128)(2,1)}, u32[]{:S(2)}, u32[]{:S(2)}) collective-permute-start(bf16[256,1536]{1,0:T(8,128)(2,1)S(1)} %collective-permute-done.10.refs_4_), channel_id=1, source_target_pairs={{0,1},{1,0},{2,3},{3,2},{4,5},{5,4},{6,7},{7,6},{8,9},{9,8},{10,11... | collective-permute-start | bytes 2359304 | tf_op jit(solution)/shard_map/ppermute | solution.py:555
  91.4 7.1 %collective-permute-start.15 = (bf16[256,1536]{1,0:T(8,128)(2,1)}, bf16[256,1536]{1,0:T(8,128)(2,1)}, u32[]{:S(2)}, u32[]{:S(2)}) collective-permute-start(bf16[256,1536]{1,0:T(8,128)(2,1)} %collective-permute-done.9.refs_3_), channel_id=1, source_target_pairs={{0,1},{1,0},{2,3},{3,2},{4,5},{5,4},{6,7},{7,6},{8,9},{9,8},{10,11... | collective-permute-start | bytes 2359304 | tf_op jit(solution)/shard_map/ppermute | solution.py:555
  91.9 0.8 copy-start.7
  92.7 5.8 %collective-permute-start.17 = (bf16[256,1024]{1,0:T(8,128)(2,1)S(1)}, bf16[256,1024]{1,0:T(8,128)(2,1)}, u32[]{:S(2)}, u32[]{:S(2)}) collective-permute-start(bf16[256,1024]{1,0:T(8,128)(2,1)S(1)} %collective-permute-done.11.refs_5_), channel_id=1, source_target_pairs={{0,1},{1,0},{2,3},{3,2},{4,5},{5,4},{6,7},{7,6},{8,9},{9,8},{10,11... | collective-permute-start | bytes 1572872 | tf_op jit(solution)/shard_map/ppermute | solution.py:555
  208.5 1.5 collective-permute-start.18
  210.9 4.1 %collective-permute-start.19 = (f32[1,10240]{1,0:T(1,128)S(1)}, f32[1,10240]{1,0:T(1,128)S(1)}, u32[]{:S(2)}, u32[]{:S(2)}) collective-permute-start(f32[1,10240]{1,0:T(1,128)S(1)} %add.21), channel_id=1, source_target_pairs={{0,2},{1,3},{2,0},{3,1},{4,6},{5,7},{6,4},{7,5},{8,10},{9,11},{10,... | collective-permute-start | bytes 122888 | tf_op jit(solution)/shard_map/ppermute | solution.py:555
  212.2 4.0 %collective-permute-start.20 = (f32[1,10240]{1,0:T(1,128)S(1)}, f32[1,10240]{1,0:T(1,128)S(1)}, u32[]{:S(2)}, u32[]{:S(2)}) collective-permute-start(f32[1,10240]{1,0:T(1,128)S(1)} %add.21), channel_id=1, source_target_pairs={{0,4},{1,5},{2,6},{3,7},{4,0},{5,1},{6,2},{7,3},{8,12},{9,13},{10,... | collective-permute-start | bytes 122888 | tf_op jit(solution)/shard_map/ppermute | solution.py:555
  213.0 4.9 %collective-permute-start.21 = (f32[1,10240]{1,0:T(1,128)S(1)}, f32[1,10240]{1,0:T(1,128)S(1)}, u32[]{:S(2)}, u32[]{:S(2)}) collective-permute-start(f32[1,10240]{1,0:T(1,128)S(1)} %add.21), channel_id=1, source_target_pairs={{0,6},{1,7},{2,4},{3,5},{4,2},{5,3},{6,0},{7,1},{8,14},{9,15},{10,... | collective-permute-start | bytes 122888 | tf_op jit(solution)/shard_map/ppermute | solution.py:555
  218.0 4.5 %collective-permute-start.22 = (f32[1,10240]{1,0:T(1,128)S(1)}, f32[1,10240]{1,0:T(1,128)S(1)}, u32[]{:S(2)}, u32[]{:S(2)}) collective-permute-start(f32[1,10240]{1,0:T(1,128)S(1)} %add_add_fusion.1), channel_id=1, source_target_pairs={{0,8},{1,9},{2,10},{3,11},{4,12},{5,13},{6,14},{7,15},{8,0},{9,1},... | collective-permute-start | bytes 122888 | tf_op jit(solution)/shard_map/ppermute | solution.py:555
  218.5 5.1 %collective-permute-start.23 = (f32[1,10240]{1,0:T(1,128)S(1)}, f32[1,10240]{1,0:T(1,128)S(1)}, u32[]{:S(2)}, u32[]{:S(2)}) collective-permute-start(f32[1,10240]{1,0:T(1,128)S(1)} %add_add_fusion.1), channel_id=1, source_target_pairs={{0,16},{1,17},{2,18},{3,19},{4,20},{5,21},{6,22},{7,23},{8,24},{9,... | collective-permute-start | bytes 122888 | tf_op jit(solution)/shard_map/ppermute | solution.py:555
  220.1 5.8 %collective-permute-start.24 = (f32[1,10240]{1,0:T(1,128)S(1)}, f32[1,10240]{1,0:T(1,128)S(1)}, u32[]{:S(2)}, u32[]{:S(2)}) collective-permute-start(f32[1,10240]{1,0:T(1,128)S(1)} %add_add_fusion.1), channel_id=1, source_target_pairs={{0,24},{1,25},{2,26},{3,27},{4,28},{5,29},{6,30},{7,31},{8,16},{9,... | collective-permute-start | bytes 122888 | tf_op jit(solution)/shard_map/ppermute | solution.py:555
Sparse Core Ops, SparseCore 0:
  10.9 131.2 all-gather.2

commit v8 on v7

--- a/solution.py
+++ b/solution.py
@@ -538,7 +538,7 @@
     short_out, long_out, short_grad, long_grad, sums = feed_and_attention_backward(
         shape, keep, attention, cts, weights["feed"], vectors
     )
-    sums = sum_all(sums).reshape(-1)
+    sums = sum_all(sums.reshape(-1))
     outs = []
     at = 0
     for size in (width, width, width, inner_bias.shape[0], width, width, width):

time: 234 us -> 234 us (level)
  no operation moved by 1% of the time
where the time goes in v8:
time: 234 us
  Pallas kernels  93.9 us (40%)
  waiting for transfers between devices  89 us (38%)
  starting transfers between devices  31.6 us (14%)
  between operations  14.9 us (6%)
  local copies, waits for them, and re-layouts  3.15 us (1%)
    ppermute x25, waiting for transfers between devices, exchange(): return lax.ppermute(block, 'dp', [(i, i ^ mask(i)) for i in range(count)])  71 us
    pallas_call x1, Pallas kernels, feed_and_attention_backward(): pl.pallas_call(partial(tail_kernel, shape, steps), grid=(2 * steps + 1 +...  66.4 us
    ppermute x25, starting transfers between devices, exchange(): return lax.ppermute(block, 'dp', [(i, i ^ mask(i)) for i in range(count)])  31.6 us
    pallas_call x1, Pallas kernels, attention_forward(): pl.pallas_call(partial(attention_forward_kernel, shape, weights['slots'])...  25.6 us
    all_gather x1, waiting for transfers between devices, gather_weights(): feed = lax.all_gather(pack_rows(inner, down), 'dp', axis=0, tiled=False)  18 us
  transfers between devices with their start and end apart: 26, of which 16 were waited for; matrix products, arithmetic and copies ran while one was open for 1% of the time, Pallas kernels for 11%

profile of v8, /device:TPU:0, one launch (start us, length us, event | category | flops | bytes accessed | tf_op | source)
XLA Modules:
  0.0 233.8 jit_solution(10312728677990493663)
XLA Ops:
  7.2 1.9 pack_rows.1
  9.3 4.1 %collective-permute-start.3 = (bf16[32,1536]{1,0:T(8,128)(2,1)S(1)}, bf16[32,1536]{1,0:T(8,128)(2,1)S(1)}, u32[]{:S(2)}, u32[]{:S(2)}) collective-permute-start(bf16[32,1536]{1,0:T(8,128)(2,1)S(1)} %pad_maximum_fusion.9), channel_id=1, source_target_pairs={{0,16},{1,17},{2,18},{3,19},{4,20},{5,21},{6,22},{7,23},{8,24},{9,... | collective-permute-start | bytes 294920 | tf_op jit(solution)/shard_map/ppermute | solution.py:555
  13.4 0.1 collective-permute-start.6
  13.5 2.9 %collective-permute-start = (bf16[32,1536]{1,0:T(8,128)(2,1)S(1)}, bf16[32,1536]{1,0:T(8,128)(2,1)S(1)}, u32[]{:S(2)}, u32[]{:S(2)}) collective-permute-start(bf16[32,1536]{1,0:T(8,128)(2,1)S(1)} %pad_maximum_fusion.8), channel_id=1, source_target_pairs={{0,16},{1,17},{2,18},{3,19},{4,20},{5,21},{6,22},{7,23},{8,24},{9,... | collective-permute-start | bytes 294920 | tf_op jit(solution)/shard_map/ppermute | solution.py:555
  16.4 7.6 %collective-permute-done.6 = bf16[32,1024]{1,0:T(8,128)(2,1)S(1)} collective-permute-done((bf16[32,1024]{1,0:T(8,128)(2,1)S(1)}, bf16[32,1024]{1,0:T(8,128)(2,1)S(1)}, u32[]{:S(2)}, u32[]{:S(2)}) %collective-permute-start.6) | collective-permute-done | bytes 65568 | tf_op jit(solution)/shard_map/ppermute | solution.py:555
  24.0 1.8 collective-permute-start.7
  25.8 0.4 collective-permute-start.4
  26.2 1.8 collective-permute-start.1
  28.0 4.2 %collective-permute-done.4 = bf16[64,1536]{1,0:T(8,128)(2,1)S(1)} collective-permute-done((bf16[64,1536]{1,0:T(8,128)(2,1)S(1)}, bf16[64,1536]{1,0:T(8,128)(2,1)S(1)}, u32[]{:S(2)}, u32[]{:S(2)}) %collective-permute-start.4) | collective-permute-done | bytes 196640 | tf_op jit(solution)/shard_map/ppermute | solution.py:555
  32.2 1.6 collective-permute-start.5
  33.8 0.5 collective-permute-done.1
  34.3 1.6 collective-permute-start.2
  35.9 0.6 collective-permute-start.8
  36.5 10.7 %collective-permute-done.5 = bf16[128,1536]{1,0:T(8,128)(2,1)S(1)} collective-permute-done((bf16[128,1536]{1,0:T(8,128)(2,1)S(1)}, bf16[128,1536]{1,0:T(8,128)(2,1)S(1)}, u32[]{:S(2)}, u32[]{:S(2)}) %collective-permute-start.5) | collective-permute-done | bytes 393248 | tf_op jit(solution)/shard_map/ppermute | solution.py:555
  47.3 1.1 collective-permute-start.10
  48.4 20.0 %collective-permute-done.2 = bf16[128,1536]{1,0:T(8,128)(2,1)S(1)} collective-permute-done((bf16[128,1536]{1,0:T(8,128)(2,1)S(1)}, bf16[128,1536]{1,0:T(8,128)(2,1)S(1)}, u32[]{:S(2)}, u32[]{:S(2)}) %collective-permute-start.2) | collective-permute-done | bytes 393248 | tf_op jit(solution)/shard_map/ppermute | solution.py:555
  68.5 0.6 collective-permute-start.9
  69.1 10.6 %collective-permute-done.8 = bf16[128,1024]{1,0:T(8,128)(2,1)S(1)} collective-permute-done((bf16[128,1024]{1,0:T(8,128)(2,1)S(1)}, bf16[128,1024]{1,0:T(8,128)(2,1)S(1)}, u32[]{:S(2)}, u32[]{:S(2)}) %collective-permute-start.8) | collective-permute-done | bytes 262176 | tf_op jit(solution)/shard_map/ppermute | solution.py:555
  79.7 3.8 %collective-permute-start.14 = (bf16[256,1024]{1,0:T(8,128)(2,1)S(1)}, bf16[256,1024]{1,0:T(8,128)(2,1)S(1)}, u32[]{:S(2)}, u32[]{:S(2)}) collective-permute-start(bf16[256,1024]{1,0:T(8,128)(2,1)S(1)} %constant_dynamic-update-slice_fusion.refs_2_), channel_id=1, source_target_pairs={{0,1},{1,0},{2,3},{3,2},{4,5},{5,4},{6,7},{7,6},{8,9},{9,8},{10,11... | collective-permute-start | bytes 1572872 | tf_op jit(solution)/shard_map/ppermute | solution.py:555
  83.6 5.3 %collective-permute-done.11.refs_5_ = bf16[256,1024]{1,0:T(8,128)(2,1)S(1)} collective-permute-done((bf16[256,1024]{1,0:T(8,128)(2,1)S(1)}, bf16[256,1024]{1,0:T(8,128)(2,1)S(1)}, u32[]{:S(2)}, u32[]{:S(2)}) %collective-permute-start.11) | collective-permute-done | bytes 524320 | tf_op jit(solution)/shard_map/ppermute | solution.py:555
  88.9 2.4 %collective-permute-start.12 = (bf16[256,1536]{1,0:T(8,128)(2,1)S(1)}, bf16[256,1536]{1,0:T(8,128)(2,1)}, u32[]{:S(2)}, u32[]{:S(2)}) collective-permute-start(bf16[256,1536]{1,0:T(8,128)(2,1)S(1)} %pad_maximum_fusion.refs_0_), channel_id=1, source_target_pairs={{0,1},{1,0},{2,3},{3,2},{4,5},{5,4},{6,7},{7,6},{8,9},{9,8},{10,11... | collective-permute-start | bytes 2359304 | tf_op jit(solution)/shard_map/ppermute | solution.py:555
  91.3 0.1 collective-permute-start.16
  91.4 0.4 collective-permute-start.15
  91.9 0.8 copy-done.7
  92.7 0.1 collective-permute-start.17
  93.4 0.1 fusion
  93.5 1.0 copy.33.keep
  94.5 0.8 collective-permute-done.12.refs_6_
  95.4 3.1 %collective-permute-done.17.refs_11_ = bf16[256,1024]{1,0:T(8,128)(2,1)} collective-permute-done((bf16[256,1024]{1,0:T(8,128)(2,1)S(1)}, bf16[256,1024]{1,0:T(8,128)(2,1)}, u32[]{:S(2)}, u32[]{:S(2)}) %collective-permute-start.17) | collective-permute-done | bytes 524320 | tf_op jit(solution)/shard_map/ppermute | solution.py:555
  98.5 25.6 %attention_forward.1 = (bf16[896,1024]{1,0:T(8,128)(2,1)}, bf16[896,1024]{1,0:T(8,128)(2,1)}, bf16[896,1024]{1,0:T(8,128)(2,1)}, bf16[3,16,128,128]{3,2,1,0:T(8,...) custom-call(s32[1]{0:T(128)} %bitcast.1.me, ...), custom_call_target="tpu_custom_call" | custom-call | flops 35999997952 | bytes 40000000 | tf_op jit(solution)/shard_map/attention_forward/pallas_call | solution.py:165
  124.1 18.0 %all-gather.3.cloned.1.call-done = bf16[8192,1024]{1,0:T(8,128)(2,1)} async-done(((bf16[256,1024]{1,0:T(8,128)(2,1)}), bf16[8192,1024]{1,0:T(8,128)(2,1)}) %all-gather.3.cloned.1.call-update) | async-done | bytes 16777232 | tf_op jit(solution)/shard_map/all_gather | solution.py:618
  142.2 66.4 %feed_and_attention_backward.1 = (bf16[384,1024]{1,0:T(8,128)(2,1)}, bf16[512,1024]{1,0:T(8,128)(2,1)}, bf16[384,1024]{1,0:T(8,128)(2,1)}, bf16[512,1024]{1,0:T(8,128)(2,1)}, f32[1,10240]{1,0:T(1,128)}) custom-call(f32[896,1]{1,0:T(8,128)} %copy.33.keep, f32[896,1]{1,0:T(8,128)} %get-tuple-element.27.rstd, bf16[896,1024]{1,0:T(8,128)(2,1)} %get-tuple-element.28.first, ...), custom_call_target="tpu_custom_call" | custom-call | flops 85000003584 | bytes 90000000 | tf_op jit(solution)/shard_map/feed_and_attention_backward/pallas_call | solution.py:482
  208.5 0.3 collective-permute-start.18
  208.8 1.2 collective-permute-done.18
  210.0 0.8 add.21
  210.8 1.3 collective-permute-start.19
  212.1 0.8 collective-permute-start.20
  212.9 1.4 collective-permute-start.21
  214.3 0.5 collective-permute-done.19
  214.8 1.3 collective-permute-done.20
  216.1 1.7 collective-permute-done.21
  217.8 0.5 collective-permute-start.22
  218.3 1.6 collective-permute-start.23
  219.9 2.4 %collective-permute-start.24 = (f32[10240]{0:T(1024)S(1)}, f32[10240]{0:T(1024)S(1)}, u32[]{:S(2)}, u32[]{:S(2)}) collective-permute-start(f32[10240]{0:T(1024)S(1)} %add_add_fusion.1), channel_id=1, source_target_pairs={{0,24},{1,25},{2,26},{3,27},{4,28},{5,29},{6,30},{7,31},{8,16},{9,... | collective-permute-start | bytes 122888 | tf_op jit(solution)/shard_map/ppermute | solution.py:555
  222.3 1.2 collective-permute-done.23
  223.4 2.3 collective-permute-done.24
  225.7 0.6 fusion.2
  226.3 0.6 slice.55
  (52 shorter events, 0.5 us)
Async XLA Ops:
  7.2 2.0 copy-start.3
  7.2 6.2 %copy-start.2 = (bf16[32,1024]{1,0:T(8,128)(2,1)S(1)}, bf16[32,1024]{1,0:T(8,128)(2,1)}, u32[]{:S(2)}) copy-start(bf16[32,1024]{1,0:T(8,128)(2,1)} %param.26) | copy-start | bytes 196612
  7.2 135.0 %all-gather.3.cloned.1.call-start = ((), (), s32[]{:S(2)}) async-start(), calls=%async_computation | async-start | bytes 17301504 | tf_op jit(solution)/shard_map/all_gather | solution.py:618
  9.3 16.5 %collective-permute-start.3 = (bf16[32,1536]{1,0:T(8,128)(2,1)S(1)}, bf16[32,1536]{1,0:T(8,128)(2,1)S(1)}, u32[]{:S(2)}, u32[]{:S(2)}) collective-permute-start(bf16[32,1536]{1,0:T(8,128)(2,1)S(1)} %pad_maximum_fusion.9), channel_id=1, source_target_pairs={{0,16},{1,17},{2,18},{3,19},{4,20},{5,21},{6,22},{7,23},{8,24},{9,... | collective-permute-start | bytes 294920 | tf_op jit(solution)/shard_map/ppermute | solution.py:555
  13.4 10.6 %collective-permute-start.6 = (bf16[32,1024]{1,0:T(8,128)(2,1)S(1)}, bf16[32,1024]{1,0:T(8,128)(2,1)S(1)}, u32[]{:S(2)}, u32[]{:S(2)}) collective-permute-start(bf16[32,1024]{1,0:T(8,128)(2,1)S(1)} %copy-done.2), channel_id=1, source_target_pairs={{0,16},{1,17},{2,18},{3,19},{4,20},{5,21},{6,22},{7,23},{8,24},{9,... | collective-permute-start | bytes 196616 | tf_op jit(solution)/shard_map/ppermute | solution.py:555
  13.5 12.7 %collective-permute-start = (bf16[32,1536]{1,0:T(8,128)(2,1)S(1)}, bf16[32,1536]{1,0:T(8,128)(2,1)S(1)}, u32[]{:S(2)}, u32[]{:S(2)}) collective-permute-start(bf16[32,1536]{1,0:T(8,128)(2,1)S(1)} %pad_maximum_fusion.8), channel_id=1, source_target_pairs={{0,16},{1,17},{2,18},{3,19},{4,20},{5,21},{6,22},{7,23},{8,24},{9,... | collective-permute-start | bytes 294920 | tf_op jit(solution)/shard_map/ppermute | solution.py:555
  24.0 11.9 %collective-permute-start.7 = (bf16[64,1024]{1,0:T(8,128)(2,1)S(1)}, bf16[64,1024]{1,0:T(8,128)(2,1)S(1)}, u32[]{:S(2)}, u32[]{:S(2)}) collective-permute-start(bf16[64,1024]{1,0:T(8,128)(2,1)S(1)} %pad_maximum_fusion.7), channel_id=1, source_target_pairs={{0,2},{1,5},{2,0},{3,7},{4,6},{5,1},{6,4},{7,3},{8,10},{9,13},{10,... | collective-permute-start | bytes 393224 | tf_op jit(solution)/shard_map/ppermute | solution.py:555
  25.8 6.4 %collective-permute-start.4 = (bf16[64,1536]{1,0:T(8,128)(2,1)S(1)}, bf16[64,1536]{1,0:T(8,128)(2,1)S(1)}, u32[]{:S(2)}, u32[]{:S(2)}) collective-permute-start(bf16[64,1536]{1,0:T(8,128)(2,1)S(1)} %pad_maximum_fusion.6), channel_id=1, source_target_pairs={{0,2},{1,5},{2,0},{3,7},{4,6},{5,1},{6,4},{7,3},{8,10},{9,13},{10,... | collective-permute-start | bytes 589832 | tf_op jit(solution)/shard_map/ppermute | solution.py:555
  26.2 8.1 %collective-permute-start.1 = (bf16[64,1536]{1,0:T(8,128)(2,1)S(1)}, bf16[64,1536]{1,0:T(8,128)(2,1)S(1)}, u32[]{:S(2)}, u32[]{:S(2)}) collective-permute-start(bf16[64,1536]{1,0:T(8,128)(2,1)S(1)} %pad_maximum_fusion.5), channel_id=1, source_target_pairs={{0,2},{1,5},{2,0},{3,7},{4,6},{5,1},{6,4},{7,3},{8,10},{9,13},{10,... | collective-permute-start | bytes 589832 | tf_op jit(solution)/shard_map/ppermute | solution.py:555
  32.2 15.0 %collective-permute-start.5 = (bf16[128,1536]{1,0:T(8,128)(2,1)S(1)}, bf16[128,1536]{1,0:T(8,128)(2,1)S(1)}, u32[]{:S(2)}, u32[]{:S(2)}) collective-permute-start(bf16[128,1536]{1,0:T(8,128)(2,1)S(1)} %pad_maximum_fusion.3), channel_id=1, source_target_pairs={{0,8},{1,9},{2,10},{3,11},{4,12},{5,13},{6,14},{7,15},{8,0},{9,1},... | collective-permute-start | bytes 1179656 | tf_op jit(solution)/shard_map/ppermute | solution.py:555
  34.3 34.1 %collective-permute-start.2 = (bf16[128,1536]{1,0:T(8,128)(2,1)S(1)}, bf16[128,1536]{1,0:T(8,128)(2,1)S(1)}, u32[]{:S(2)}, u32[]{:S(2)}) collective-permute-start(bf16[128,1536]{1,0:T(8,128)(2,1)S(1)} %pad_maximum_fusion.2), channel_id=1, source_target_pairs={{0,8},{1,9},{2,10},{3,11},{4,12},{5,13},{6,14},{7,15},{8,0},{9,1},... | collective-permute-start | bytes 1179656 | tf_op jit(solution)/shard_map/ppermute | solution.py:555
  35.9 43.7 %collective-permute-start.8 = (bf16[128,1024]{1,0:T(8,128)(2,1)S(1)}, bf16[128,1024]{1,0:T(8,128)(2,1)S(1)}, u32[]{:S(2)}, u32[]{:S(2)}) collective-permute-start(bf16[128,1024]{1,0:T(8,128)(2,1)S(1)} %pad_maximum_fusion.4), channel_id=1, source_target_pairs={{0,8},{1,9},{2,10},{3,11},{4,12},{5,13},{6,14},{7,15},{8,0},{9,1},... | collective-permute-start | bytes 786440 | tf_op jit(solution)/shard_map/ppermute | solution.py:555
  47.3 51.2 %copy-start = (bf16[256,1536]{1,0:T(8,128)(2,1)}, bf16[256,1536]{1,0:T(8,128)(2,1)S(1)}, u32[]{:S(2)}) copy-start(bf16[256,1536]{1,0:T(8,128)(2,1)S(1)} %pad_maximum_fusion.1.refs_1_) | copy-start | bytes 2359300
  47.3 46.1 %copy-start.8 = (s32[3]{0:T(128)S(1)}, s32[3]{0:T(128)}, u32[]{:S(2)}) copy-start(s32[3]{0:T(128)} %short_lengths.1) | copy-start | bytes 40
  47.3 44.0 %collective-permute-start.10 = (bf16[256,1536]{1,0:T(8,128)(2,1)S(1)}, bf16[256,1536]{1,0:T(8,128)(2,1)S(1)}, u32[]{:S(2)}, u32[]{:S(2)}) collective-permute-start(bf16[256,1536]{1,0:T(8,128)(2,1)S(1)} %pad_maximum_fusion.1.refs_1_), channel_id=1, source_target_pairs={{0,4},{1,3},{2,6},{3,1},{4,0},{5,7},{6,2},{7,5},{8,12},{9,11},{10,... | collective-permute-start | bytes 2359304 | tf_op jit(solution)/shard_map/ppermute | solution.py:555
  68.4 30.0 %copy-start.1 = (bf16[256,1536]{1,0:T(8,128)(2,1)}, bf16[256,1536]{1,0:T(8,128)(2,1)S(1)}, u32[]{:S(2)}) copy-start(bf16[256,1536]{1,0:T(8,128)(2,1)S(1)} %pad_maximum_fusion.refs_0_) | copy-start | bytes 2359300
  68.5 23.0 %collective-permute-start.9 = (bf16[256,1536]{1,0:T(8,128)(2,1)S(1)}, bf16[256,1536]{1,0:T(8,128)(2,1)}, u32[]{:S(2)}, u32[]{:S(2)}) collective-permute-start(bf16[256,1536]{1,0:T(8,128)(2,1)S(1)} %pad_maximum_fusion.refs_0_), channel_id=1, source_target_pairs={{0,4},{1,3},{2,6},{3,1},{4,0},{5,7},{6,2},{7,5},{8,12},{9,11},{10,... | collective-permute-start | bytes 2359304 | tf_op jit(solution)/shard_map/ppermute | solution.py:555
  79.7 18.8 %copy-start.4 = (bf16[256,1024]{1,0:T(8,128)(2,1)}, bf16[256,1024]{1,0:T(8,128)(2,1)S(1)}, u32[]{:S(2)}) copy-start(bf16[256,1024]{1,0:T(8,128)(2,1)S(1)} %constant_dynamic-update-slice_fusion.refs_2_) | copy-start | bytes 1572868
  79.7 9.2 %collective-permute-start.11 = (bf16[256,1024]{1,0:T(8,128)(2,1)S(1)}, bf16[256,1024]{1,0:T(8,128)(2,1)S(1)}, u32[]{:S(2)}, u32[]{:S(2)}) collective-permute-start(bf16[256,1024]{1,0:T(8,128)(2,1)S(1)} %constant_dynamic-update-slice_fusion.refs_2_), channel_id=1, source_target_pairs={{0,4},{1,3},{2,6},{3,1},{4,0},{5,7},{6,2},{7,5},{8,12},{9,11},{10,... | collective-permute-start | bytes 1572872 | tf_op jit(solution)/shard_map/ppermute | solution.py:555
  79.7 12.1 %collective-permute-start.14 = (bf16[256,1024]{1,0:T(8,128)(2,1)S(1)}, bf16[256,1024]{1,0:T(8,128)(2,1)S(1)}, u32[]{:S(2)}, u32[]{:S(2)}) collective-permute-start(bf16[256,1024]{1,0:T(8,128)(2,1)S(1)} %constant_dynamic-update-slice_fusion.refs_2_), channel_id=1, source_target_pairs={{0,1},{1,0},{2,3},{3,2},{4,5},{5,4},{6,7},{7,6},{8,9},{9,8},{10,11... | collective-permute-start | bytes 1572872 | tf_op jit(solution)/shard_map/ppermute | solution.py:555
  83.6 10.9 %collective-permute-start.13 = (bf16[256,1536]{1,0:T(8,128)(2,1)S(1)}, bf16[256,1536]{1,0:T(8,128)(2,1)}, u32[]{:S(2)}, u32[]{:S(2)}) collective-permute-start(bf16[256,1536]{1,0:T(8,128)(2,1)S(1)} %pad_maximum_fusion.1.refs_1_), channel_id=1, source_target_pairs={{0,1},{1,0},{2,3},{3,2},{4,5},{5,4},{6,7},{7,6},{8,9},{9,8},{10,11... | collective-permute-start | bytes 2359304 | tf_op jit(solution)/shard_map/ppermute | solution.py:555
  88.9 9.6 %copy-start.6 = (bf16[256,1024]{1,0:T(8,128)(2,1)}, bf16[256,1024]{1,0:T(8,128)(2,1)S(1)}, u32[]{:S(2)}) copy-start(bf16[256,1024]{1,0:T(8,128)(2,1)S(1)} %collective-permute-done.11.refs_5_) | copy-start | bytes 1572868
  88.9 6.4 %collective-permute-start.12 = (bf16[256,1536]{1,0:T(8,128)(2,1)S(1)}, bf16[256,1536]{1,0:T(8,128)(2,1)}, u32[]{:S(2)}, u32[]{:S(2)}) collective-permute-start(bf16[256,1536]{1,0:T(8,128)(2,1)S(1)} %pad_maximum_fusion.refs_0_), channel_id=1, source_target_pairs={{0,1},{1,0},{2,3},{3,2},{4,5},{5,4},{6,7},{7,6},{8,9},{9,8},{10,11... | collective-permute-start | bytes 2359304 | tf_op jit(solution)/shard_map/ppermute | solution.py:555
  91.3 7.2 %copy-start.5 = (bf16[256,1536]{1,0:T(8,128)(2,1)}, bf16[256,1536]{1,0:T(8,128)(2,1)S(1)}, u32[]{:S(2)}) copy-start(bf16[256,1536]{1,0:T(8,128)(2,1)S(1)} %collective-permute-done.10.refs_4_) | copy-start | bytes 2359300
  91.3 7.1 %collective-permute-start.16 = (bf16[256,1536]{1,0:T(8,128)(2,1)S(1)}, bf16[256,1536]{1,0:T(8,128)(2,1)}, u32[]{:S(2)}, u32[]{:S(2)}) collective-permute-start(bf16[256,1536]{1,0:T(8,128)(2,1)S(1)} %collective-permute-done.10.refs_4_), channel_id=1, source_target_pairs={{0,1},{1,0},{2,3},{3,2},{4,5},{5,4},{6,7},{7,6},{8,9},{9,8},{10,11... | collective-permute-start | bytes 2359304 | tf_op jit(solution)/shard_map/ppermute | solution.py:555
  91.4 7.1 %collective-permute-start.15 = (bf16[256,1536]{1,0:T(8,128)(2,1)}, bf16[256,1536]{1,0:T(8,128)(2,1)}, u32[]{:S(2)}, u32[]{:S(2)}) collective-permute-start(bf16[256,1536]{1,0:T(8,128)(2,1)} %collective-permute-done.9.refs_3_), channel_id=1, source_target_pairs={{0,1},{1,0},{2,3},{3,2},{4,5},{5,4},{6,7},{7,6},{8,9},{9,8},{10,11... | collective-permute-start | bytes 2359304 | tf_op jit(solution)/shard_map/ppermute | solution.py:555
  91.9 0.8 copy-start.7
  92.7 5.8 %collective-permute-start.17 = (bf16[256,1024]{1,0:T(8,128)(2,1)S(1)}, bf16[256,1024]{1,0:T(8,128)(2,1)}, u32[]{:S(2)}, u32[]{:S(2)}) collective-permute-start(bf16[256,1024]{1,0:T(8,128)(2,1)S(1)} %collective-permute-done.11.refs_5_), channel_id=1, source_target_pairs={{0,1},{1,0},{2,3},{3,2},{4,5},{5,4},{6,7},{7,6},{8,9},{9,8},{10,11... | collective-permute-start | bytes 1572872 | tf_op jit(solution)/shard_map/ppermute | solution.py:555
  208.5 1.5 collective-permute-start.18
  210.8 4.0 %collective-permute-start.19 = (f32[10240]{0:T(1024)S(1)}, f32[10240]{0:T(1024)S(1)}, u32[]{:S(2)}, u32[]{:S(2)}) collective-permute-start(f32[10240]{0:T(1024)S(1)} %add.21), channel_id=1, source_target_pairs={{0,2},{1,3},{2,0},{3,1},{4,6},{5,7},{6,4},{7,5},{8,10},{9,11},{10,... | collective-permute-start | bytes 122888 | tf_op jit(solution)/shard_map/ppermute | solution.py:555
  212.1 4.0 %collective-permute-start.20 = (f32[10240]{0:T(1024)S(1)}, f32[10240]{0:T(1024)S(1)}, u32[]{:S(2)}, u32[]{:S(2)}) collective-permute-start(f32[10240]{0:T(1024)S(1)} %add.21), channel_id=1, source_target_pairs={{0,4},{1,5},{2,6},{3,7},{4,0},{5,1},{6,2},{7,3},{8,12},{9,13},{10,... | collective-permute-start | bytes 122888 | tf_op jit(solution)/shard_map/ppermute | solution.py:555
  212.9 4.9 %collective-permute-start.21 = (f32[10240]{0:T(1024)S(1)}, f32[10240]{0:T(1024)S(1)}, u32[]{:S(2)}, u32[]{:S(2)}) collective-permute-start(f32[10240]{0:T(1024)S(1)} %add.21), channel_id=1, source_target_pairs={{0,6},{1,7},{2,4},{3,5},{4,2},{5,3},{6,0},{7,1},{8,14},{9,15},{10,... | collective-permute-start | bytes 122888 | tf_op jit(solution)/shard_map/ppermute | solution.py:555
  217.8 4.5 %collective-permute-start.22 = (f32[10240]{0:T(1024)S(1)}, f32[10240]{0:T(1024)S(1)}, u32[]{:S(2)}, u32[]{:S(2)}) collective-permute-start(f32[10240]{0:T(1024)S(1)} %add_add_fusion.1), channel_id=1, source_target_pairs={{0,8},{1,9},{2,10},{3,11},{4,12},{5,13},{6,14},{7,15},{8,0},{9,1},... | collective-permute-start | bytes 122888 | tf_op jit(solution)/shard_map/ppermute | solution.py:555
  218.3 5.1 %collective-permute-start.23 = (f32[10240]{0:T(1024)S(1)}, f32[10240]{0:T(1024)S(1)}, u32[]{:S(2)}, u32[]{:S(2)}) collective-permute-start(f32[10240]{0:T(1024)S(1)} %add_add_fusion.1), channel_id=1, source_target_pairs={{0,16},{1,17},{2,18},{3,19},{4,20},{5,21},{6,22},{7,23},{8,24},{9,... | collective-permute-start | bytes 122888 | tf_op jit(solution)/shard_map/ppermute | solution.py:555
  219.9 5.8 %collective-permute-start.24 = (f32[10240]{0:T(1024)S(1)}, f32[10240]{0:T(1024)S(1)}, u32[]{:S(2)}, u32[]{:S(2)}) collective-permute-start(f32[10240]{0:T(1024)S(1)} %add_add_fusion.1), channel_id=1, source_target_pairs={{0,24},{1,25},{2,26},{3,27},{4,28},{5,29},{6,30},{7,31},{8,16},{9,... | collective-permute-start | bytes 122888 | tf_op jit(solution)/shard_map/ppermute | solution.py:555
Sparse Core Ops, SparseCore 0:
  10.9 131.2 all-gather.2
